TPU v7x, 512 devices: a whole 4x4x16 slice. The times are simulated.
512 devices in a mesh: ctx: 16 (over z_lo, core), kvh: 8 (over x, z_hi), sess: 4 (over y).
Axes of the slice: x: 4, y: 4, z: 16 (z_hi: 2, z_lo: 8; z = z_hi * 8 + z_lo), core: 2. Of those that a mesh axis runs over, the one named last changes fastest.
Arguments:
- queries: bfloat16 [1024, 8, 16, 128], P(('sess', 'ctx'), 'kvh'), parts along dimension 0, may hold values from -64 to 64
- new_keys: bfloat16 [1024, 8, 128], P(('sess', 'ctx'), 'kvh'), parts along dimension 0, may hold values from -8 to 8
- new_values: bfloat16 [1024, 8, 128], P(('sess', 'ctx'), 'kvh'), parts along dimension 0, may hold values from -6 to 6
- cache_k: bfloat16 [32, 32768, 128], P(('sess', 'kvh'), 'ctx'), parts along dimension 0, may hold values from -4 to 4
- cache_v: bfloat16 [32, 32768, 128], P(('sess', 'kvh'), 'ctx'), parts along dimension 0, may hold values from -6 to 6
- span_bounds: int32 [16, 2], P('sess'), parts along dimension 0, may hold values from 0 to 256, as said below
- cache_len: int32 [64], P('sess'), parts along dimension 0, may hold values from 512 to 2048, as said below
- doc_start: int32 [4], P('sess'), parts along dimension 0, may hold values from 0 to 4095
Outputs:
- attended: bfloat16 [1024, 8, 16, 128], P(('sess', 'ctx'), 'kvh'), parts along dimension 0
There are 4 independent parts, one for each index of `sess`. A program takes and returns all parts, laid end to end along the dimension named above; each array names one. Nothing has to cross between parts.
Inputs may be any that keep to these rules, and one draw needn't show every extreme that they name: `span_bounds`: span k lies within tokens k * 64 to (k + 1) * 64, and its start is below its end; spans are disjoint. `cache_len`: some shard is full in every draw.
All inputs are finite; a program needn't handle non-finite values.
Results may differ from a plain program's by a relative error of at most 0.013.
Values may be sent and summed in bfloat16 or wider, within the bound.
No kernel may reach another device: no remote copies, remote signals or barrier semaphores. Data moves between devices by JAX's collectives and lax.ppermute only.
A program may use at most 64 MiB of HBM per device.

v0:
```python
import math

import jax
import jax.numpy as jnp
from jax import lax
from jax.sharding import PartitionSpec as P


def cache_valid(first, count, cache_dev, nshard, cache_len, doc_start):
    rowids = first + jnp.arange(count, dtype=jnp.int32)
    shard = rowids // cache_dev
    slot = rowids % cache_dev
    table = shard[:, None] == jnp.arange(nshard, dtype=jnp.int32)[None, :]
    limit = jnp.sum(jnp.where(table, cache_len[None, :], 0), axis=1)
    return (slot < limit) & (slot * nshard + shard >= doc_start[0])


def partial_attend(qrows, keys, values, visible, scale):
    scores = jnp.einsum("rd,cd->rc", qrows, keys, preferred_element_type=jnp.float32) * scale
    scores = jnp.where(visible, scores, -1e30)
    peak = jnp.max(scores, axis=1)
    weights = jnp.exp(scores - peak[:, None])
    totals = jnp.sum(weights, axis=1)
    numer = jnp.dot(weights.astype(jnp.bfloat16), values, preferred_element_type=jnp.float32)
    return (peak, totals, numer)


def shard_partial(qrows, keys, values, visible, scale):
    peak, totals, numer = partial_attend(qrows, keys, values, visible, scale)
    lse_rows = peak + jnp.log(totals)
    outputs = (numer / totals[:, None]).astype(jnp.bfloat16)
    return (lse_rows, outputs)


def joined(first, second):
    peak = jnp.maximum(first[0], second[0])
    left = jnp.exp(first[0] - peak)
    right = jnp.exp(second[0] - peak)
    return (
        peak,
        first[1] * left + second[1] * right,
        first[2] * left[..., None] + second[2] * right[..., None],
    )


def on_device(queries, new_keys, new_values, cache_k, cache_v, span_bounds, cache_len, doc_start):
    nshard = lax.axis_size("ctx")
    myself = lax.axis_index("ctx")
    tq_dev = queries.shape[0]
    group = queries.shape[2]
    head_dim = queries.shape[3]
    cache_dev = cache_k.shape[1]
    all_tokens = tq_dev * nshard
    scale = 1.0 / math.sqrt(head_dim)
    fresh_k, fresh_v = (
        lax.all_gather(new_keys, "ctx", axis=0, tiled=True),
        lax.all_gather(new_values, "ctx", axis=0, tiled=True),
    )
    own_rows = queries.reshape(tq_dev * group, head_dim)
    own_tokens = myself * tq_dev + jnp.arange(tq_dev, dtype=jnp.int32)
    row_tokens = jnp.repeat(own_tokens, group)
    key_tokens = jnp.arange(all_tokens, dtype=jnp.int32)
    inspan_rows = (span_bounds[:, 0:1] <= row_tokens[None, :]) & (
        row_tokens[None, :] < span_bounds[:, 1:2]
    )
    inspan_keys = (span_bounds[:, 0:1] <= key_tokens[None, :]) & (
        key_tokens[None, :] < span_bounds[:, 1:2]
    )
    same_span = jnp.any(inspan_rows[:, :, None] & inspan_keys[:, None, :], axis=0)
    fresh_ok = (key_tokens[None, :] <= row_tokens[:, None]) | same_span
    fresh = partial_attend(own_rows, fresh_k[:, 0, :], fresh_v[:, 0, :], fresh_ok, scale)
    every = lax.all_gather(queries, "ctx", axis=0, tiled=True)
    count_rows = all_tokens * group
    step_rows = math.gcd(count_rows, 1024)
    blocks = every.reshape(count_rows // step_rows, step_rows, head_dim)
    visible = cache_valid(myself * cache_dev, cache_dev, cache_dev, nshard, cache_len, doc_start)[
        None, :
    ]

    def local_block(block):
        return shard_partial(block, cache_k[0], cache_v[0], visible, scale)

    lses, outs = lax.map(local_block, blocks)
    lses = lses.reshape(all_tokens, group)
    outs = outs.reshape(all_tokens, group, head_dim)
    got_out = lax.all_to_all(outs[None], "ctx", split_axis=1, concat_axis=0, tiled=True)
    got_lse = lax.all_to_all(lses[None], "ctx", split_axis=1, concat_axis=0, tiled=True)
    best = jnp.max(got_lse, axis=0)
    factor = jnp.exp(got_lse - best[None])
    summed_t = jnp.sum(factor, axis=0)
    summed_o = jnp.sum(got_out.astype(jnp.float32) * factor[..., None], axis=0)
    carried = (best.reshape(-1), summed_t.reshape(-1), summed_o.reshape(-1, head_dim))
    peak, totals, numer = joined(carried, fresh)
    result = (numer / totals[:, None]).astype(jnp.bfloat16)
    return result.reshape(tq_dev, 1, group, head_dim)


def solution(mesh):
    return jax.shard_map(
        on_device,
        mesh=mesh,
        in_specs=(
            P(("sess", "ctx"), "kvh", None, None),
            P(("sess", "ctx"), "kvh", None),
            P(("sess", "ctx"), "kvh", None),
            P(("sess", "kvh"), "ctx", None),
            P(("sess", "kvh"), "ctx", None),
            P("sess", None),
            P("sess"),
            P("sess"),
        ),
        out_specs=P(("sess", "ctx"), "kvh", None, None),
        check_vma=False,
    )
```

profile of v0, /device:TPU:1, one launch (start us, length us, event | category | flops | bytes accessed | tf_op | source)
XLA Modules:
  0.0 293.7 jit_solution(10283717166731381672)
XLA Ops:
  6.5 0.7 all-gather.2.cloned.1.call-update
  7.9 0.8 select_reduce_fusion
  8.7 0.1 compare_and_fusion
  8.8 104.5 %all-gather.2.cloned.1.call-done = bf16[256,1,16,128]{3,2,1,0:T(8,128)(2,1)} async-done(((bf16[16,1,16,128]{3,2,1,0:T(8,128)(2,1)}), bf16[256,1,16,128]{3,2,1,0:T(8,128)(2,1)}) %all-gather.2.cloned.1.call-update) | async-done | bytes 1048592 | tf_op jit(solution)/shard_map/all_gather | solution.py:72
  113.3 56.5 %while.12 = (s32[]{:T(128)}, f32[4,1024]{1,0:T(4,128)S(1)}, bf16[4,1024,128]{2,1,0:T(8,128)(2,1)}, pred[1,2048]{1,0:T(4,128)(4,1)S(1)}, bf16[4,1024,128]{2,1,0:T...) while((s32[]{:T(128)}, f32[4,1024]{1,0:T(4,128)S(1)}, ...), condition=%wide.region_4.5_spmd, body=%wide.region_1.4_spmd.sunk | while | flops 1097071616 | bytes 62441648 | solution.py:83
  113.3 0.0 copy-start.5
  113.4 2.7 fusion.56
  116.0 3.2 %copy-done = f32[1024,2048]{1,0:T(8,128)} copy-done((f32[1024,2048]{1,0:T(8,128)}, f32[1024,2048]{1,0:T(8,128)S(1)}, u32[]{:S(2)}) %copy-start) | copy-done | bytes 8388632 | tf_op jit(solution)/shard_map/while
  119.2 2.2 fusion.57
  121.5 0.1 dynamic_update_slice.12
  121.6 5.9 %fusion.58 = bf16[4,1024,128]{2,1,0:T(8,128)(2,1)} fusion(bf16[4,1024,128]{2,1,0:T(8,128)(2,1)} %get-tuple-element.131, s32[]{:T(128)S(6)} %copy.21, f32[1024,2048]{1,0:T(8,128)} %copy-done, f32[1024]{0:T(1024)S(1)} %get-tuple-element.117, pred[2048]{0:T(1024)(128)(4,1)S(1)} %reduce.4, bf16[1,2048,128]{2,1,0:T(8,128)(2,1)S(1)} %copy-done.5, ...), kind=kOutput, calls=%fused_computation.10.clone.1 | convolution fusion | flops 545521664 | bytes 9185284 | tf_op jit(solution)/shard_map/while/body/eval_jaxpr/dot_general | solution.py:24
  127.5 2.6 fusion.56
  130.1 3.2 %copy-done = f32[1024,2048]{1,0:T(8,128)} copy-done((f32[1024,2048]{1,0:T(8,128)}, f32[1024,2048]{1,0:T(8,128)S(1)}, u32[]{:S(2)}) %copy-start) | copy-done | bytes 8388632 | tf_op jit(solution)/shard_map/while
  133.3 2.2 fusion.57
  135.6 0.1 dynamic_update_slice.12
  135.7 5.9 %fusion.58 = bf16[4,1024,128]{2,1,0:T(8,128)(2,1)} fusion(bf16[4,1024,128]{2,1,0:T(8,128)(2,1)} %get-tuple-element.131, s32[]{:T(128)S(6)} %copy.21, f32[1024,2048]{1,0:T(8,128)} %copy-done, f32[1024]{0:T(1024)S(1)} %get-tuple-element.117, pred[2048]{0:T(1024)(128)(4,1)S(1)} %reduce.4, bf16[1,2048,128]{2,1,0:T(8,128)(2,1)S(1)} %copy-done.5, ...), kind=kOutput, calls=%fused_computation.10.clone.1 | convolution fusion | flops 545521664 | bytes 9185284 | tf_op jit(solution)/shard_map/while/body/eval_jaxpr/dot_general | solution.py:24
  141.6 2.6 fusion.56
  144.2 3.2 %copy-done = f32[1024,2048]{1,0:T(8,128)} copy-done((f32[1024,2048]{1,0:T(8,128)}, f32[1024,2048]{1,0:T(8,128)S(1)}, u32[]{:S(2)}) %copy-start) | copy-done | bytes 8388632 | tf_op jit(solution)/shard_map/while
  147.5 2.2 fusion.57
  149.7 0.1 dynamic_update_slice.12
  149.8 5.9 %fusion.58 = bf16[4,1024,128]{2,1,0:T(8,128)(2,1)} fusion(bf16[4,1024,128]{2,1,0:T(8,128)(2,1)} %get-tuple-element.131, s32[]{:T(128)S(6)} %copy.21, f32[1024,2048]{1,0:T(8,128)} %copy-done, f32[1024]{0:T(1024)S(1)} %get-tuple-element.117, pred[2048]{0:T(1024)(128)(4,1)S(1)} %reduce.4, bf16[1,2048,128]{2,1,0:T(8,128)(2,1)S(1)} %copy-done.5, ...), kind=kOutput, calls=%fused_computation.10.clone.1 | convolution fusion | flops 545521664 | bytes 9185284 | tf_op jit(solution)/shard_map/while/body/eval_jaxpr/dot_general | solution.py:24
  155.7 2.7 fusion.56
  158.4 3.2 %copy-done = f32[1024,2048]{1,0:T(8,128)} copy-done((f32[1024,2048]{1,0:T(8,128)}, f32[1024,2048]{1,0:T(8,128)S(1)}, u32[]{:S(2)}) %copy-start) | copy-done | bytes 8388632 | tf_op jit(solution)/shard_map/while
  161.6 2.2 fusion.57
  163.8 0.1 dynamic_update_slice.12
  163.9 5.9 %fusion.58 = bf16[4,1024,128]{2,1,0:T(8,128)(2,1)} fusion(bf16[4,1024,128]{2,1,0:T(8,128)(2,1)} %get-tuple-element.131, s32[]{:T(128)S(6)} %copy.21, f32[1024,2048]{1,0:T(8,128)} %copy-done, f32[1024]{0:T(1024)S(1)} %get-tuple-element.117, pred[2048]{0:T(1024)(128)(4,1)S(1)} %reduce.4, bf16[1,2048,128]{2,1,0:T(8,128)(2,1)S(1)} %copy-done.5, ...), kind=kOutput, calls=%fused_computation.10.clone.1 | convolution fusion | flops 545521664 | bytes 9185284 | tf_op jit(solution)/shard_map/while/body/eval_jaxpr/dot_general | solution.py:24
  169.8 0.1 broadcast_in_dim_reshape.10
  169.9 0.5 broadcast.222
  170.4 1.0 reduce.1
  171.4 0.1 reshape.312
  171.5 19.8 %all_to_all.21 = f32[16,1,256]{2,1,0:T(1,128)S(1)} all-to-all(f32[16,1,256]{2,1,0:T(1,128)S(1)} %reshape.312), channel_id=1, replica_groups=mesh['ctx'=16,'kvh'=8,'sess'=4] {'ctx'}, dimensions={0} | all-to-all | bytes 32768 | tf_op jit(solution)/shard_map/all_to_all | solution.py:87
  191.3 4.2 %all-to-all-start = ((bf16[1,256,16,128]{3,2,0,1:T(8,128)(2,1)}), bf16[1,256,16,128]{3,2,0,1:T(8,128)(2,1)S(1)}, u32[]{:S(2)}, u32[]{:S(2)}) async-start(bf16[1,256,16,128]{3,2,0,1:T(8,128)(2,1)} %bitcast.8), calls=%async_computation | async-start | bytes 2097152 | tf_op jit(solution)/shard_map/all_to_all | solution.py:86
  195.5 0.1 broadcast_in_dim.66
  195.6 0.1 le.50
  195.7 0.1 compare_and_fusion.1
  195.7 0.2 and_reduce_fusion
  196.0 0.1 copy.14
  196.1 51.8 %all_gather.10 = bf16[256,1,128]{2,0,1:T(8,128)(2,1)S(1)} all-gather(bf16[16,1,128]{2,0,1:T(8,128)(2,1)S(1)} %copy-done.2), channel_id=1, replica_groups=mesh['ctx'=16,'kvh'=8,'sess'=4] {'ctx'}, dimensions={0}, use_global_device_ids=true | all-gather | bytes 69632 | tf_op jit(solution)/shard_map/all_gather | solution.py:56
  247.9 35.7 %all_gather.11 = bf16[256,1,128]{2,0,1:T(8,128)(2,1)S(1)} all-gather(bf16[16,1,128]{2,0,1:T(8,128)(2,1)S(1)} %copy-done.3), channel_id=1, replica_groups=mesh['ctx'=16,'kvh'=8,'sess'=4] {'ctx'}, dimensions={0}, use_global_device_ids=true | all-gather | bytes 69632 | tf_op jit(solution)/shard_map/all_gather | solution.py:57
  283.6 0.2 fusion.47
  283.9 0.1 fusion.32
  283.9 0.7 reduce.2
  284.6 0.2 reshape.313
  284.9 0.1 reshape.306
  285.0 0.1 reshape.308
  285.1 0.7 fusion.26
  285.8 0.1 bitcast_multiply_fusion
  285.9 0.9 fusion.30
  (37 shorter events, 0.3 us)
Async XLA Ops:
  6.5 106.8 %all-gather.2.cloned.1.call-start = ((), (), s32[]{:S(2)}) async-start(), calls=%async_computation.2 | async-start | bytes 1114112 | tf_op jit(solution)/shard_map/all_gather | solution.py:72
  113.3 82.4 %copy-start.4 = (s32[4,2]{0,1:T(2,128)S(1)}, s32[4,2]{0,1:T(2,128)}, u32[]{:S(2)}) copy-start(s32[4,2]{0,1:T(2,128)} %param.15) | copy-start | bytes 100
  113.3 82.8 %copy-start.2 = (bf16[16,1,128]{2,0,1:T(8,128)(2,1)S(1)}, bf16[16,1,128]{2,0,1:T(8,128)(2,1)}, u32[]{:S(2)}) copy-start(bf16[16,1,128]{2,0,1:T(8,128)(2,1)} %param.11) | copy-start | bytes 12292
  113.3 134.6 %copy-start.3 = (bf16[16,1,128]{2,0,1:T(8,128)(2,1)S(1)}, bf16[16,1,128]{2,0,1:T(8,128)(2,1)}, u32[]{:S(2)}) copy-start(bf16[16,1,128]{2,0,1:T(8,128)(2,1)} %param.12) | copy-start | bytes 12292
  113.3 170.3 %copy-start.1 = (bf16[16,1,16,128]{3,2,1,0:T(8,128)(2,1)S(1)}, bf16[16,1,16,128]{3,2,1,0:T(8,128)(2,1)}, u32[]{:S(2)}) copy-start(bf16[16,1,16,128]{3,2,1,0:T(8,128)(2,1)} %param.10) | copy-start | bytes 196612
  113.3 8.2 %copy-start.5 = (bf16[1,2048,128]{2,1,0:T(8,128)(2,1)S(1)}, bf16[1,2048,128]{2,1,0:T(8,128)(2,1)}, u32[]{:S(2)}) copy-start(bf16[1,2048,128]{2,1,0:T(8,128)(2,1)} %get-tuple-element.145) | copy-start | bytes 1572868 | tf_op jit(solution)/shard_map/while
  116.0 3.2 %copy-start = (f32[1024,2048]{1,0:T(8,128)}, f32[1024,2048]{1,0:T(8,128)S(1)}, u32[]{:S(2)}) copy-start(f32[1024,2048]{1,0:T(8,128)S(1)} %get-tuple-element.118) | copy-start | bytes 25165828 | tf_op jit(solution)/shard_map/while
  127.5 8.2 %copy-start.5 = (bf16[1,2048,128]{2,1,0:T(8,128)(2,1)S(1)}, bf16[1,2048,128]{2,1,0:T(8,128)(2,1)}, u32[]{:S(2)}) copy-start(bf16[1,2048,128]{2,1,0:T(8,128)(2,1)} %get-tuple-element.145) | copy-start | bytes 1572868 | tf_op jit(solution)/shard_map/while
  130.1 3.2 %copy-start = (f32[1024,2048]{1,0:T(8,128)}, f32[1024,2048]{1,0:T(8,128)S(1)}, u32[]{:S(2)}) copy-start(f32[1024,2048]{1,0:T(8,128)S(1)} %get-tuple-element.118) | copy-start | bytes 25165828 | tf_op jit(solution)/shard_map/while
  141.6 8.2 %copy-start.5 = (bf16[1,2048,128]{2,1,0:T(8,128)(2,1)S(1)}, bf16[1,2048,128]{2,1,0:T(8,128)(2,1)}, u32[]{:S(2)}) copy-start(bf16[1,2048,128]{2,1,0:T(8,128)(2,1)} %get-tuple-element.145) | copy-start | bytes 1572868 | tf_op jit(solution)/shard_map/while
  144.2 3.2 %copy-start = (f32[1024,2048]{1,0:T(8,128)}, f32[1024,2048]{1,0:T(8,128)S(1)}, u32[]{:S(2)}) copy-start(f32[1024,2048]{1,0:T(8,128)S(1)} %get-tuple-element.118) | copy-start | bytes 25165828 | tf_op jit(solution)/shard_map/while
  155.7 8.2 %copy-start.5 = (bf16[1,2048,128]{2,1,0:T(8,128)(2,1)S(1)}, bf16[1,2048,128]{2,1,0:T(8,128)(2,1)}, u32[]{:S(2)}) copy-start(bf16[1,2048,128]{2,1,0:T(8,128)(2,1)} %get-tuple-element.145) | copy-start | bytes 1572868 | tf_op jit(solution)/shard_map/while
  158.3 3.2 %copy-start = (f32[1024,2048]{1,0:T(8,128)}, f32[1024,2048]{1,0:T(8,128)S(1)}, u32[]{:S(2)}) copy-start(f32[1024,2048]{1,0:T(8,128)S(1)} %get-tuple-element.118) | copy-start | bytes 25165828 | tf_op jit(solution)/shard_map/while
  191.3 93.8 %all-to-all-start = ((bf16[1,256,16,128]{3,2,0,1:T(8,128)(2,1)}), bf16[1,256,16,128]{3,2,0,1:T(8,128)(2,1)S(1)}, u32[]{:S(2)}, u32[]{:S(2)}) async-start(bf16[1,256,16,128]{3,2,0,1:T(8,128)(2,1)} %bitcast.8), calls=%async_computation | async-start | bytes 2097152 | tf_op jit(solution)/shard_map/all_to_all | solution.py:86
Sparse Core Ops, SparseCore 0:
  9.4 103.8 all-gather.1
where the time goes:
time: 294 us
  blocking collectives  107 us (36%)
  waiting for transfers between devices  105 us (36%)
  matrix products  35.2 us (12%)
  local copies, waits for them, and re-layouts  14.6 us (5%)
  between operations  14.2 us (5%)
  other arithmetic  12.7 us (4%)
  starting transfers between devices  4.21 us (1%)
    all_gather x1, waiting for transfers between devices, on_device(): every = lax.all_gather(queries, 'ctx', axis=0, tiled=True)  105 us
    all_gather x1, blocking collectives, on_device(): lax.all_gather(new_keys, 'ctx', axis=0, tiled=True)  51.8 us
    all_gather x1, blocking collectives, on_device(): lax.all_gather(new_values, 'ctx', axis=0, tiled=True)  35.7 us
    dot_general x5, matrix products, partial_attend(): jnp.dot(weights.astype(jnp.bfloat16), values, preferred_element_type=jnp....  24.4 us
    all_to_all x1, blocking collectives, on_device(): lax.all_to_all(lses[None], 'ctx', split_axis=1, concat_axis=0, tiled=True)  19.8 us
    while x16, local copies, waits for them, and re-layouts  12.9 us
    dot_general x5, matrix products, partial_attend(): jnp.einsum('rd,cd->rc', qrows, keys, preferred_element_type=jnp.float32)  10.8 us
    reduce_sum x5, other arithmetic, partial_attend(): totals = jnp.sum(weights, axis=1)  8.9 us
  transfers between devices with their start and end apart: 2, of which 1 were waited for; matrix products, arithmetic and copies ran while one was open for 1% of the time, Pallas kernels for 0%

commit v1 on v0

v1 whole, which is shorter than its diff:
```python
import functools
import math

import jax
import jax.numpy as jnp
from jax import lax
from jax.experimental import pallas as pl
from jax.experimental.pallas import tpu as pltpu
from jax.sharding import Mesh
from jax.sharding import PartitionSpec as P

F32 = jnp.float32
BF16 = jnp.bfloat16
HIDDEN = -1e30
CHUNK = 1024
TILE = 128
EXTRA = 16
NT = (((1,), (1,)), ((), ()))


def pieces(x):
    hi = x.astype(BF16).astype(F32)
    mid = (x - hi).astype(BF16).astype(F32)
    return hi, mid, x - hi - mid


def write_message(out, numer, peak, total):
    dim = numer.shape[0]
    out[0:dim, :] = numer.astype(BF16)
    row = lax.broadcasted_iota(jnp.int32, (EXTRA, numer.shape[1]), 0)
    tail = jnp.zeros((EXTRA, numer.shape[1]), F32)
    for at, piece in enumerate(pieces(peak) + pieces(total)):
        tail = jnp.where(row == at, piece, tail)
    out[dim : dim + EXTRA, :] = tail.astype(BF16)


def read_message(ref):
    dim = ref.shape[0] - EXTRA
    tail = ref[dim : dim + EXTRA, :].astype(F32)
    peak = tail[0:1] + tail[1:2] + tail[2:3]
    total = tail[3:4] + tail[4:5] + tail[5:6]
    return ref[0:dim, :].astype(F32), peak, total


def merge(refs):
    parts = [read_message(ref) for ref in refs]
    peak = functools.reduce(jnp.maximum, [p[1] for p in parts])
    factors = [jnp.exp2(p[1] - peak) for p in parts]
    total = sum(p[2] * f for p, f in zip(parts, factors))
    numer = sum(p[0] * f for p, f in zip(parts, factors))
    return numer, peak, total


def pack_kernel(count, where, *refs):
    k_hbm, v_hbm, nk_hbm, nv_hbm, q_hbm, cache_len, doc_start = refs[:7]
    pack, rep = refs[7:9]
    kbuf, vbuf, nvbuf, qsem, ksem, vsem, nsem = refs[9:]
    rows, dim = kbuf.shape
    new = nvbuf.shape[0]
    me = where()
    first = lax.div(jnp.maximum(doc_start[0] - me + count - 1, 0), count)
    limit = cache_len[me]

    q_copies = [pltpu.make_async_copy(q_hbm, rep.at[j], qsem.at[j]) for j in range(rep.shape[0])]
    k_copy = pltpu.make_async_copy(k_hbm.at[0], kbuf, ksem)
    v_copy = pltpu.make_async_copy(v_hbm.at[0], vbuf, vsem)
    nk_copy = pltpu.make_async_copy(nk_hbm, pack.at[pl.ds(rows, new)], nsem.at[0])
    nv_copy = pltpu.make_async_copy(nv_hbm, nvbuf, nsem.at[1])
    copies = [*q_copies, nk_copy, nv_copy]
    for copy in [k_copy, v_copy, *copies]:
        copy.start()

    safe = rows // 8
    step = 4 * TILE
    base = rows + new
    k_copy.wait()
    spare = kbuf[safe : safe + 16, :][0:1].astype(F32)
    for at in range(0, rows, step):
        slot = lax.broadcasted_iota(jnp.int32, (step, dim), 0) + at
        ok = (slot >= first) & (slot < limit)
        pack[at : at + step, :] = jnp.where(ok, kbuf[at : at + step, :].astype(F32), spare).astype(BF16)
    v_copy.wait()
    for at in range(0, rows, TILE):
        to = base + at // TILE * (dim + EXTRA)
        slot = lax.broadcasted_iota(jnp.int32, (TILE, dim), 0) + at
        ok = (slot >= first) & (slot < limit)
        values = jnp.where(ok, vbuf[at : at + TILE, :].astype(F32), 0.0)
        pack[to : to + dim, :] = values.T.astype(BF16)
        slot = lax.broadcasted_iota(jnp.int32, (EXTRA, TILE), 1) + at
        row = lax.broadcasted_iota(jnp.int32, (EXTRA, TILE), 0)
        ok = (slot >= first) & (slot < limit) & (row == 0)
        pack[to + dim : to + dim + EXTRA, :] = jnp.where(ok, 1.0, 0.0).astype(BF16)
    for copy in copies:
        copy.wait()
    to = base + rows // TILE * (dim + EXTRA)
    odd = lax.rem(me, 2) == 1
    own = nvbuf[...].astype(F32)
    none = jnp.zeros_like(own)
    both = [jnp.where(odd, none, own), jnp.where(odd, own, none), jnp.zeros((TILE - 2 * new, dim), F32)]
    pack[to : to + dim, :] = jnp.concatenate(both, axis=0).T.astype(BF16)
    row = lax.broadcasted_iota(jnp.int32, (EXTRA, TILE), 0)
    column = lax.broadcasted_iota(jnp.int32, (EXTRA, TILE), 1)
    mine = lax.div(column, new) == lax.rem(me, 2)
    pack[to + dim : to + dim + EXTRA, :] = jnp.where((row == 0) & mine, 1.0, 0.0).astype(BF16)


def fresh_mask(me, owner, spans, new, group, rows):
    key = lax.broadcasted_iota(jnp.int32, (2 * new, rows), 0) + (me - lax.rem(me, 2)) * new
    token = lax.div(lax.broadcasted_iota(jnp.int32, (1, rows), 1), group) + owner * new
    ok = key <= token
    for k in range(spans.shape[1]):
        lo, hi = spans[0, k], spans[1, k]
        ok = ok | ((token >= lo) & (token < hi) & (key >= lo) & (key < hi))
    return ok


def attend_kernel(where, away, cache_dev, new, group, scale2, spans, own, other, q_ref, out, s0, s1, fresh_k, fresh_v):
    n, rows, dim = q_ref.shape
    me = where()
    core = lax.rem(me, 2)
    quad = (me - lax.rem(me, 2 * n)) ^ (2 * n if away else 0)
    base = cache_dev + new
    tall = dim + EXTRA
    s_refs = (s0, s1)

    odd = core == 1
    mine, theirs = own[cache_dev:base, :].astype(F32), other[cache_dev:base, :].astype(F32)
    fresh_k[0:new, :] = jnp.where(odd, theirs, mine).astype(BF16)
    fresh_k[new : 2 * new, :] = jnp.where(odd, mine, theirs).astype(BF16)
    at = base + cache_dev // TILE * tall
    fresh_v[...] = (own[at : at + tall, :].astype(F32) + other[at : at + tall, :].astype(F32)).astype(BF16)

    tiles = [(which, at) for which in (0, 1) for at in range(0, cache_dev, CHUNK)] + [None]

    def scores(b, tile, peak):
        if tile is None:
            s = lax.dot_general(fresh_k[...], q_ref[b], NT, preferred_element_type=F32)
            s = jnp.where(fresh_mask(me, quad + 2 * b + core, spans, new, group, rows), s, HIDDEN)
            to, size = 2 * cache_dev, 2 * new
        else:
            which, at = tile
            s = lax.dot_general((own, other)[which][at : at + CHUNK, :], q_ref[b], NT, preferred_element_type=F32)
            to, size = which * cache_dev + at, CHUNK
        s_refs[b % 2][to : to + size, :] = s
        top = jnp.max(s.reshape(size // 8, 8, rows), axis=0)
        return top if peak is None else jnp.maximum(peak, top)

    def weigh(b, tile, peak, acc):
        if tile is None:
            s = s_refs[b % 2][2 * cache_dev : 2 * cache_dev + 2 * new, :]
            p = jnp.exp2((s - peak) * scale2)
            p = jnp.concatenate([p, jnp.zeros((TILE - 2 * new, rows), F32)], axis=0).astype(BF16)
            v = fresh_v[...]
        else:
            which, at = tile
            to = which * cache_dev + at
            p = jnp.exp2((s_refs[b % 2][to : to + CHUNK, :] - peak) * scale2).astype(BF16)
            starts = [base + (at // TILE + j) * tall for j in range(CHUNK // TILE)]
            v = jnp.concatenate([(own, other)[which][i : i + tall, :] for i in starts], axis=1)
        o = jnp.dot(v, p, preferred_element_type=F32)
        return o if acc is None else acc + o

    peak = None
    for tile in tiles:
        peak = scores(0, tile, peak)
    for b in range(n):
        top = jnp.max(peak, axis=0, keepdims=True)
        acc, peak = None, None
        for tile in tiles:
            acc = weigh(b, tile, top, acc)
            if b + 1 < n:
                peak = scores(b + 1, tile, peak)
        write_message(out.at[b], acc[0:dim], top * scale2, acc[dim : dim + 1])


def merge_kernel(got, out):
    write_message(out, *merge([got.at[j] for j in range(got.shape[0])]))


def final_kernel(got, back, out):
    numer, _, total = merge([got.at[j] for j in range(got.shape[0])] + [back])
    out[...] = (numer / total).T.astype(BF16)


def on_device(queries, new_keys, new_values, cache_k, cache_v, span_bounds, cache_len, doc_start):
    far, near, cores = (lax.axis_size(name) for name in ("far", "near", "core"))
    new, _, group, dim = queries.shape
    rows = new * group
    cache_dev = cache_k.shape[1]
    packed = cache_dev + new + (cache_dev // TILE + 1) * (dim + EXTRA)
    scale2 = math.log2(math.e) / math.sqrt(dim)

    def where():
        return (lax.axis_index("far") * near + lax.axis_index("near")) * cores + lax.axis_index("core")

    def across(x, axis):
        return lax.ppermute(x, axis, [(0, 1), (1, 0)])

    def quad(x):
        return lax.all_to_all(x, "near", split_axis=0, concat_axis=0, tiled=True)

    hbm = pl.BlockSpec(memory_space=pltpu.HBM)
    vmem = pl.BlockSpec(memory_space=pltpu.VMEM)
    smem = pl.BlockSpec(memory_space=pltpu.SMEM)
    params = pltpu.CompilerParams(vmem_limit_bytes=32 * 1024 * 1024)
    message = jax.ShapeDtypeStruct((dim + EXTRA, rows), BF16)
    dma = pltpu.SemaphoreType.DMA

    q = queries.reshape(rows, dim)
    q_far = across(q, "far")
    own, q_rep = pl.pallas_call(
        functools.partial(pack_kernel, far * near * cores, where),
        out_shape=[jax.ShapeDtypeStruct((packed, dim), BF16), jax.ShapeDtypeStruct((near, rows, dim), BF16)],
        in_specs=[hbm] * 5 + [smem] * 2,
        out_specs=[vmem] * 2,
        scratch_shapes=[
            pltpu.VMEM((cache_dev, dim), BF16),
            pltpu.VMEM((cache_dev, dim), BF16),
            pltpu.VMEM((new, dim), BF16),
            dma((near,)),
            dma,
            dma,
            dma((2,)),
        ],
        compiler_params=params,
        name="pack",
    )(cache_k, cache_v, new_keys.reshape(new, dim), new_values.reshape(new, dim), q, cache_len, doc_start)
    q_near = quad(q_rep)
    other = across(own, "core")
    q_far = quad(jnp.broadcast_to(q_far[None], (near, rows, dim)))

    spans = span_bounds.T
    cost = pl.CostEstimate(
        flops=4 * near * rows * 2 * cache_dev * dim,
        bytes_accessed=4 << 20,
        transcendentals=near * rows * 2 * cache_dev,
    )

    def attend(blocks, away, name):
        return pl.pallas_call(
            functools.partial(attend_kernel, where, away, cache_dev, new, group, scale2),
            out_shape=jax.ShapeDtypeStruct((near,) + message.shape, BF16),
            in_specs=[smem] + [vmem] * 3,
            out_specs=vmem,
            scratch_shapes=[pltpu.VMEM((2 * cache_dev + 2 * new, rows), F32)] * 2
            + [pltpu.VMEM((2 * new, dim), BF16), pltpu.VMEM((dim + EXTRA, TILE), BF16)],
            compiler_params=params,
            cost_estimate=cost,
            name=name,
        )(spans, own, other, blocks)

    near_out = attend(q_near, False, "near_blocks")
    far_out = attend(q_far, True, "far_blocks")
    far_got = quad(far_out)
    near_got = quad(near_out)
    far_sum = pl.pallas_call(
        merge_kernel, out_shape=message, in_specs=[vmem], out_specs=vmem, compiler_params=params, name="merge_far"
    )(far_got)
    back = across(far_sum, "far")
    result = pl.pallas_call(
        final_kernel,
        out_shape=jax.ShapeDtypeStruct((rows, dim), BF16),
        in_specs=[vmem] * 2,
        out_specs=vmem,
        compiler_params=params,
        name="merge_all",
    )(near_got, back)
    return result.reshape(new, 1, group, dim)


def solution(mesh):
    ctx, kvh, sess = (mesh.shape[name] for name in ("ctx", "kvh", "sess"))
    devices = mesh.devices.reshape(2, ctx // 4, 2, kvh, sess)
    split = Mesh(devices, ("far", "near", "core", "kvh", "sess"))
    ctx = ("far", "near", "core")
    return jax.shard_map(
        on_device,
        mesh=split,
        in_specs=(
            P(("sess",) + ctx, "kvh", None, None),
            P(("sess",) + ctx, "kvh", None),
            P(("sess",) + ctx, "kvh", None),
            P(("sess", "kvh"), ctx, None),
            P(("sess", "kvh"), ctx, None),
            P("sess", None),
            P("sess"),
            P("sess"),
        ),
        out_specs=P(("sess",) + ctx, "kvh", None, None),
        check_vma=False,
    )
```

time: 294 us -> 78.2 us (0.27)
  the two profiles are of different devices: /device:TPU:1 before, /device:TPU:74 now
where the time goes in v1:
time: 78.2 us; the launch traced here: 77.5 us
  starting transfers between devices  41 us (52%)
  Pallas kernels  19.9 us (25%)
  waiting for transfers between devices  11.2 us (14%)
  local copies, waits for them, and re-layouts  4.65 us (6%)
    all_to_all x4, starting transfers between devices, quad(): return lax.all_to_all(x, 'near', split_axis=0, concat_axis=0, tiled=True)  21.6 us
    ppermute x3, starting transfers between devices, across(): return lax.ppermute(x, axis, [(0, 1), (1, 0)])  19.3 us
    pallas_call x2, Pallas kernels, attend(): pl.pallas_call(functools.partial(attend_kernel, where, away, cache_dev, n...  16.7 us
    ppermute x3, waiting for transfers between devices, across(): return lax.ppermute(x, axis, [(0, 1), (1, 0)])  11.2 us
    unnamed x14, local copies, waits for them, and re-layouts  3.91 us
    pallas_call x1, Pallas kernels, on_device(): pl.pallas_call(functools.partial(pack_kernel, far * near * cores, where),...  2.34 us
  transfers between devices with their start and end apart: 7, of which 2 were waited for; matrix products, arithmetic and copies ran while one was open for 0% of the time, Pallas kernels for 25%

profile of v1, /device:TPU:74, one launch (start us, length us, event | category | flops | bytes accessed | tf_op | source)
XLA Modules:
  0.0 77.5 jit_solution(2452359417805885177)
XLA Ops:
  0.0 0.0 copy-start
  0.0 9.2 %collective-permute-start.1 = (bf16[256,128]{1,0:T(8,128)(2,1)}, bf16[256,128]{1,0:T(8,128)(2,1)S(1)}, u32[]{:S(2)}, u32[]{:S(2)}) collective-permute-start(bf16[256,128]{1,0:T(8,128)(2,1)} %bitcast.7), channel_id=1, source_target_pairs={{0,256},{256,0},{1,257},{257,1},{2,258},{258,2},{3,259},{259,3},{4... | collective-permute-start | bytes 196616 | tf_op jit(solution)/shard_map/ppermute | solution.py:197
  9.2 3.8 %collective-permute-done.1 = bf16[256,128]{1,0:T(8,128)(2,1)S(1)} collective-permute-done((bf16[256,128]{1,0:T(8,128)(2,1)}, bf16[256,128]{1,0:T(8,128)(2,1)S(1)}, u32[]{:S(2)}, u32[]{:S(2)}) %collective-permute-start.1) | collective-permute-done | bytes 65568 | tf_op jit(solution)/shard_map/ppermute | solution.py:197
  13.1 0.7 broadcast_in_dim.2
  13.8 0.0 copy-start.6
  13.8 6.3 %all-to-all-start.2 = ((bf16[4,256,128]{2,1,0:T(8,128)(2,1)}), bf16[4,256,128]{2,1,0:T(8,128)(2,1)S(1)}, u32[]{:S(2)}, u32[]{:S(2)}) async-start(bf16[4,256,128]{2,1,0:T(8,128)(2,1)} %broadcast_in_dim.2), calls=%async_computation.2 | async-start | bytes 524288 | tf_op jit(solution)/shard_map/all_to_all | solution.py:200
  20.8 0.0 copy-done
  20.8 0.0 copy-start.1
  20.8 1.0 %copy-done.1 = bf16[1,2048,128]{2,1,0:T(8,128)(2,1)S(1)} copy-done((bf16[1,2048,128]{2,1,0:T(8,128)(2,1)S(1)}, bf16[1,2048,128]{2,1,0:T(8,128)(2,1)}, u32[]{:S(2)}) %copy-start.1) | copy-done | bytes 524312
  21.9 0.0 copy-start.2
  21.9 0.8 %copy-done.2 = bf16[16,1,16,128]{3,2,1,0:T(8,128)(2,1)S(1)} copy-done((bf16[16,1,16,128]{3,2,1,0:T(8,128)(2,1)S(1)}, bf16[16,1,16,128]{3,2,1,0:T(8,128)(2,1)}, u32[]{:S(2)}) %copy-start.2) | copy-done | bytes 65560
  22.7 0.0 copy-start.3
  22.7 0.7 copy-done.3
  23.4 0.0 copy-start.4
  23.4 0.7 copy-done.4
  24.1 0.0 copy-start.5
  24.1 0.7 copy-done.5
  24.7 2.3 %pack.1 = (bf16[4512,128]{1,0:T(8,128)(2,1)S(1)}, bf16[4,256,128]{2,1,0:T(8,128)(2,1)}) custom-call(bf16[1,2048,128]{2,1,0:T(8,128)(2,1)S(1)} %copy-done, bf16[1,2048,128]{2,1,0:T(8,128)(2,1)S(1)} %copy-done.1, bf16[16,128]{1,0:T(8,128)(2,1)S(1)} %bitcast.9, bf16[16,128]{1,0:T(8,128)(2,1)S(1)} %bitcast.10, bf16[256,128]{1,0:T(8,128)(2,1)S(1)} %bitcast.8, ...), custom_call_target="tpu_custom_call" | custom-call | tf_op jit(solution)/shard_map/pack/pallas_call | solution.py:211
  27.1 1.9 %collective-permute-start = (bf16[4512,128]{1,0:T(8,128)(2,1)S(1)}, bf16[4512,128]{1,0:T(8,128)(2,1)S(1)}, u32[]{:S(2)}, u32[]{:S(2)}) collective-permute-start(bf16[4512,128]{1,0:T(8,128)(2,1)S(1)} %get-tuple-element.7.own), channel_id=1, source_target_pairs={{0,32},{32,0},{1,33},{33,1},{2,34},{34,2},{3,35},{35,3},{4,36},{36... | collective-permute-start | bytes 3465224 | tf_op jit(solution)/shard_map/ppermute | solution.py:197
  29.0 0.0 all-to-all-done.2.q_ref
  29.0 5.1 %all-to-all-start = ((bf16[4,256,128]{2,1,0:T(8,128)(2,1)}), bf16[4,256,128]{2,1,0:T(8,128)(2,1)S(1)}, u32[]{:S(2)}, u32[]{:S(2)}) async-start(bf16[4,256,128]{2,1,0:T(8,128)(2,1)} %get-tuple-element.8), calls=%async_computation | async-start | bytes 524288 | tf_op jit(solution)/shard_map/all_to_all | solution.py:200
  34.1 0.0 collective-permute-done.other
  34.1 0.0 copy-done.6
  34.1 8.3 %far_blocks.1 = bf16[4,144,256]{2,1,0:T(8,128)(2,1)} custom-call(s32[2,4]{1,0:T(2,128)S(1)} %bitcast.11, bf16[4512,128]{1,0:T(8,128)(2,1)S(1)} %get-tuple-element.7.own, bf16[4512,128]{1,0:T(8,128)(2,1)S(1)} %collective-permute-done.other, bf16[4,256,128]{2,1,0:T(8,128)(2,1)S(1)} %all-to-all-done.2.q_ref), custom_call_target="tpu_custom_call" | custom-call | flops 2147483648 | bytes 4194304 | tf_op jit(solution)/shard_map/far_blocks/pallas_call | solution.py:240
  42.5 0.0 all-to-all-done.q_ref
  42.5 5.1 %all-to-all-start.3 = ((bf16[4,144,256]{2,1,0:T(8,128)(2,1)}), bf16[4,144,256]{2,1,0:T(8,128)(2,1)S(1)}, u32[]{:S(2)}, u32[]{:S(2)}) async-start(bf16[4,144,256]{2,1,0:T(8,128)(2,1)} %far_blocks.1), calls=%async_computation.3 | async-start | bytes 589824 | tf_op jit(solution)/shard_map/all_to_all | solution.py:200
  47.6 8.4 %near_blocks.1 = bf16[4,144,256]{2,1,0:T(8,128)(2,1)} custom-call(s32[2,4]{1,0:T(2,128)S(1)} %bitcast.12, bf16[4512,128]{1,0:T(8,128)(2,1)S(1)} %get-tuple-element.7.own, bf16[4512,128]{1,0:T(8,128)(2,1)S(1)} %collective-permute-done.other, bf16[4,256,128]{2,1,0:T(8,128)(2,1)S(1)} %all-to-all-done.q_ref), custom_call_target="tpu_custom_call" | custom-call | flops 2147483648 | bytes 4194304 | tf_op jit(solution)/shard_map/near_blocks/pallas_call | solution.py:240
  55.9 0.0 all-to-all-done.3.got
  55.9 5.1 %all-to-all-start.1 = ((bf16[4,144,256]{2,1,0:T(8,128)(2,1)}), bf16[4,144,256]{2,1,0:T(8,128)(2,1)S(1)}, u32[]{:S(2)}, u32[]{:S(2)}) async-start(bf16[4,144,256]{2,1,0:T(8,128)(2,1)} %near_blocks.1), calls=%async_computation.1 | async-start | bytes 589824 | tf_op jit(solution)/shard_map/all_to_all | solution.py:200
  61.0 0.1 merge_far.1
  61.1 8.2 %collective-permute-start.2 = (bf16[144,256]{1,0:T(8,128)(2,1)S(1)}, bf16[144,256]{1,0:T(8,128)(2,1)S(1)}, u32[]{:S(2)}, u32[]{:S(2)}) collective-permute-start(bf16[144,256]{1,0:T(8,128)(2,1)S(1)} %merge_far.1), channel_id=1, source_target_pairs={{0,256},{256,0},{1,257},{257,1},{2,258},{258,2},{3,259},{259,3},{4... | collective-permute-start | bytes 221192 | tf_op jit(solution)/shard_map/ppermute | solution.py:197
  69.3 0.0 all-to-all-done.1.got
  69.3 7.3 %collective-permute-done.2.back = bf16[144,256]{1,0:T(8,128)(2,1)S(1)} collective-permute-done((bf16[144,256]{1,0:T(8,128)(2,1)S(1)}, bf16[144,256]{1,0:T(8,128)(2,1)S(1)}, u32[]{:S(2)}, u32[]{:S(2)}) %collective-permute-start.2) | collective-permute-done | bytes 73760 | tf_op jit(solution)/shard_map/ppermute | solution.py:197
  76.7 0.8 %merge_all.1 = bf16[256,128]{1,0:T(8,128)(2,1)} custom-call(bf16[4,144,256]{2,1,0:T(8,128)(2,1)S(1)} %all-to-all-done.1.got, bf16[144,256]{1,0:T(8,128)(2,1)S(1)} %collective-permute-done.2.back), custom_call_target="tpu_custom_call" | custom-call | tf_op jit(solution)/shard_map/merge_all/pallas_call | solution.py:260
Async XLA Ops:
  0.0 20.8 %copy-start = (bf16[1,2048,128]{2,1,0:T(8,128)(2,1)S(1)}, bf16[1,2048,128]{2,1,0:T(8,128)(2,1)}, u32[]{:S(2)}) copy-start(bf16[1,2048,128]{2,1,0:T(8,128)(2,1)} %refs_0_.1) | copy-start | bytes 1572868
  0.0 13.1 %collective-permute-start.1 = (bf16[256,128]{1,0:T(8,128)(2,1)}, bf16[256,128]{1,0:T(8,128)(2,1)S(1)}, u32[]{:S(2)}, u32[]{:S(2)}) collective-permute-start(bf16[256,128]{1,0:T(8,128)(2,1)} %bitcast.7), channel_id=1, source_target_pairs={{0,256},{256,0},{1,257},{257,1},{2,258},{258,2},{3,259},{259,3},{4... | collective-permute-start | bytes 196616 | tf_op jit(solution)/shard_map/ppermute | solution.py:197
  13.8 20.3 %copy-start.6 = (s32[4,2]{0,1:T(2,128)S(1)}, s32[4,2]{0,1:T(2,128)}, u32[]{:S(2)}) copy-start(s32[4,2]{0,1:T(2,128)} %param.13) | copy-start | bytes 100
  13.8 15.2 %all-to-all-start.2 = ((bf16[4,256,128]{2,1,0:T(8,128)(2,1)}), bf16[4,256,128]{2,1,0:T(8,128)(2,1)S(1)}, u32[]{:S(2)}, u32[]{:S(2)}) async-start(bf16[4,256,128]{2,1,0:T(8,128)(2,1)} %broadcast_in_dim.2), calls=%async_computation.2 | async-start | bytes 524288 | tf_op jit(solution)/shard_map/all_to_all | solution.py:200
  20.8 1.0 %copy-start.1 = (bf16[1,2048,128]{2,1,0:T(8,128)(2,1)S(1)}, bf16[1,2048,128]{2,1,0:T(8,128)(2,1)}, u32[]{:S(2)}) copy-start(bf16[1,2048,128]{2,1,0:T(8,128)(2,1)} %refs_1_.1) | copy-start | bytes 1572868
  21.9 0.8 %copy-start.2 = (bf16[16,1,16,128]{3,2,1,0:T(8,128)(2,1)S(1)}, bf16[16,1,16,128]{3,2,1,0:T(8,128)(2,1)}, u32[]{:S(2)}) copy-start(bf16[16,1,16,128]{3,2,1,0:T(8,128)(2,1)} %param.8) | copy-start | bytes 196612
  22.7 0.7 copy-start.3
  23.4 0.7 copy-start.4
  24.1 0.7 copy-start.5
  27.1 7.0 %collective-permute-start = (bf16[4512,128]{1,0:T(8,128)(2,1)S(1)}, bf16[4512,128]{1,0:T(8,128)(2,1)S(1)}, u32[]{:S(2)}, u32[]{:S(2)}) collective-permute-start(bf16[4512,128]{1,0:T(8,128)(2,1)S(1)} %get-tuple-element.7.own), channel_id=1, source_target_pairs={{0,32},{32,0},{1,33},{33,1},{2,34},{34,2},{3,35},{35,3},{4,36},{36... | collective-permute-start | bytes 3465224 | tf_op jit(solution)/shard_map/ppermute | solution.py:197
  29.0 13.5 %all-to-all-start = ((bf16[4,256,128]{2,1,0:T(8,128)(2,1)}), bf16[4,256,128]{2,1,0:T(8,128)(2,1)S(1)}, u32[]{:S(2)}, u32[]{:S(2)}) async-start(bf16[4,256,128]{2,1,0:T(8,128)(2,1)} %get-tuple-element.8), calls=%async_computation | async-start | bytes 524288 | tf_op jit(solution)/shard_map/all_to_all | solution.py:200
  42.5 13.5 %all-to-all-start.3 = ((bf16[4,144,256]{2,1,0:T(8,128)(2,1)}), bf16[4,144,256]{2,1,0:T(8,128)(2,1)S(1)}, u32[]{:S(2)}, u32[]{:S(2)}) async-start(bf16[4,144,256]{2,1,0:T(8,128)(2,1)} %far_blocks.1), calls=%async_computation.3 | async-start | bytes 589824 | tf_op jit(solution)/shard_map/all_to_all | solution.py:200
  55.9 13.4 %all-to-all-start.1 = ((bf16[4,144,256]{2,1,0:T(8,128)(2,1)}), bf16[4,144,256]{2,1,0:T(8,128)(2,1)S(1)}, u32[]{:S(2)}, u32[]{:S(2)}) async-start(bf16[4,144,256]{2,1,0:T(8,128)(2,1)} %near_blocks.1), calls=%async_computation.1 | async-start | bytes 589824 | tf_op jit(solution)/shard_map/all_to_all | solution.py:200
  61.1 15.6 %collective-permute-start.2 = (bf16[144,256]{1,0:T(8,128)(2,1)S(1)}, bf16[144,256]{1,0:T(8,128)(2,1)S(1)}, u32[]{:S(2)}, u32[]{:S(2)}) collective-permute-start(bf16[144,256]{1,0:T(8,128)(2,1)S(1)} %merge_far.1), channel_id=1, source_target_pairs={{0,256},{256,0},{1,257},{257,1},{2,258},{258,2},{3,259},{259,3},{4... | collective-permute-start | bytes 221192 | tf_op jit(solution)/shard_map/ppermute | solution.py:197

commit v2 on v1

--- a/solution.py
+++ b/solution.py
@@ -12,8 +12,9 @@
 F32 = jnp.float32
 BF16 = jnp.bfloat16
 HIDDEN = -1e30
-CHUNK = 1024
+CHUNK = 512
 TILE = 128
+WIDE = 512
 EXTRA = 16
 NT = (((1,), (1,)), ((), ()))
 
@@ -52,21 +53,19 @@
 
 
 def pack_kernel(count, where, *refs):
-    k_hbm, v_hbm, nk_hbm, nv_hbm, q_hbm, cache_len, doc_start = refs[:7]
-    pack, rep = refs[7:9]
-    kbuf, vbuf, nvbuf, qsem, ksem, vsem, nsem = refs[9:]
+    k_hbm, v_hbm, nk_hbm, nv_hbm, cache_len, doc_start, pack = refs[:7]
+    kbuf, vbuf, nvbuf, ksem, vsem, nsem = refs[7:]
     rows, dim = kbuf.shape
     new = nvbuf.shape[0]
     me = where()
     first = lax.div(jnp.maximum(doc_start[0] - me + count - 1, 0), count)
     limit = cache_len[me]
 
-    q_copies = [pltpu.make_async_copy(q_hbm, rep.at[j], qsem.at[j]) for j in range(rep.shape[0])]
     k_copy = pltpu.make_async_copy(k_hbm.at[0], kbuf, ksem)
     v_copy = pltpu.make_async_copy(v_hbm.at[0], vbuf, vsem)
     nk_copy = pltpu.make_async_copy(nk_hbm, pack.at[pl.ds(rows, new)], nsem.at[0])
     nv_copy = pltpu.make_async_copy(nv_hbm, nvbuf, nsem.at[1])
-    copies = [*q_copies, nk_copy, nv_copy]
+    copies = [nk_copy, nv_copy]
     for copy in [k_copy, v_copy, *copies]:
         copy.start()
 
@@ -104,9 +103,8 @@
     pack[to + dim : to + dim + EXTRA, :] = jnp.where((row == 0) & mine, 1.0, 0.0).astype(BF16)
 
 
-def fresh_mask(me, owner, spans, new, group, rows):
-    key = lax.broadcasted_iota(jnp.int32, (2 * new, rows), 0) + (me - lax.rem(me, 2)) * new
-    token = lax.div(lax.broadcasted_iota(jnp.int32, (1, rows), 1), group) + owner * new
+def fresh_mask(me, token, spans, new):
+    key = lax.broadcasted_iota(jnp.int32, (2 * new, token.shape[1]), 0) + (me - lax.rem(me, 2)) * new
     ok = key <= token
     for k in range(spans.shape[1]):
         lo, hi = spans[0, k], spans[1, k]
@@ -115,10 +113,12 @@
 
 
 def attend_kernel(where, away, cache_dev, new, group, scale2, spans, own, other, q_ref, out, s0, s1, fresh_k, fresh_v):
-    n, rows, dim = q_ref.shape
+    members, part, dim = q_ref.shape
+    pair = WIDE // part
+    n, rows = members // pair, WIDE
     me = where()
     core = lax.rem(me, 2)
-    quad = (me - lax.rem(me, 2 * n)) ^ (2 * n if away else 0)
+    quad = (me - lax.rem(me, 2 * members)) ^ (2 * members if away else 0)
     base = cache_dev + new
     tall = dim + EXTRA
     s_refs = (s0, s1)
@@ -132,14 +132,20 @@
 
     tiles = [(which, at) for which in (0, 1) for at in range(0, cache_dev, CHUNK)] + [None]
 
+    def block(b):
+        return q_ref[pair * b : pair * (b + 1)].reshape(rows, dim)
+
     def scores(b, tile, peak):
         if tile is None:
-            s = lax.dot_general(fresh_k[...], q_ref[b], NT, preferred_element_type=F32)
-            s = jnp.where(fresh_mask(me, quad + 2 * b + core, spans, new, group, rows), s, HIDDEN)
+            s = lax.dot_general(fresh_k[...], block(b), NT, preferred_element_type=F32)
+            lane = lax.broadcasted_iota(jnp.int32, (1, rows), 1)
+            owner = quad + (pair * b + lax.div(lane, part)) * 2 + core
+            token = owner * new + lax.div(lax.rem(lane, part), group)
+            s = jnp.where(fresh_mask(me, token, spans, new), s, HIDDEN)
             to, size = 2 * cache_dev, 2 * new
         else:
             which, at = tile
-            s = lax.dot_general((own, other)[which][at : at + CHUNK, :], q_ref[b], NT, preferred_element_type=F32)
+            s = lax.dot_general((own, other)[which][at : at + CHUNK, :], block(b), NT, preferred_element_type=F32)
             to, size = which * cache_dev + at, CHUNK
         s_refs[b % 2][to : to + size, :] = s
         top = jnp.max(s.reshape(size // 8, 8, rows), axis=0)
@@ -170,10 +176,18 @@
             acc = weigh(b, tile, top, acc)
             if b + 1 < n:
                 peak = scores(b + 1, tile, peak)
-        write_message(out.at[b], acc[0:dim], top * scale2, acc[dim : dim + 1])
-
-
-def merge_kernel(got, out):
+        for j in range(pair):
+            cut = slice(j * part, (j + 1) * part)
+            write_message(out.at[pair * b + j], acc[0:dim, cut], top[:, cut] * scale2, acc[dim : dim + 1, cut])
+
+
+def spread_kernel(q, q_far, _, near_out, far_out):
+    for j in range(near_out.shape[0]):
+        near_out[j] = q[...]
+        far_out[j] = q_far[...]
+
+
+def merge_kernel(got, _, out, kept):
     write_message(out, *merge([got.at[j] for j in range(got.shape[0])]))
 
 
@@ -202,32 +216,40 @@
     hbm = pl.BlockSpec(memory_space=pltpu.HBM)
     vmem = pl.BlockSpec(memory_space=pltpu.VMEM)
     smem = pl.BlockSpec(memory_space=pltpu.SMEM)
-    params = pltpu.CompilerParams(vmem_limit_bytes=32 * 1024 * 1024)
+    params = pltpu.CompilerParams(vmem_limit_bytes=40 * 1024 * 1024)
     message = jax.ShapeDtypeStruct((dim + EXTRA, rows), BF16)
     dma = pltpu.SemaphoreType.DMA
 
     q = queries.reshape(rows, dim)
     q_far = across(q, "far")
-    own, q_rep = pl.pallas_call(
+    own = pl.pallas_call(
         functools.partial(pack_kernel, far * near * cores, where),
-        out_shape=[jax.ShapeDtypeStruct((packed, dim), BF16), jax.ShapeDtypeStruct((near, rows, dim), BF16)],
-        in_specs=[hbm] * 5 + [smem] * 2,
-        out_specs=[vmem] * 2,
+        out_shape=jax.ShapeDtypeStruct((packed, dim), BF16),
+        in_specs=[hbm] * 4 + [smem] * 2,
+        out_specs=vmem,
         scratch_shapes=[
             pltpu.VMEM((cache_dev, dim), BF16),
             pltpu.VMEM((cache_dev, dim), BF16),
             pltpu.VMEM((new, dim), BF16),
-            dma((near,)),
             dma,
             dma,
             dma((2,)),
         ],
         compiler_params=params,
         name="pack",
-    )(cache_k, cache_v, new_keys.reshape(new, dim), new_values.reshape(new, dim), q, cache_len, doc_start)
-    q_near = quad(q_rep)
+    )(cache_k, cache_v, new_keys.reshape(new, dim), new_values.reshape(new, dim), cache_len, doc_start)
+    slots = jax.ShapeDtypeStruct((near, rows, dim), BF16)
+    q_near, q_far = pl.pallas_call(
+        spread_kernel,
+        out_shape=[slots] * 2,
+        in_specs=[vmem, vmem, pl.BlockSpec(memory_space=pl.ANY)],
+        out_specs=[vmem] * 2,
+        compiler_params=params,
+        name="spread",
+    )(q, q_far, own)
+    q_far = quad(q_far)
     other = across(own, "core")
-    q_far = quad(jnp.broadcast_to(q_far[None], (near, rows, dim)))
+    q_near = quad(q_near)
 
     spans = span_bounds.T
     cost = pl.CostEstimate(
@@ -242,21 +264,28 @@
             out_shape=jax.ShapeDtypeStruct((near,) + message.shape, BF16),
             in_specs=[smem] + [vmem] * 3,
             out_specs=vmem,
-            scratch_shapes=[pltpu.VMEM((2 * cache_dev + 2 * new, rows), F32)] * 2
+            scratch_shapes=[pltpu.VMEM((2 * cache_dev + 2 * new, WIDE), F32)] * 2
             + [pltpu.VMEM((2 * new, dim), BF16), pltpu.VMEM((dim + EXTRA, TILE), BF16)],
             compiler_params=params,
             cost_estimate=cost,
             name=name,
         )(spans, own, other, blocks)
 
-    near_out = attend(q_near, False, "near_blocks")
     far_out = attend(q_far, True, "far_blocks")
     far_got = quad(far_out)
+    near_out = attend(q_near, False, "near_blocks")
+    anywhere = pl.BlockSpec(memory_space=pl.ANY)
+    far_sum, near_out = pl.pallas_call(
+        merge_kernel,
+        out_shape=[message, jax.ShapeDtypeStruct(near_out.shape, BF16)],
+        in_specs=[vmem, anywhere],
+        out_specs=[vmem, anywhere],
+        input_output_aliases={1: 1},
+        compiler_params=params,
+        name="merge_far",
+    )(far_got, near_out)
+    back = across(far_sum, "far")
     near_got = quad(near_out)
-    far_sum = pl.pallas_call(
-        merge_kernel, out_shape=message, in_specs=[vmem], out_specs=vmem, compiler_params=params, name="merge_far"
-    )(far_got)
-    back = across(far_sum, "far")
     result = pl.pallas_call(
         final_kernel,
         out_shape=jax.ShapeDtypeStruct((rows, dim), BF16),

time: 78.2 us -> 73.3 us (0.937)
  the two profiles are of different devices: /device:TPU:74 before, /device:TPU:76 now
where the time goes in v2:
time: 73.3 us; the launch traced here: 72.7 us
  starting transfers between devices  40.2 us (55%)
  Pallas kernels  18.7 us (26%)
  waiting for transfers between devices  8.97 us (12%)
  local copies, waits for them, and re-layouts  4.11 us (6%)
    all_to_all x4, starting transfers between devices, quad(): return lax.all_to_all(x, 'near', split_axis=0, concat_axis=0, tiled=True)  22.2 us
    ppermute x3, starting transfers between devices, across(): return lax.ppermute(x, axis, [(0, 1), (1, 0)])  18 us
    pallas_call x2, Pallas kernels, attend(): pl.pallas_call(functools.partial(attend_kernel, where, away, cache_dev, n...  15.5 us
    ppermute x3, waiting for transfers between devices, across(): return lax.ppermute(x, axis, [(0, 1), (1, 0)])  5.35 us
    unnamed x14, local copies, waits for them, and re-layouts  4.11 us
    all_to_all x4, waiting for transfers between devices, quad(): return lax.all_to_all(x, 'near', split_axis=0, concat_axis=0, tiled=True)  3.62 us
  transfers between devices with their start and end apart: 7, of which 2 were waited for; matrix products, arithmetic and copies ran while one was open for 0% of the time, Pallas kernels for 23%

profile of v2, /device:TPU:76, one launch (start us, length us, event | category | flops | bytes accessed | tf_op | source)
XLA Modules:
  0.0 72.7 jit_solution(3329188838661581705)
XLA Ops:
  0.0 9.1 %collective-permute-start.1 = (bf16[256,128]{1,0:T(8,128)(2,1)}, bf16[256,128]{1,0:T(8,128)(2,1)S(1)}, u32[]{:S(2)}, u32[]{:S(2)}) collective-permute-start(bf16[256,128]{1,0:T(8,128)(2,1)} %bitcast.7), channel_id=1, source_target_pairs={{0,256},{256,0},{1,257},{257,1},{2,258},{258,2},{3,259},{259,3},{4... | collective-permute-start | bytes 196616 | tf_op jit(solution)/shard_map/ppermute | solution.py:211
  9.7 0.0 copy-start
  9.7 1.0 %copy-done = bf16[1,2048,128]{2,1,0:T(8,128)(2,1)S(1)} copy-done((bf16[1,2048,128]{2,1,0:T(8,128)(2,1)S(1)}, bf16[1,2048,128]{2,1,0:T(8,128)(2,1)}, u32[]{:S(2)}) %copy-start) | copy-done | bytes 524312
  10.8 0.0 copy-start.1
  10.8 1.0 %copy-done.1 = bf16[1,2048,128]{2,1,0:T(8,128)(2,1)S(1)} copy-done((bf16[1,2048,128]{2,1,0:T(8,128)(2,1)S(1)}, bf16[1,2048,128]{2,1,0:T(8,128)(2,1)}, u32[]{:S(2)}) %copy-start.1) | copy-done | bytes 524312
  11.8 0.0 copy-start.3
  11.8 0.7 copy-done.3
  12.5 0.0 copy-start.4
  12.5 0.7 copy-done.4
  13.2 0.0 copy-start.5
  13.2 0.7 copy-done.5
  13.9 0.0 copy-start.2
  13.9 1.4 %pack.1._.own = bf16[4512,128]{1,0:T(8,128)(2,1)S(1)} custom-call(bf16[1,2048,128]{2,1,0:T(8,128)(2,1)S(1)} %copy-done, bf16[1,2048,128]{2,1,0:T(8,128)(2,1)S(1)} %copy-done.1, bf16[16,128]{1,0:T(8,128)(2,1)S(1)} %bitcast.9, bf16[16,128]{1,0:T(8,128)(2,1)S(1)} %bitcast.10, s32[16]{0:T(128)S(1)} %copy-done.5, s32[1]{0:T(128)S(6)} %copy.12.refs_5_), custom_call_target="tpu_custom_call" | custom-call | tf_op jit(solution)/shard_map/pack/pallas_call | solution.py:225
  15.2 0.0 copy-start.6
  15.2 0.0 collective-permute-done.1.q_far
  15.3 0.0 copy-done.2
  15.3 0.9 %spread.1 = (bf16[4,256,128]{2,1,0:T(8,128)(2,1)}, bf16[4,256,128]{2,1,0:T(8,128)(2,1)}) custom-call(bf16[256,128]{1,0:T(8,128)(2,1)S(1)} %bitcast.8, bf16[256,128]{1,0:T(8,128)(2,1)S(1)} %collective-permute-done.1.q_far, bf16[4512,128]{1,0:T(8,128)(2,1)S(1)} %pack.1._.own), custom_call_target="tpu_custom_call" | custom-call | tf_op jit(solution)/shard_map/spread/pallas_call | solution.py:242
  16.1 5.5 %all-to-all-start = ((bf16[4,256,128]{2,1,0:T(8,128)(2,1)}), bf16[4,256,128]{2,1,0:T(8,128)(2,1)S(1)}, u32[]{:S(2)}, u32[]{:S(2)}) async-start(bf16[4,256,128]{2,1,0:T(8,128)(2,1)} %get-tuple-element.9), calls=%async_computation | async-start | bytes 524288 | tf_op jit(solution)/shard_map/all_to_all | solution.py:214
  21.7 1.9 %collective-permute-start = (bf16[4512,128]{1,0:T(8,128)(2,1)S(1)}, bf16[4512,128]{1,0:T(8,128)(2,1)S(1)}, u32[]{:S(2)}, u32[]{:S(2)}) collective-permute-start(bf16[4512,128]{1,0:T(8,128)(2,1)S(1)} %pack.1._.own), channel_id=1, source_target_pairs={{0,32},{32,0},{1,33},{33,1},{2,34},{34,2},{3,35},{35,3},{4,36},{36... | collective-permute-start | bytes 3465224 | tf_op jit(solution)/shard_map/ppermute | solution.py:211
  23.6 3.6 %all-to-all-done.q_ref = bf16[4,256,128]{2,1,0:T(8,128)(2,1)S(1)} async-done(((bf16[4,256,128]{2,1,0:T(8,128)(2,1)}), bf16[4,256,128]{2,1,0:T(8,128)(2,1)S(1)}, u32[]{:S(2)}, u32[]{:S(2)}) %all-to-all-start) | async-done | bytes 262176 | tf_op jit(solution)/shard_map/all_to_all | solution.py:214
  27.2 6.4 %all-to-all-start.2 = ((bf16[4,256,128]{2,1,0:T(8,128)(2,1)}), bf16[4,256,128]{2,1,0:T(8,128)(2,1)S(1)}, u32[]{:S(2)}, u32[]{:S(2)}) async-start(bf16[4,256,128]{2,1,0:T(8,128)(2,1)} %get-tuple-element.10), calls=%async_computation.2 | async-start | bytes 524288 | tf_op jit(solution)/shard_map/all_to_all | solution.py:214
  33.7 0.0 collective-permute-done.other
  33.7 0.0 copy-done.6
  33.7 7.8 %far_blocks.1 = bf16[4,144,256]{2,1,0:T(8,128)(2,1)} custom-call(s32[2,4]{1,0:T(2,128)S(1)} %bitcast.11, bf16[4512,128]{1,0:T(8,128)(2,1)S(1)} %pack.1._.own, bf16[4512,128]{1,0:T(8,128)(2,1)S(1)} %collective-permute-done.other, bf16[4,256,128]{2,1,0:T(8,128)(2,1)S(1)} %all-to-all-done.q_ref), custom_call_target="tpu_custom_call" | custom-call | flops 2147483648 | bytes 4194304 | tf_op jit(solution)/shard_map/far_blocks/pallas_call | solution.py:262
  41.4 0.0 all-to-all-done.2.q_ref
  41.4 5.1 %all-to-all-start.1 = ((bf16[4,144,256]{2,1,0:T(8,128)(2,1)}), bf16[4,144,256]{2,1,0:T(8,128)(2,1)S(1)}, u32[]{:S(2)}, u32[]{:S(2)}) async-start(bf16[4,144,256]{2,1,0:T(8,128)(2,1)} %far_blocks.1), calls=%async_computation.1 | async-start | bytes 589824 | tf_op jit(solution)/shard_map/all_to_all | solution.py:214
  46.5 7.8 %near_blocks.1._ = bf16[4,144,256]{2,1,0:T(8,128)(2,1)} custom-call(s32[2,4]{1,0:T(2,128)S(1)} %bitcast.12, bf16[4512,128]{1,0:T(8,128)(2,1)S(1)} %pack.1._.own, bf16[4512,128]{1,0:T(8,128)(2,1)S(1)} %collective-permute-done.other, bf16[4,256,128]{2,1,0:T(8,128)(2,1)S(1)} %all-to-all-done.2.q_ref), custom_call_target="tpu_custom_call" | custom-call | flops 2147483648 | bytes 4194304 | tf_op jit(solution)/shard_map/near_blocks/pallas_call | solution.py:262
  54.3 0.0 all-to-all-done.1.got
  54.3 0.1 merge_far.1
  54.4 5.1 %all-to-all-start.3 = ((bf16[4,144,256]{2,1,0:T(8,128)(2,1)}), bf16[4,144,256]{2,1,0:T(8,128)(2,1)S(1)}, u32[]{:S(2)}, u32[]{:S(2)}) async-start(bf16[4,144,256]{2,1,0:T(8,128)(2,1)} %get-tuple-element.11), calls=%async_computation.3 | async-start | bytes 589824 | tf_op jit(solution)/shard_map/all_to_all | solution.py:214
  59.5 7.0 %collective-permute-start.2 = (bf16[144,256]{1,0:T(8,128)(2,1)S(1)}, bf16[144,256]{1,0:T(8,128)(2,1)S(1)}, u32[]{:S(2)}, u32[]{:S(2)}) collective-permute-start(bf16[144,256]{1,0:T(8,128)(2,1)S(1)} %get-tuple-element.12), channel_id=1, source_target_pairs={{0,256},{256,0},{1,257},{257,1},{2,258},{258,2},{3,259},{259,3},{4... | collective-permute-start | bytes 221192 | tf_op jit(solution)/shard_map/ppermute | solution.py:211
  66.5 5.3 %collective-permute-done.2.back = bf16[144,256]{1,0:T(8,128)(2,1)S(1)} collective-permute-done((bf16[144,256]{1,0:T(8,128)(2,1)S(1)}, bf16[144,256]{1,0:T(8,128)(2,1)S(1)}, u32[]{:S(2)}, u32[]{:S(2)}) %collective-permute-start.2) | collective-permute-done | bytes 73760 | tf_op jit(solution)/shard_map/ppermute | solution.py:211
  71.9 0.0 all-to-all-done.3.got
  71.9 0.8 %merge_all.1 = bf16[256,128]{1,0:T(8,128)(2,1)} custom-call(bf16[4,144,256]{2,1,0:T(8,128)(2,1)S(1)} %all-to-all-done.3.got, bf16[144,256]{1,0:T(8,128)(2,1)S(1)} %collective-permute-done.2.back), custom_call_target="tpu_custom_call" | custom-call | tf_op jit(solution)/shard_map/merge_all/pallas_call | solution.py:289
Async XLA Ops:
  0.0 15.3 %collective-permute-start.1 = (bf16[256,128]{1,0:T(8,128)(2,1)}, bf16[256,128]{1,0:T(8,128)(2,1)S(1)}, u32[]{:S(2)}, u32[]{:S(2)}) collective-permute-start(bf16[256,128]{1,0:T(8,128)(2,1)} %bitcast.7), channel_id=1, source_target_pairs={{0,256},{256,0},{1,257},{257,1},{2,258},{258,2},{3,259},{259,3},{4... | collective-permute-start | bytes 196616 | tf_op jit(solution)/shard_map/ppermute | solution.py:211
  9.7 1.0 %copy-start = (bf16[1,2048,128]{2,1,0:T(8,128)(2,1)S(1)}, bf16[1,2048,128]{2,1,0:T(8,128)(2,1)}, u32[]{:S(2)}) copy-start(bf16[1,2048,128]{2,1,0:T(8,128)(2,1)} %refs_0_.1) | copy-start | bytes 1572868
  10.8 1.0 %copy-start.1 = (bf16[1,2048,128]{2,1,0:T(8,128)(2,1)S(1)}, bf16[1,2048,128]{2,1,0:T(8,128)(2,1)}, u32[]{:S(2)}) copy-start(bf16[1,2048,128]{2,1,0:T(8,128)(2,1)} %refs_1_.1) | copy-start | bytes 1572868
  11.8 0.7 copy-start.3
  12.5 0.7 copy-start.4
  13.2 0.7 copy-start.5
  13.9 1.4 %copy-start.2 = (bf16[16,1,16,128]{3,2,1,0:T(8,128)(2,1)S(1)}, bf16[16,1,16,128]{3,2,1,0:T(8,128)(2,1)}, u32[]{:S(2)}) copy-start(bf16[16,1,16,128]{3,2,1,0:T(8,128)(2,1)} %param.8) | copy-start | bytes 196612
  15.2 18.4 %copy-start.6 = (s32[4,2]{0,1:T(2,128)S(1)}, s32[4,2]{0,1:T(2,128)}, u32[]{:S(2)}) copy-start(s32[4,2]{0,1:T(2,128)} %param.13) | copy-start | bytes 100
  16.1 11.1 %all-to-all-start = ((bf16[4,256,128]{2,1,0:T(8,128)(2,1)}), bf16[4,256,128]{2,1,0:T(8,128)(2,1)S(1)}, u32[]{:S(2)}, u32[]{:S(2)}) async-start(bf16[4,256,128]{2,1,0:T(8,128)(2,1)} %get-tuple-element.9), calls=%async_computation | async-start | bytes 524288 | tf_op jit(solution)/shard_map/all_to_all | solution.py:214
  21.7 12.0 %collective-permute-start = (bf16[4512,128]{1,0:T(8,128)(2,1)S(1)}, bf16[4512,128]{1,0:T(8,128)(2,1)S(1)}, u32[]{:S(2)}, u32[]{:S(2)}) collective-permute-start(bf16[4512,128]{1,0:T(8,128)(2,1)S(1)} %pack.1._.own), channel_id=1, source_target_pairs={{0,32},{32,0},{1,33},{33,1},{2,34},{34,2},{3,35},{35,3},{4,36},{36... | collective-permute-start | bytes 3465224 | tf_op jit(solution)/shard_map/ppermute | solution.py:211
  27.2 14.2 %all-to-all-start.2 = ((bf16[4,256,128]{2,1,0:T(8,128)(2,1)}), bf16[4,256,128]{2,1,0:T(8,128)(2,1)S(1)}, u32[]{:S(2)}, u32[]{:S(2)}) async-start(bf16[4,256,128]{2,1,0:T(8,128)(2,1)} %get-tuple-element.10), calls=%async_computation.2 | async-start | bytes 524288 | tf_op jit(solution)/shard_map/all_to_all | solution.py:214
  41.4 12.9 %all-to-all-start.1 = ((bf16[4,144,256]{2,1,0:T(8,128)(2,1)}), bf16[4,144,256]{2,1,0:T(8,128)(2,1)S(1)}, u32[]{:S(2)}, u32[]{:S(2)}) async-start(bf16[4,144,256]{2,1,0:T(8,128)(2,1)} %far_blocks.1), calls=%async_computation.1 | async-start | bytes 589824 | tf_op jit(solution)/shard_map/all_to_all | solution.py:214
  54.4 17.5 %all-to-all-start.3 = ((bf16[4,144,256]{2,1,0:T(8,128)(2,1)}), bf16[4,144,256]{2,1,0:T(8,128)(2,1)S(1)}, u32[]{:S(2)}, u32[]{:S(2)}) async-start(bf16[4,144,256]{2,1,0:T(8,128)(2,1)} %get-tuple-element.11), calls=%async_computation.3 | async-start | bytes 589824 | tf_op jit(solution)/shard_map/all_to_all | solution.py:214
  59.5 12.4 %collective-permute-start.2 = (bf16[144,256]{1,0:T(8,128)(2,1)S(1)}, bf16[144,256]{1,0:T(8,128)(2,1)S(1)}, u32[]{:S(2)}, u32[]{:S(2)}) collective-permute-start(bf16[144,256]{1,0:T(8,128)(2,1)S(1)} %get-tuple-element.12), channel_id=1, source_target_pairs={{0,256},{256,0},{1,257},{257,1},{2,258},{258,2},{3,259},{259,3},{4... | collective-permute-start | bytes 221192 | tf_op jit(solution)/shard_map/ppermute | solution.py:211

commit v3 on v2

--- a/solution.py
+++ b/solution.py
@@ -12,7 +12,7 @@
 F32 = jnp.float32
 BF16 = jnp.bfloat16
 HIDDEN = -1e30
-CHUNK = 512
+CHUNK = 256
 TILE = 128
 WIDE = 512
 EXTRA = 16
@@ -112,7 +112,7 @@
     return ok
 
 
-def attend_kernel(where, away, cache_dev, new, group, scale2, spans, own, other, q_ref, out, s0, s1, fresh_k, fresh_v):
+def attend_kernel(where, away, cache_dev, new, group, scale2, spans, own, other, q_ref, out, s0, s1, acc, fresh_k, fresh_v):
     members, part, dim = q_ref.shape
     pair = WIDE // part
     n, rows = members // pair, WIDE
@@ -122,6 +122,7 @@
     base = cache_dev + new
     tall = dim + EXTRA
     s_refs = (s0, s1)
+    halves = (own, other)
 
     odd = core == 1
     mine, theirs = own[cache_dev:base, :].astype(F32), other[cache_dev:base, :].astype(F32)
@@ -130,52 +131,63 @@
     at = base + cache_dev // TILE * tall
     fresh_v[...] = (own[at : at + tall, :].astype(F32) + other[at : at + tall, :].astype(F32)).astype(BF16)
 
-    tiles = [(which, at) for which in (0, 1) for at in range(0, cache_dev, CHUNK)] + [None]
-
     def block(b):
         return q_ref[pair * b : pair * (b + 1)].reshape(rows, dim)
 
-    def scores(b, tile, peak):
-        if tile is None:
-            s = lax.dot_general(fresh_k[...], block(b), NT, preferred_element_type=F32)
-            lane = lax.broadcasted_iota(jnp.int32, (1, rows), 1)
-            owner = quad + (pair * b + lax.div(lane, part)) * 2 + core
-            token = owner * new + lax.div(lax.rem(lane, part), group)
-            s = jnp.where(fresh_mask(me, token, spans, new), s, HIDDEN)
-            to, size = 2 * cache_dev, 2 * new
-        else:
-            which, at = tile
-            s = lax.dot_general((own, other)[which][at : at + CHUNK, :], block(b), NT, preferred_element_type=F32)
-            to, size = which * cache_dev + at, CHUNK
-        s_refs[b % 2][to : to + size, :] = s
-        top = jnp.max(s.reshape(size // 8, 8, rows), axis=0)
-        return top if peak is None else jnp.maximum(peak, top)
-
-    def weigh(b, tile, peak, acc):
-        if tile is None:
-            s = s_refs[b % 2][2 * cache_dev : 2 * cache_dev + 2 * new, :]
-            p = jnp.exp2((s - peak) * scale2)
-            p = jnp.concatenate([p, jnp.zeros((TILE - 2 * new, rows), F32)], axis=0).astype(BF16)
-            v = fresh_v[...]
-        else:
-            which, at = tile
-            to = which * cache_dev + at
-            p = jnp.exp2((s_refs[b % 2][to : to + CHUNK, :] - peak) * scale2).astype(BF16)
-            starts = [base + (at // TILE + j) * tall for j in range(CHUNK // TILE)]
-            v = jnp.concatenate([(own, other)[which][i : i + tall, :] for i in starts], axis=1)
-        o = jnp.dot(v, p, preferred_element_type=F32)
-        return o if acc is None else acc + o
-
-    peak = None
-    for tile in tiles:
-        peak = scores(0, tile, peak)
+    def top_of(s):
+        return jnp.max(s.reshape(s.shape[0] // 8, 8, rows), axis=0)
+
+    def fresh_scores(b):
+        s = lax.dot_general(fresh_k[...], block(b), NT, preferred_element_type=F32)
+        lane = lax.broadcasted_iota(jnp.int32, (1, rows), 1)
+        owner = quad + (pair * b + lax.div(lane, part)) * 2 + core
+        token = owner * new + lax.div(lax.rem(lane, part), group)
+        s = jnp.where(fresh_mask(me, token, spans, new), s, HIDDEN)
+        s_refs[b % 2][2 * cache_dev : 2 * cache_dev + 2 * new, :] = s
+        return top_of(s)
+
+    def scores(b, i, peak):
+        for which, ref in enumerate(halves):
+            keys = ref[pl.ds(pl.multiple_of(i * CHUNK, CHUNK), CHUNK), :]
+            s = lax.dot_general(keys, block(b), NT, preferred_element_type=F32)
+            s_refs[b % 2][pl.ds(pl.multiple_of(which * cache_dev + i * CHUNK, CHUNK), CHUNK), :] = s
+            peak = jnp.maximum(peak, top_of(s))
+        return peak
+
+    def fresh_weigh(b, peak):
+        s = s_refs[b % 2][2 * cache_dev : 2 * cache_dev + 2 * new, :]
+        p = jnp.exp2((s - peak) * scale2)
+        p = jnp.concatenate([p, jnp.zeros((TILE - 2 * new, rows), F32)], axis=0).astype(BF16)
+        acc[...] = jnp.dot(fresh_v[...], p, preferred_element_type=F32)
+
+    def weigh(b, i, peak):
+        ps, vs = [], []
+        for which, ref in enumerate(halves):
+            s = s_refs[b % 2][pl.ds(pl.multiple_of(which * cache_dev + i * CHUNK, CHUNK), CHUNK), :]
+            ps.append(jnp.exp2((s - peak) * scale2).astype(BF16))
+            for j in range(CHUNK // TILE):
+                vs.append(ref[pl.ds(pl.multiple_of(base + (i * (CHUNK // TILE) + j) * tall, 16), tall), :])
+        acc[...] += jnp.dot(jnp.concatenate(vs, axis=1), jnp.concatenate(ps, axis=0), preferred_element_type=F32)
+
+    steps = cache_dev // CHUNK
+    peak = lax.fori_loop(0, steps, lambda i, peak: scores(0, i, peak), fresh_scores(0))
     for b in range(n):
         top = jnp.max(peak, axis=0, keepdims=True)
-        acc, peak = None, None
-        for tile in tiles:
-            acc = weigh(b, tile, top, acc)
-            if b + 1 < n:
-                peak = scores(b + 1, tile, peak)
+        fresh_weigh(b, top)
+        if b + 1 < n:
+
+            def both(i, peak, b=b, top=top):
+                weigh(b, i, top)
+                return scores(b + 1, i, peak)
+
+            peak = lax.fori_loop(0, steps, both, fresh_scores(b + 1))
+        else:
+
+            def last(i, carry, b=b, top=top):
+                weigh(b, i, top)
+                return carry
+
+            lax.fori_loop(0, steps, last, 0)
         for j in range(pair):
             cut = slice(j * part, (j + 1) * part)
             write_message(out.at[pair * b + j], acc[0:dim, cut], top[:, cut] * scale2, acc[dim : dim + 1, cut])
@@ -265,7 +277,7 @@
             in_specs=[smem] + [vmem] * 3,
             out_specs=vmem,
             scratch_shapes=[pltpu.VMEM((2 * cache_dev + 2 * new, WIDE), F32)] * 2
-            + [pltpu.VMEM((2 * new, dim), BF16), pltpu.VMEM((dim + EXTRA, TILE), BF16)],
+            + [pltpu.VMEM((dim + EXTRA, WIDE), F32), pltpu.VMEM((2 * new, dim), BF16), pltpu.VMEM((dim + EXTRA, TILE), BF16)],
             compiler_params=params,
             cost_estimate=cost,
             name=name,

time: 73.3 us -> 79.5 us (1.085)
  Pallas kernels: 18.7 us -> 24.9 us
    pallas_call x2, Pallas kernels: 15.5 us -> 21.7 us  [attend(): pl.pallas_call(functools.partial(attend_kernel, where, away, cache_dev, n...]
  transfers between devices with their start and end apart: 7 -> 7, of which waited for: 2 -> 2; matrix products, arithmetic and copies ran while one was open for 0% -> 0% of each run, Pallas kernels for 23% -> 29%
where the time goes in v3:
time: 79.5 us; the launch traced here: 78.8 us
  starting transfers between devices  40.2 us (51%)
  Pallas kernels  24.9 us (31%)
  waiting for transfers between devices  8.97 us (11%)
  local copies, waits for them, and re-layouts  4.11 us (5%)
    all_to_all x4, starting transfers between devices, quad(): return lax.all_to_all(x, 'near', split_axis=0, concat_axis=0, tiled=True)  22.2 us
    pallas_call x2, Pallas kernels, attend(): pl.pallas_call(functools.partial(attend_kernel, where, away, cache_dev, n...  21.7 us
    ppermute x3, starting transfers between devices, across(): return lax.ppermute(x, axis, [(0, 1), (1, 0)])  18 us
    ppermute x3, waiting for transfers between devices, across(): return lax.ppermute(x, axis, [(0, 1), (1, 0)])  5.35 us
    unnamed x14, local copies, waits for them, and re-layouts  4.11 us
    all_to_all x4, waiting for transfers between devices, quad(): return lax.all_to_all(x, 'near', split_axis=0, concat_axis=0, tiled=True)  3.62 us
  transfers between devices with their start and end apart: 7, of which 2 were waited for; matrix products, arithmetic and copies ran while one was open for 0% of the time, Pallas kernels for 29%

profile of v3, /device:TPU:76, one launch (start us, length us, event | category | flops | bytes accessed | tf_op | source)
XLA Modules:
  0.0 78.8 jit_solution(6939220160562190992)
XLA Ops:
  0.0 9.1 %collective-permute-start.1 = (bf16[256,128]{1,0:T(8,128)(2,1)}, bf16[256,128]{1,0:T(8,128)(2,1)S(1)}, u32[]{:S(2)}, u32[]{:S(2)}) collective-permute-start(bf16[256,128]{1,0:T(8,128)(2,1)} %bitcast.7), channel_id=1, source_target_pairs={{0,256},{256,0},{1,257},{257,1},{2,258},{258,2},{3,259},{259,3},{4... | collective-permute-start | bytes 196616 | tf_op jit(solution)/shard_map/ppermute | solution.py:223
  9.7 0.0 copy-start
  9.7 1.0 %copy-done = bf16[1,2048,128]{2,1,0:T(8,128)(2,1)S(1)} copy-done((bf16[1,2048,128]{2,1,0:T(8,128)(2,1)S(1)}, bf16[1,2048,128]{2,1,0:T(8,128)(2,1)}, u32[]{:S(2)}) %copy-start) | copy-done | bytes 524312
  10.8 0.0 copy-start.1
  10.8 1.0 %copy-done.1 = bf16[1,2048,128]{2,1,0:T(8,128)(2,1)S(1)} copy-done((bf16[1,2048,128]{2,1,0:T(8,128)(2,1)S(1)}, bf16[1,2048,128]{2,1,0:T(8,128)(2,1)}, u32[]{:S(2)}) %copy-start.1) | copy-done | bytes 524312
  11.8 0.0 copy-start.3
  11.8 0.7 copy-done.3
  12.5 0.0 copy-start.4
  12.5 0.7 copy-done.4
  13.2 0.0 copy-start.5
  13.2 0.7 copy-done.5
  13.9 0.0 copy-start.2
  13.9 1.4 %pack.1._.own = bf16[4512,128]{1,0:T(8,128)(2,1)S(1)} custom-call(bf16[1,2048,128]{2,1,0:T(8,128)(2,1)S(1)} %copy-done, bf16[1,2048,128]{2,1,0:T(8,128)(2,1)S(1)} %copy-done.1, bf16[16,128]{1,0:T(8,128)(2,1)S(1)} %bitcast.9, bf16[16,128]{1,0:T(8,128)(2,1)S(1)} %bitcast.10, s32[16]{0:T(128)S(1)} %copy-done.5, s32[1]{0:T(128)S(6)} %copy.12.refs_5_), custom_call_target="tpu_custom_call" | custom-call | tf_op jit(solution)/shard_map/pack/pallas_call | solution.py:237
  15.2 0.0 copy-start.6
  15.2 0.0 collective-permute-done.1.q_far
  15.3 0.0 copy-done.2
  15.3 0.9 %spread.1 = (bf16[4,256,128]{2,1,0:T(8,128)(2,1)}, bf16[4,256,128]{2,1,0:T(8,128)(2,1)}) custom-call(bf16[256,128]{1,0:T(8,128)(2,1)S(1)} %bitcast.8, bf16[256,128]{1,0:T(8,128)(2,1)S(1)} %collective-permute-done.1.q_far, bf16[4512,128]{1,0:T(8,128)(2,1)S(1)} %pack.1._.own), custom_call_target="tpu_custom_call" | custom-call | tf_op jit(solution)/shard_map/spread/pallas_call | solution.py:254
  16.1 5.5 %all-to-all-start = ((bf16[4,256,128]{2,1,0:T(8,128)(2,1)}), bf16[4,256,128]{2,1,0:T(8,128)(2,1)S(1)}, u32[]{:S(2)}, u32[]{:S(2)}) async-start(bf16[4,256,128]{2,1,0:T(8,128)(2,1)} %get-tuple-element.9), calls=%async_computation | async-start | bytes 524288 | tf_op jit(solution)/shard_map/all_to_all | solution.py:226
  21.7 1.9 %collective-permute-start = (bf16[4512,128]{1,0:T(8,128)(2,1)S(1)}, bf16[4512,128]{1,0:T(8,128)(2,1)S(1)}, u32[]{:S(2)}, u32[]{:S(2)}) collective-permute-start(bf16[4512,128]{1,0:T(8,128)(2,1)S(1)} %pack.1._.own), channel_id=1, source_target_pairs={{0,32},{32,0},{1,33},{33,1},{2,34},{34,2},{3,35},{35,3},{4,36},{36... | collective-permute-start | bytes 3465224 | tf_op jit(solution)/shard_map/ppermute | solution.py:223
  23.6 3.6 %all-to-all-done.q_ref = bf16[4,256,128]{2,1,0:T(8,128)(2,1)S(1)} async-done(((bf16[4,256,128]{2,1,0:T(8,128)(2,1)}), bf16[4,256,128]{2,1,0:T(8,128)(2,1)S(1)}, u32[]{:S(2)}, u32[]{:S(2)}) %all-to-all-start) | async-done | bytes 262176 | tf_op jit(solution)/shard_map/all_to_all | solution.py:226
  27.2 6.4 %all-to-all-start.2 = ((bf16[4,256,128]{2,1,0:T(8,128)(2,1)}), bf16[4,256,128]{2,1,0:T(8,128)(2,1)S(1)}, u32[]{:S(2)}, u32[]{:S(2)}) async-start(bf16[4,256,128]{2,1,0:T(8,128)(2,1)} %get-tuple-element.10), calls=%async_computation.2 | async-start | bytes 524288 | tf_op jit(solution)/shard_map/all_to_all | solution.py:226
  33.7 0.0 collective-permute-done.other
  33.7 0.0 copy-done.6
  33.7 10.9 %far_blocks.1 = bf16[4,144,256]{2,1,0:T(8,128)(2,1)} custom-call(s32[2,4]{1,0:T(2,128)S(1)} %bitcast.11, bf16[4512,128]{1,0:T(8,128)(2,1)S(1)} %pack.1._.own, bf16[4512,128]{1,0:T(8,128)(2,1)S(1)} %collective-permute-done.other, bf16[4,256,128]{2,1,0:T(8,128)(2,1)S(1)} %all-to-all-done.q_ref), custom_call_target="tpu_custom_call" | custom-call | flops 2147483648 | bytes 4194304 | tf_op jit(solution)/shard_map/far_blocks/pallas_call | solution.py:274
  44.5 0.0 all-to-all-done.2.q_ref
  44.5 5.1 %all-to-all-start.1 = ((bf16[4,144,256]{2,1,0:T(8,128)(2,1)}), bf16[4,144,256]{2,1,0:T(8,128)(2,1)S(1)}, u32[]{:S(2)}, u32[]{:S(2)}) async-start(bf16[4,144,256]{2,1,0:T(8,128)(2,1)} %far_blocks.1), calls=%async_computation.1 | async-start | bytes 589824 | tf_op jit(solution)/shard_map/all_to_all | solution.py:226
  49.6 10.9 %near_blocks.1._ = bf16[4,144,256]{2,1,0:T(8,128)(2,1)} custom-call(s32[2,4]{1,0:T(2,128)S(1)} %bitcast.12, bf16[4512,128]{1,0:T(8,128)(2,1)S(1)} %pack.1._.own, bf16[4512,128]{1,0:T(8,128)(2,1)S(1)} %collective-permute-done.other, bf16[4,256,128]{2,1,0:T(8,128)(2,1)S(1)} %all-to-all-done.2.q_ref), custom_call_target="tpu_custom_call" | custom-call | flops 2147483648 | bytes 4194304 | tf_op jit(solution)/shard_map/near_blocks/pallas_call | solution.py:274
  60.5 0.0 all-to-all-done.1.got
  60.5 0.1 merge_far.1
  60.6 5.1 %all-to-all-start.3 = ((bf16[4,144,256]{2,1,0:T(8,128)(2,1)}), bf16[4,144,256]{2,1,0:T(8,128)(2,1)S(1)}, u32[]{:S(2)}, u32[]{:S(2)}) async-start(bf16[4,144,256]{2,1,0:T(8,128)(2,1)} %get-tuple-element.11), calls=%async_computation.3 | async-start | bytes 589824 | tf_op jit(solution)/shard_map/all_to_all | solution.py:226
  65.7 7.0 %collective-permute-start.2 = (bf16[144,256]{1,0:T(8,128)(2,1)S(1)}, bf16[144,256]{1,0:T(8,128)(2,1)S(1)}, u32[]{:S(2)}, u32[]{:S(2)}) collective-permute-start(bf16[144,256]{1,0:T(8,128)(2,1)S(1)} %get-tuple-element.12), channel_id=1, source_target_pairs={{0,256},{256,0},{1,257},{257,1},{2,258},{258,2},{3,259},{259,3},{4... | collective-permute-start | bytes 221192 | tf_op jit(solution)/shard_map/ppermute | solution.py:223
  72.7 5.3 %collective-permute-done.2.back = bf16[144,256]{1,0:T(8,128)(2,1)S(1)} collective-permute-done((bf16[144,256]{1,0:T(8,128)(2,1)S(1)}, bf16[144,256]{1,0:T(8,128)(2,1)S(1)}, u32[]{:S(2)}, u32[]{:S(2)}) %collective-permute-start.2) | collective-permute-done | bytes 73760 | tf_op jit(solution)/shard_map/ppermute | solution.py:223
  78.1 0.0 all-to-all-done.3.got
  78.1 0.8 %merge_all.1 = bf16[256,128]{1,0:T(8,128)(2,1)} custom-call(bf16[4,144,256]{2,1,0:T(8,128)(2,1)S(1)} %all-to-all-done.3.got, bf16[144,256]{1,0:T(8,128)(2,1)S(1)} %collective-permute-done.2.back), custom_call_target="tpu_custom_call" | custom-call | tf_op jit(solution)/shard_map/merge_all/pallas_call | solution.py:301
Async XLA Ops:
  0.0 15.3 %collective-permute-start.1 = (bf16[256,128]{1,0:T(8,128)(2,1)}, bf16[256,128]{1,0:T(8,128)(2,1)S(1)}, u32[]{:S(2)}, u32[]{:S(2)}) collective-permute-start(bf16[256,128]{1,0:T(8,128)(2,1)} %bitcast.7), channel_id=1, source_target_pairs={{0,256},{256,0},{1,257},{257,1},{2,258},{258,2},{3,259},{259,3},{4... | collective-permute-start | bytes 196616 | tf_op jit(solution)/shard_map/ppermute | solution.py:223
  9.7 1.0 %copy-start = (bf16[1,2048,128]{2,1,0:T(8,128)(2,1)S(1)}, bf16[1,2048,128]{2,1,0:T(8,128)(2,1)}, u32[]{:S(2)}) copy-start(bf16[1,2048,128]{2,1,0:T(8,128)(2,1)} %refs_0_.1) | copy-start | bytes 1572868
  10.8 1.0 %copy-start.1 = (bf16[1,2048,128]{2,1,0:T(8,128)(2,1)S(1)}, bf16[1,2048,128]{2,1,0:T(8,128)(2,1)}, u32[]{:S(2)}) copy-start(bf16[1,2048,128]{2,1,0:T(8,128)(2,1)} %refs_1_.1) | copy-start | bytes 1572868
  11.8 0.7 copy-start.3
  12.5 0.7 copy-start.4
  13.2 0.7 copy-start.5
  13.9 1.4 %copy-start.2 = (bf16[16,1,16,128]{3,2,1,0:T(8,128)(2,1)S(1)}, bf16[16,1,16,128]{3,2,1,0:T(8,128)(2,1)}, u32[]{:S(2)}) copy-start(bf16[16,1,16,128]{3,2,1,0:T(8,128)(2,1)} %param.8) | copy-start | bytes 196612
  15.2 18.4 %copy-start.6 = (s32[4,2]{0,1:T(2,128)S(1)}, s32[4,2]{0,1:T(2,128)}, u32[]{:S(2)}) copy-start(s32[4,2]{0,1:T(2,128)} %param.13) | copy-start | bytes 100
  16.1 11.1 %all-to-all-start = ((bf16[4,256,128]{2,1,0:T(8,128)(2,1)}), bf16[4,256,128]{2,1,0:T(8,128)(2,1)S(1)}, u32[]{:S(2)}, u32[]{:S(2)}) async-start(bf16[4,256,128]{2,1,0:T(8,128)(2,1)} %get-tuple-element.9), calls=%async_computation | async-start | bytes 524288 | tf_op jit(solution)/shard_map/all_to_all | solution.py:226
  21.7 12.0 %collective-permute-start = (bf16[4512,128]{1,0:T(8,128)(2,1)S(1)}, bf16[4512,128]{1,0:T(8,128)(2,1)S(1)}, u32[]{:S(2)}, u32[]{:S(2)}) collective-permute-start(bf16[4512,128]{1,0:T(8,128)(2,1)S(1)} %pack.1._.own), channel_id=1, source_target_pairs={{0,32},{32,0},{1,33},{33,1},{2,34},{34,2},{3,35},{35,3},{4,36},{36... | collective-permute-start | bytes 3465224 | tf_op jit(solution)/shard_map/ppermute | solution.py:223
  27.2 17.3 %all-to-all-start.2 = ((bf16[4,256,128]{2,1,0:T(8,128)(2,1)}), bf16[4,256,128]{2,1,0:T(8,128)(2,1)S(1)}, u32[]{:S(2)}, u32[]{:S(2)}) async-start(bf16[4,256,128]{2,1,0:T(8,128)(2,1)} %get-tuple-element.10), calls=%async_computation.2 | async-start | bytes 524288 | tf_op jit(solution)/shard_map/all_to_all | solution.py:226
  44.5 16.0 %all-to-all-start.1 = ((bf16[4,144,256]{2,1,0:T(8,128)(2,1)}), bf16[4,144,256]{2,1,0:T(8,128)(2,1)S(1)}, u32[]{:S(2)}, u32[]{:S(2)}) async-start(bf16[4,144,256]{2,1,0:T(8,128)(2,1)} %far_blocks.1), calls=%async_computation.1 | async-start | bytes 589824 | tf_op jit(solution)/shard_map/all_to_all | solution.py:226
  60.6 17.5 %all-to-all-start.3 = ((bf16[4,144,256]{2,1,0:T(8,128)(2,1)}), bf16[4,144,256]{2,1,0:T(8,128)(2,1)S(1)}, u32[]{:S(2)}, u32[]{:S(2)}) async-start(bf16[4,144,256]{2,1,0:T(8,128)(2,1)} %get-tuple-element.11), calls=%async_computation.3 | async-start | bytes 589824 | tf_op jit(solution)/shard_map/all_to_all | solution.py:226
  65.7 12.4 %collective-permute-start.2 = (bf16[144,256]{1,0:T(8,128)(2,1)S(1)}, bf16[144,256]{1,0:T(8,128)(2,1)S(1)}, u32[]{:S(2)}, u32[]{:S(2)}) collective-permute-start(bf16[144,256]{1,0:T(8,128)(2,1)S(1)} %get-tuple-element.12), channel_id=1, source_target_pairs={{0,256},{256,0},{1,257},{257,1},{2,258},{258,2},{3,259},{259,3},{4... | collective-permute-start | bytes 221192 | tf_op jit(solution)/shard_map/ppermute | solution.py:223

commit v4 on v2

v4 whole, which is shorter than its diff:
```python
import functools
import math

import jax
import jax.numpy as jnp
from jax import lax
from jax.experimental import pallas as pl
from jax.experimental.pallas import tpu as pltpu
from jax.sharding import Mesh
from jax.sharding import PartitionSpec as P

F32 = jnp.float32
BF16 = jnp.bfloat16
HIDDEN = -1e30
CHUNK = 1024
TILE = 128
WIDE = 512
EXTRA = 16
NT = (((1,), (1,)), ((), ()))


def pieces(x):
    hi = x.astype(BF16).astype(F32)
    mid = (x - hi).astype(BF16).astype(F32)
    return hi, mid, x - hi - mid


def write_message(out, numer, peak, total):
    dim = numer.shape[0]
    out[0:dim, :] = numer.astype(BF16)
    row = lax.broadcasted_iota(jnp.int32, (EXTRA, numer.shape[1]), 0)
    tail = jnp.zeros((EXTRA, numer.shape[1]), F32)
    for at, piece in enumerate(pieces(peak) + pieces(total)):
        tail = jnp.where(row == at, piece, tail)
    out[dim : dim + EXTRA, :] = tail.astype(BF16)


def read_message(ref):
    dim = ref.shape[0] - EXTRA
    tail = ref[dim : dim + EXTRA, :].astype(F32)
    peak = tail[0:1] + tail[1:2] + tail[2:3]
    total = tail[3:4] + tail[4:5] + tail[5:6]
    return ref[0:dim, :].astype(F32), peak, total


def merge(refs):
    parts = [read_message(ref) for ref in refs]
    peak = functools.reduce(jnp.maximum, [p[1] for p in parts])
    factors = [jnp.exp(p[1] - peak) for p in parts]
    total = sum(p[2] * f for p, f in zip(parts, factors))
    numer = sum(p[0] * f for p, f in zip(parts, factors))
    return numer, peak, total


def pack_kernel(count, where, *refs):
    k_hbm, v_hbm, nk_hbm, nv_hbm, cache_len, doc_start, pack = refs[:7]
    kbuf, vbuf, ksem, vsem, nsem = refs[7:]
    rows, dim = kbuf.shape
    new = nk_hbm.shape[0]
    base = rows + new
    me = where()
    first = lax.div(jnp.maximum(doc_start[0] - me + count - 1, 0), count)
    limit = cache_len[me]

    k_copy = pltpu.make_async_copy(k_hbm.at[0], kbuf, ksem)
    v_copy = pltpu.make_async_copy(v_hbm.at[0], vbuf, vsem)
    nk_copy = pltpu.make_async_copy(nk_hbm, pack.at[pl.ds(rows, new)], nsem.at[0])
    nv_copy = pltpu.make_async_copy(nv_hbm, pack.at[pl.ds(base + rows, new)], nsem.at[1])
    for copy in (k_copy, v_copy, nk_copy, nv_copy):
        copy.start()

    safe = rows // 8
    step = 512
    k_copy.wait()
    spare = kbuf[safe : safe + 16, :][0:1].astype(F32)
    for at in range(0, rows, step):
        slot = lax.broadcasted_iota(jnp.int32, (step, dim), 0) + at
        ok = (slot >= first) & (slot < limit)
        pack[at : at + step, :] = jnp.where(ok, kbuf[at : at + step, :].astype(F32), spare).astype(BF16)
        to = 2 * base + at
        pack[to : to + step, :] = jnp.where(ok, 1.0, 0.0).astype(BF16)
    v_copy.wait()
    for at in range(0, rows, step):
        slot = lax.broadcasted_iota(jnp.int32, (step, dim), 0) + at
        ok = (slot >= first) & (slot < limit)
        to = base + at
        pack[to : to + step, :] = jnp.where(ok, vbuf[at : at + step, :].astype(F32), 0.0).astype(BF16)
    nk_copy.wait()
    nv_copy.wait()


def fresh_mask(me, token, spans, new):
    key = lax.broadcasted_iota(jnp.int32, (token.shape[0], TILE), 1)
    real = key < 2 * new
    key = key + (me - lax.rem(me, 2)) * new
    ok = key <= token
    for k in range(spans.shape[1]):
        lo, hi = spans[0, k], spans[1, k]
        ok = ok | ((token >= lo) & (token < hi) & (key >= lo) & (key < hi))
    return ok & real


def attend(me, owners, cache_dev, new, group, scale, spans, own, other, blocks, outs, scratch):
    *s_refs, fresh_k, fresh_v = scratch
    part, dim = blocks[0].shape
    pair = WIDE // part
    n, rows = len(blocks) // pair, WIDE
    base = cache_dev + new

    odd = lax.rem(me, 2) == 1
    fill = TILE - 2 * new
    fresh = []
    for at in (cache_dev, base + cache_dev):
        mine, theirs = own[at : at + new, :].astype(F32), other[at : at + new, :].astype(F32)
        low, high = jnp.where(odd, theirs, mine), jnp.where(odd, mine, theirs)
        fresh.append(jnp.concatenate([low, high, jnp.zeros((fill, dim), F32)], axis=0))
    fresh_k[...] = fresh[0].astype(BF16)
    fresh_v[:, 0:dim] = fresh[1].astype(BF16)
    fresh_v[:, dim : 2 * dim] = jnp.ones((TILE, dim), F32).astype(BF16)

    tiles = [None] + [(which, at) for which in (0, 1) for at in range(0, cache_dev, CHUNK)]

    def place(tile):
        if tile is None:
            return slice(2 * cache_dev, 2 * cache_dev + TILE)
        start = tile[0] * cache_dev + tile[1]
        return slice(start, start + CHUNK)

    def scores(b, tile, peak):
        q = jnp.concatenate([blocks[pair * b + j][...] for j in range(pair)], axis=0)
        if tile is None:
            keys = fresh_k[...]
        else:
            which, at = tile
            keys = (own, other)[which][at : at + CHUNK, :]
        s = lax.dot_general(q, keys, NT, preferred_element_type=F32)
        if tile is None:
            inside = lax.div(lax.broadcasted_iota(jnp.int32, (part, 1), 0), group)
            token = jnp.concatenate([owners[pair * b + j] * new + inside for j in range(pair)], axis=0)
            s = jnp.where(fresh_mask(me, token, spans, new), s, HIDDEN)
        s_refs[b % 2][:, place(tile)] = s
        for j in range(s.shape[1] // TILE):
            top = s[:, j * TILE : (j + 1) * TILE]
            peak = top if peak is None else jnp.maximum(peak, top)
        return peak

    def weigh(b, tile, top, acc):
        p = jnp.exp((s_refs[b % 2][:, place(tile)] - top) * scale).astype(BF16)
        if tile is None:
            v = fresh_v[...]
        else:
            which, at = tile
            ref = (own, other)[which]
            v, m = base + at, 2 * base + at
            v = jnp.concatenate([ref[v : v + CHUNK, :], ref[m : m + CHUNK, :]], axis=1)
        o = jnp.dot(p, v, preferred_element_type=F32)
        return o if acc is None else acc + o

    peak = None
    for tile in tiles:
        peak = scores(0, tile, peak)
    lane = lax.broadcasted_iota(jnp.int32, (part, dim), 1)
    for b in range(n):
        top = jnp.max(peak, axis=1, keepdims=True)
        acc, peak = None, None
        for tile in tiles:
            acc = weigh(b, tile, top, acc)
            if b + 1 < n:
                peak = scores(b + 1, tile, peak)
        for j in range(pair):
            cut = slice(j * part, (j + 1) * part)
            both = jnp.where(lane == 0, top[cut] * scale, acc[cut, dim : 2 * dim]).T
            write_message(outs[pair * b + j], acc[cut, 0:dim].T, both[0:1], both[1:2])


def blocks_kernel(where, away, cache_dev, new, group, scale, spans, own, other, q_ref, _, out, *scratch):
    me = where()
    near = q_ref.shape[0]
    first = (me - lax.rem(me, 2 * near)) ^ (2 * near if away else 0)
    owners = [first + 2 * j + lax.rem(me, 2) for j in range(near)]
    blocks = [q_ref.at[j] for j in range(near)]
    outs = [out.at[j] for j in range(near)]
    attend(me, owners, cache_dev, new, group, scale, spans, own, other, blocks, outs, scratch)


def spread_kernel(q, _, out, kept):
    for j in range(out.shape[0]):
        out[j] = q[...]


def merge_kernel(got, _, out, kept):
    write_message(out, *merge([got.at[j] for j in range(got.shape[0])]))


def final_kernel(got, back, out):
    numer, _, total = merge([got.at[j] for j in range(got.shape[0])] + [back])
    out[...] = (numer / total).T.astype(BF16)


def on_device(queries, new_keys, new_values, cache_k, cache_v, span_bounds, cache_len, doc_start):
    far, near, cores = (lax.axis_size(name) for name in ("far", "near", "core"))
    new, _, group, dim = queries.shape
    rows = new * group
    cache_dev = cache_k.shape[1]
    packed = 3 * cache_dev + 2 * new
    scale = 1.0 / math.sqrt(dim)

    def where():
        return (lax.axis_index("far") * near + lax.axis_index("near")) * cores + lax.axis_index("core")

    def across(x, axis):
        return lax.ppermute(x, axis, [(0, 1), (1, 0)])

    def quad(x):
        return lax.all_to_all(x, "near", split_axis=0, concat_axis=0, tiled=True)

    hbm = pl.BlockSpec(memory_space=pltpu.HBM)
    vmem = pl.BlockSpec(memory_space=pltpu.VMEM)
    smem = pl.BlockSpec(memory_space=pltpu.SMEM)
    params = pltpu.CompilerParams(vmem_limit_bytes=36 * 1024 * 1024)
    message = jax.ShapeDtypeStruct((dim + EXTRA, rows), BF16)
    dma = pltpu.SemaphoreType.DMA

    q = queries.reshape(rows, dim)
    q_far = across(q, "far")
    own = pl.pallas_call(
        functools.partial(pack_kernel, far * near * cores, where),
        out_shape=jax.ShapeDtypeStruct((packed, dim), BF16),
        in_specs=[hbm] * 4 + [smem] * 2,
        out_specs=vmem,
        scratch_shapes=[
            pltpu.VMEM((cache_dev, dim), BF16),
            pltpu.VMEM((cache_dev, dim), BF16),
            dma,
            dma,
            dma((2,)),
        ],
        compiler_params=params,
        name="pack",
    )(cache_k, cache_v, new_keys.reshape(new, dim), new_values.reshape(new, dim), cache_len, doc_start)
    anywhere = pl.BlockSpec(memory_space=pl.ANY)
    q_far, own = pl.pallas_call(
        spread_kernel,
        out_shape=[jax.ShapeDtypeStruct((near, rows, dim), BF16), jax.ShapeDtypeStruct(own.shape, BF16)],
        in_specs=[vmem, anywhere],
        out_specs=[vmem, anywhere],
        input_output_aliases={1: 1},
        compiler_params=params,
        name="spread",
    )(q_far, own)
    q_far = quad(q_far)
    other = across(own, "core")
    q_near = lax.all_gather(q, "near", axis=0)

    spans = span_bounds.T
    cost = pl.CostEstimate(
        flops=4 * near * rows * 2 * cache_dev * dim,
        bytes_accessed=4 << 20,
        transcendentals=near * rows * 2 * cache_dev,
    )

    sizes = (cache_dev, new, group, scale)
    scratch = [pltpu.VMEM((WIDE, 2 * cache_dev + TILE), F32)] * 2
    scratch += [pltpu.VMEM((TILE, dim), BF16), pltpu.VMEM((TILE, 2 * dim), BF16)]
    partials = jax.ShapeDtypeStruct((near,) + message.shape, BF16)

    def attend_blocks(blocks, before, away, name):
        return pl.pallas_call(
            functools.partial(blocks_kernel, where, away, *sizes),
            out_shape=partials,
            in_specs=[smem] + [vmem] * 3 + [anywhere],
            out_specs=vmem,
            scratch_shapes=scratch,
            compiler_params=params,
            cost_estimate=cost,
            name=name,
        )(spans, own, other, blocks, before)

    far_out = attend_blocks(q_far, q_far, True, "far_blocks")
    far_got = quad(far_out)
    near_out = attend_blocks(q_near, far_out, False, "near_blocks")
    far_sum, near_out = pl.pallas_call(
        merge_kernel,
        out_shape=[message, partials],
        in_specs=[vmem, anywhere],
        out_specs=[vmem, anywhere],
        input_output_aliases={1: 1},
        compiler_params=params,
        name="merge_far",
    )(far_got, near_out)
    back = across(far_sum, "far")
    near_got = quad(near_out)
    result = pl.pallas_call(
        final_kernel,
        out_shape=jax.ShapeDtypeStruct((rows, dim), BF16),
        in_specs=[vmem] * 2,
        out_specs=vmem,
        compiler_params=params,
        name="merge_all",
    )(near_got, back)
    return result.reshape(new, 1, group, dim)


def solution(mesh):
    ctx, kvh, sess = (mesh.shape[name] for name in ("ctx", "kvh", "sess"))
    devices = mesh.devices.reshape(2, ctx // 4, 2, kvh, sess)
    split = Mesh(devices, ("far", "near", "core", "kvh", "sess"))
    ctx = ("far", "near", "core")
    return jax.shard_map(
        on_device,
        mesh=split,
        in_specs=(
            P(("sess",) + ctx, "kvh", None, None),
            P(("sess",) + ctx, "kvh", None),
            P(("sess",) + ctx, "kvh", None),
            P(("sess", "kvh"), ctx, None),
            P(("sess", "kvh"), ctx, None),
            P("sess", None),
            P("sess"),
            P("sess"),
        ),
        out_specs=P(("sess",) + ctx, "kvh", None, None),
        check_vma=False,
    )
```

time: 73.3 us -> 83.6 us (1.14)
  blocking collectives: 0 us -> 27.7 us
  starting transfers between devices: 40.2 us -> 29.5 us
  waiting for transfers between devices: 8.97 us -> 4.7 us
  Pallas kernels: 18.7 us -> 16.2 us
    all_gather x0 -> x1, blocking collectives: none -> 15.5 us  [on_device(): q_near = lax.all_gather(q, 'near', axis=0)]
    all_to_all x0 -> x1, blocking collectives: none -> 12.2 us  [quad(): return lax.all_to_all(x, 'near', split_axis=0, concat_axis=0, tiled=True)]
    all_to_all x4 -> x2, starting transfers between devices: 22.2 us -> 11.8 us  [quad(): return lax.all_to_all(x, 'near', split_axis=0, concat_axis=0, tiled=True)]
    all_to_all x4 -> x2, waiting for transfers between devices: 3.62 us -> 0.01 us  [quad(): return lax.all_to_all(x, 'near', split_axis=0, concat_axis=0, tiled=True)]
    pallas_call x4, Pallas kernels: 16.5 us -> 14.3 us  [the longest x2 14.1 us: attend_blocks(): pl.pallas_call(functools.partial(blocks_kernel, where, away, *sizes), out...]
  transfers between devices with their start and end apart: 7 -> 5, of which waited for: 2 -> 1; matrix products, arithmetic and copies ran while one was open for 0% -> 0% of each run, Pallas kernels for 23% -> 10%
where the time goes in v4:
time: 83.6 us; the launch traced here: 83 us
  starting transfers between devices  29.5 us (35%)
  blocking collectives  27.7 us (33%)
  Pallas kernels  16.2 us (19%)
  waiting for transfers between devices  4.7 us (6%)
  local copies, waits for them, and re-layouts  4.11 us (5%)
    ppermute x3, starting transfers between devices, across(): return lax.ppermute(x, axis, [(0, 1), (1, 0)])  17.7 us
    all_gather x1, blocking collectives, on_device(): q_near = lax.all_gather(q, 'near', axis=0)  15.5 us
    pallas_call x2, Pallas kernels, attend_blocks(): pl.pallas_call(functools.partial(blocks_kernel, where, away, *sizes), out...  14.1 us
    all_to_all x1, blocking collectives, quad(): return lax.all_to_all(x, 'near', split_axis=0, concat_axis=0, tiled=True)  12.2 us
    all_to_all x2, starting transfers between devices, quad(): return lax.all_to_all(x, 'near', split_axis=0, concat_axis=0, tiled=True)  11.8 us
    ppermute x3, waiting for transfers between devices, across(): return lax.ppermute(x, axis, [(0, 1), (1, 0)])  4.7 us
    unnamed x14, local copies, waits for them, and re-layouts  4.11 us
  transfers between devices with their start and end apart: 5, of which 1 were waited for; matrix products, arithmetic and copies ran while one was open for 0% of the time, Pallas kernels for 10%

profile of v4, /device:TPU:76, one launch (start us, length us, event | category | flops | bytes accessed | tf_op | source)
XLA Modules:
  0.0 83.0 jit_solution(410314746280095404)
XLA Ops:
  0.0 9.1 %collective-permute-start = (bf16[256,128]{1,0:T(8,128)(2,1)}, bf16[256,128]{1,0:T(8,128)(2,1)S(1)}, u32[]{:S(2)}, u32[]{:S(2)}) collective-permute-start(bf16[256,128]{1,0:T(8,128)(2,1)} %bitcast.12), channel_id=1, source_target_pairs={{0,256},{256,0},{1,257},{257,1},{2,258},{258,2},{3,259},{259,3},{4... | collective-permute-start | bytes 196616 | tf_op jit(solution)/shard_map/ppermute | solution.py:212
  9.7 0.0 copy-start
  9.8 1.0 %copy-done = bf16[1,2048,128]{2,1,0:T(8,128)(2,1)S(1)} copy-done((bf16[1,2048,128]{2,1,0:T(8,128)(2,1)S(1)}, bf16[1,2048,128]{2,1,0:T(8,128)(2,1)}, u32[]{:S(2)}) %copy-start) | copy-done | bytes 524312
  10.8 0.0 copy-start.1
  10.8 1.0 %copy-done.1 = bf16[1,2048,128]{2,1,0:T(8,128)(2,1)S(1)} copy-done((bf16[1,2048,128]{2,1,0:T(8,128)(2,1)S(1)}, bf16[1,2048,128]{2,1,0:T(8,128)(2,1)}, u32[]{:S(2)}) %copy-start.1) | copy-done | bytes 524312
  11.8 0.0 copy-start.2
  11.8 0.7 copy-done.2
  12.5 0.0 copy-start.3
  12.5 0.7 copy-done.3
  13.2 0.0 copy-start.4
  13.2 0.7 copy-done.4
  13.9 1.2 %pack.1._ = bf16[6176,128]{1,0:T(8,128)(2,1)S(1)} custom-call(bf16[1,2048,128]{2,1,0:T(8,128)(2,1)S(1)} %copy-done, bf16[1,2048,128]{2,1,0:T(8,128)(2,1)S(1)} %copy-done.1, bf16[16,128]{1,0:T(8,128)(2,1)S(1)} %bitcast.8, bf16[16,128]{1,0:T(8,128)(2,1)S(1)} %bitcast.9, s32[16]{0:T(128)S(1)} %copy-done.4, s32[1]{0:T(128)S(6)} %copy.15.refs_5_), custom_call_target="tpu_custom_call" | custom-call | tf_op jit(solution)/shard_map/pack/pallas_call | solution.py:226
  15.1 0.0 copy-start.5
  15.1 0.0 collective-permute-done.q
  15.1 1.9 %collective-permute-start.1 = (bf16[6176,128]{1,0:T(8,128)(2,1)S(1)}, bf16[6176,128]{1,0:T(8,128)(2,1)S(1)}, u32[]{:S(2)}, u32[]{:S(2)}) collective-permute-start(bf16[6176,128]{1,0:T(8,128)(2,1)S(1)} %get-tuple-element.9.own), channel_id=1, source_target_pairs={{0,32},{32,0},{1,33},{33,1},{2,34},{34,2},{3,35},{35,3},{4,36},{36... | collective-permute-start | bytes 4743176 | tf_op jit(solution)/shard_map/ppermute | solution.py:212
  17.1 12.2 %all_to_all.15.q_ref._ = bf16[4,256,128]{2,1,0:T(8,128)(2,1)S(1)} all-to-all(bf16[4,256,128]{2,1,0:T(8,128)(2,1)S(1)} %get-tuple-element.10), channel_id=1, replica_groups=mesh['far'=2,'near'=4,'core'=2,'kvh'=8,'sess'=4] {'near'}, dimensions={0} | all-to-all | bytes 524288 | tf_op jit(solution)/shard_map/all_to_all | solution.py:215
  29.2 0.0 collective-permute-done.1.other
  29.2 0.0 copy-done.5
  29.2 0.0 copy-start.6
  29.2 7.1 %far_blocks.1._ = bf16[4,144,256]{2,1,0:T(8,128)(2,1)} custom-call(s32[2,4]{1,0:T(2,128)S(1)} %bitcast.10, bf16[6176,128]{1,0:T(8,128)(2,1)S(1)} %get-tuple-element.9.own, bf16[6176,128]{1,0:T(8,128)(2,1)S(1)} %collective-permute-done.1.other, bf16[4,256,128]{2,1,0:T(8,128)(2,1)S(1)} %all_to_all.15.q_ref._, bf16[4,256,128]{2,1,0:T(8,128)(2,1)S(1)} %all_to_all.15.q_ref._), custom_call_target="tpu_custom_call" | custom-call | flops 2147483648 | bytes 4194304 | tf_op jit(solution)/shard_map/far_blocks/pallas_call | solution.py:268
  36.3 6.1 %all-to-all-start.1 = ((bf16[4,144,256]{2,1,0:T(8,128)(2,1)}), bf16[4,144,256]{2,1,0:T(8,128)(2,1)S(1)}, u32[]{:S(2)}, u32[]{:S(2)}) async-start(bf16[4,144,256]{2,1,0:T(8,128)(2,1)} %far_blocks.1._), calls=%async_computation.1 | async-start | bytes 589824 | tf_op jit(solution)/shard_map/all_to_all | solution.py:215
  42.4 0.0 copy-done.6
  42.4 15.5 %all_gather.3.q_ref = bf16[4,256,128]{2,1,0:T(8,128)(2,1)S(1)} all-gather(bf16[1,256,128]{2,1,0:T(8,128)(2,1)S(1)} %bitcast.13), channel_id=1, replica_groups=mesh['far'=2,'near'=4,'core'=2,'kvh'=8,'sess'=4] {'near'}, dimensions={0}, use_global_device_ids=true | all-gather | bytes 327680 | tf_op jit(solution)/shard_map/all_gather | solution.py:253
  58.0 7.1 %near_blocks.1._ = bf16[4,144,256]{2,1,0:T(8,128)(2,1)} custom-call(s32[2,4]{1,0:T(2,128)S(1)} %bitcast.11, bf16[6176,128]{1,0:T(8,128)(2,1)S(1)} %get-tuple-element.9.own, bf16[6176,128]{1,0:T(8,128)(2,1)S(1)} %collective-permute-done.1.other, bf16[4,256,128]{2,1,0:T(8,128)(2,1)S(1)} %all_gather.3.q_ref, bf16[4,144,256]{2,1,0:T(8,128)(2,1)} %far_blocks.1._), custom_call_target="tpu_custom_call" | custom-call | flops 2147483648 | bytes 4194304 | tf_op jit(solution)/shard_map/near_blocks/pallas_call | solution.py:268
  65.1 0.0 all-to-all-done.1.got
  65.1 0.1 merge_far.1
  65.1 5.7 %all-to-all-start.2 = ((bf16[4,144,256]{2,1,0:T(8,128)(2,1)}), bf16[4,144,256]{2,1,0:T(8,128)(2,1)S(1)}, u32[]{:S(2)}, u32[]{:S(2)}) async-start(bf16[4,144,256]{2,1,0:T(8,128)(2,1)} %get-tuple-element.11), calls=%async_computation.2 | async-start | bytes 589824 | tf_op jit(solution)/shard_map/all_to_all | solution.py:215
  70.9 6.7 %collective-permute-start.2 = (bf16[144,256]{1,0:T(8,128)(2,1)S(1)}, bf16[144,256]{1,0:T(8,128)(2,1)S(1)}, u32[]{:S(2)}, u32[]{:S(2)}) collective-permute-start(bf16[144,256]{1,0:T(8,128)(2,1)S(1)} %get-tuple-element.12), channel_id=1, source_target_pairs={{0,256},{256,0},{1,257},{257,1},{2,258},{258,2},{3,259},{259,3},{4... | collective-permute-start | bytes 221192 | tf_op jit(solution)/shard_map/ppermute | solution.py:212
  77.5 4.7 %collective-permute-done.2.back = bf16[144,256]{1,0:T(8,128)(2,1)S(1)} collective-permute-done((bf16[144,256]{1,0:T(8,128)(2,1)S(1)}, bf16[144,256]{1,0:T(8,128)(2,1)S(1)}, u32[]{:S(2)}, u32[]{:S(2)}) %collective-permute-start.2) | collective-permute-done | bytes 73760 | tf_op jit(solution)/shard_map/ppermute | solution.py:212
  82.2 0.0 all-to-all-done.2.got
  82.2 0.8 merge_all.1
  (1 shorter events, 0.0 us)
Async XLA Ops:
  0.0 15.1 %collective-permute-start = (bf16[256,128]{1,0:T(8,128)(2,1)}, bf16[256,128]{1,0:T(8,128)(2,1)S(1)}, u32[]{:S(2)}, u32[]{:S(2)}) collective-permute-start(bf16[256,128]{1,0:T(8,128)(2,1)} %bitcast.12), channel_id=1, source_target_pairs={{0,256},{256,0},{1,257},{257,1},{2,258},{258,2},{3,259},{259,3},{4... | collective-permute-start | bytes 196616 | tf_op jit(solution)/shard_map/ppermute | solution.py:212
  9.7 1.0 %copy-start = (bf16[1,2048,128]{2,1,0:T(8,128)(2,1)S(1)}, bf16[1,2048,128]{2,1,0:T(8,128)(2,1)}, u32[]{:S(2)}) copy-start(bf16[1,2048,128]{2,1,0:T(8,128)(2,1)} %refs_0_.1) | copy-start | bytes 1572868
  10.8 1.0 %copy-start.1 = (bf16[1,2048,128]{2,1,0:T(8,128)(2,1)S(1)}, bf16[1,2048,128]{2,1,0:T(8,128)(2,1)}, u32[]{:S(2)}) copy-start(bf16[1,2048,128]{2,1,0:T(8,128)(2,1)} %refs_1_.1) | copy-start | bytes 1572868
  11.8 0.7 copy-start.2
  12.5 0.7 copy-start.3
  13.2 0.7 copy-start.4
  15.1 14.2 %copy-start.5 = (s32[4,2]{0,1:T(2,128)S(1)}, s32[4,2]{0,1:T(2,128)}, u32[]{:S(2)}) copy-start(s32[4,2]{0,1:T(2,128)} %param.13) | copy-start | bytes 100
  15.1 14.1 %collective-permute-start.1 = (bf16[6176,128]{1,0:T(8,128)(2,1)S(1)}, bf16[6176,128]{1,0:T(8,128)(2,1)S(1)}, u32[]{:S(2)}, u32[]{:S(2)}) collective-permute-start(bf16[6176,128]{1,0:T(8,128)(2,1)S(1)} %get-tuple-element.9.own), channel_id=1, source_target_pairs={{0,32},{32,0},{1,33},{33,1},{2,34},{34,2},{3,35},{35,3},{4,36},{36... | collective-permute-start | bytes 4743176 | tf_op jit(solution)/shard_map/ppermute | solution.py:212
  29.2 13.2 %copy-start.6 = (bf16[16,1,16,128]{3,2,1,0:T(8,128)(2,1)S(1)}, bf16[16,1,16,128]{3,2,1,0:T(8,128)(2,1)}, u32[]{:S(2)}) copy-start(bf16[16,1,16,128]{3,2,1,0:T(8,128)(2,1)} %param.8) | copy-start | bytes 196612
  36.3 28.8 %all-to-all-start.1 = ((bf16[4,144,256]{2,1,0:T(8,128)(2,1)}), bf16[4,144,256]{2,1,0:T(8,128)(2,1)S(1)}, u32[]{:S(2)}, u32[]{:S(2)}) async-start(bf16[4,144,256]{2,1,0:T(8,128)(2,1)} %far_blocks.1._), calls=%async_computation.1 | async-start | bytes 589824 | tf_op jit(solution)/shard_map/all_to_all | solution.py:215
  65.1 17.1 %all-to-all-start.2 = ((bf16[4,144,256]{2,1,0:T(8,128)(2,1)}), bf16[4,144,256]{2,1,0:T(8,128)(2,1)S(1)}, u32[]{:S(2)}, u32[]{:S(2)}) async-start(bf16[4,144,256]{2,1,0:T(8,128)(2,1)} %get-tuple-element.11), calls=%async_computation.2 | async-start | bytes 589824 | tf_op jit(solution)/shard_map/all_to_all | solution.py:215
  70.9 11.4 %collective-permute-start.2 = (bf16[144,256]{1,0:T(8,128)(2,1)S(1)}, bf16[144,256]{1,0:T(8,128)(2,1)S(1)}, u32[]{:S(2)}, u32[]{:S(2)}) collective-permute-start(bf16[144,256]{1,0:T(8,128)(2,1)S(1)} %get-tuple-element.12), channel_id=1, source_target_pairs={{0,256},{256,0},{1,257},{257,1},{2,258},{258,2},{3,259},{259,3},{4... | collective-permute-start | bytes 221192 | tf_op jit(solution)/shard_map/ppermute | solution.py:212

commit v5 on v4

--- a/solution.py
+++ b/solution.py
@@ -14,7 +14,6 @@
 HIDDEN = -1e30
 CHUNK = 1024
 TILE = 128
-WIDE = 512
 EXTRA = 16
 NT = (((1,), (1,)), ((), ()))
 
@@ -100,11 +99,10 @@
     return ok & real
 
 
-def attend(me, owners, cache_dev, new, group, scale, spans, own, other, blocks, outs, scratch):
+def attend(me, owners, pair, cache_dev, new, group, scale, spans, own, other, blocks, outs, scratch):
     *s_refs, fresh_k, fresh_v = scratch
     part, dim = blocks[0].shape
-    pair = WIDE // part
-    n, rows = len(blocks) // pair, WIDE
+    n = len(blocks) // pair
     base = cache_dev + new
 
     odd = lax.rem(me, 2) == 1
@@ -138,14 +136,14 @@
             inside = lax.div(lax.broadcasted_iota(jnp.int32, (part, 1), 0), group)
             token = jnp.concatenate([owners[pair * b + j] * new + inside for j in range(pair)], axis=0)
             s = jnp.where(fresh_mask(me, token, spans, new), s, HIDDEN)
-        s_refs[b % 2][:, place(tile)] = s
+        s_refs[b % len(s_refs)][:, place(tile)] = s
         for j in range(s.shape[1] // TILE):
             top = s[:, j * TILE : (j + 1) * TILE]
             peak = top if peak is None else jnp.maximum(peak, top)
         return peak
 
     def weigh(b, tile, top, acc):
-        p = jnp.exp((s_refs[b % 2][:, place(tile)] - top) * scale).astype(BF16)
+        p = jnp.exp((s_refs[b % len(s_refs)][:, place(tile)] - top) * scale).astype(BF16)
         if tile is None:
             v = fresh_v[...]
         else:
@@ -173,14 +171,33 @@
             write_message(outs[pair * b + j], acc[cut, 0:dim].T, both[0:1], both[1:2])
 
 
-def blocks_kernel(where, away, cache_dev, new, group, scale, spans, own, other, q_ref, _, out, *scratch):
+def own_far_kernel(where, sizes, spans, own, other, q_far, q, out, slots, *scratch):
+    me = where()
+    near = slots.shape[0]
+    for j in range(near):
+        slots[j] = q[...]
+    attend(me, [me ^ (2 * near)], 1, *sizes, spans, own, other, [q_far], [out], scratch)
+
+
+def far_kernel(where, sizes, spans, own, other, q_ref, mine, out, *scratch):
     me = where()
     near = q_ref.shape[0]
-    first = (me - lax.rem(me, 2 * near)) ^ (2 * near if away else 0)
+    at = lax.rem(lax.div(me, 2), near)
+    first = (me - lax.rem(me, 2 * near)) ^ (2 * near)
+    out[at] = mine[...]
+    members = [lax.rem(at + j, near) for j in range(1, near)]
+    owners = [first + 2 * j + lax.rem(me, 2) for j in members]
+    blocks, outs = [q_ref.at[j] for j in members], [out.at[j] for j in members]
+    attend(me, owners, near - 1, *sizes, spans, own, other, blocks, outs, scratch)
+
+
+def near_kernel(where, sizes, spans, own, other, q_ref, _, out, *scratch):
+    me = where()
+    near = q_ref.shape[0]
+    first = me - lax.rem(me, 2 * near)
     owners = [first + 2 * j + lax.rem(me, 2) for j in range(near)]
-    blocks = [q_ref.at[j] for j in range(near)]
-    outs = [out.at[j] for j in range(near)]
-    attend(me, owners, cache_dev, new, group, scale, spans, own, other, blocks, outs, scratch)
+    blocks, outs = [q_ref.at[j] for j in range(near)], [out.at[j] for j in range(near)]
+    attend(me, owners, 2, *sizes, spans, own, other, blocks, outs, scratch)
 
 
 def spread_kernel(q, _, out, kept):
@@ -239,7 +256,7 @@
         name="pack",
     )(cache_k, cache_v, new_keys.reshape(new, dim), new_values.reshape(new, dim), cache_len, doc_start)
     anywhere = pl.BlockSpec(memory_space=pl.ANY)
-    q_far, own = pl.pallas_call(
+    q_slots, own = pl.pallas_call(
         spread_kernel,
         out_shape=[jax.ShapeDtypeStruct((near, rows, dim), BF16), jax.ShapeDtypeStruct(own.shape, BF16)],
         in_specs=[vmem, anywhere],
@@ -248,37 +265,38 @@
         compiler_params=params,
         name="spread",
     )(q_far, own)
-    q_far = quad(q_far)
+    q_slots = quad(q_slots)
     other = across(own, "core")
-    q_near = lax.all_gather(q, "near", axis=0)
 
     spans = span_bounds.T
-    cost = pl.CostEstimate(
-        flops=4 * near * rows * 2 * cache_dev * dim,
-        bytes_accessed=4 << 20,
-        transcendentals=near * rows * 2 * cache_dev,
+    sizes = (cache_dev, new, group, scale)
+    partials = jax.ShapeDtypeStruct((near,) + message.shape, BF16)
+
+    def attend_call(kernel, last, out_shape, unit, count, name):
+        return pl.pallas_call(
+            functools.partial(kernel, where, sizes),
+            out_shape=out_shape,
+            in_specs=[smem] + [vmem] * 3 + [last],
+            out_specs=jax.tree.map(lambda _: vmem, out_shape),
+            scratch_shapes=[pltpu.VMEM((unit * rows, 2 * cache_dev + TILE), F32)] * (count // unit)
+            + [pltpu.VMEM((TILE, dim), BF16), pltpu.VMEM((TILE, 2 * dim), BF16)],
+            compiler_params=params,
+            cost_estimate=pl.CostEstimate(
+                flops=4 * count * rows * 2 * cache_dev * dim,
+                bytes_accessed=4 << 20,
+                transcendentals=count * rows * 2 * cache_dev,
+            ),
+            name=name,
+        )
+
+    slots = jax.ShapeDtypeStruct((near, rows, dim), BF16)
+    own_far, near_slots = attend_call(own_far_kernel, vmem, [message, slots], 1, 1, "own_far")(spans, own, other, q_far, q)
+    q_near = quad(near_slots)
+    far_out = attend_call(far_kernel, vmem, partials, near - 1, near - 1, "far_blocks")(
+        spans, own, other, q_slots, own_far
     )
-
-    sizes = (cache_dev, new, group, scale)
-    scratch = [pltpu.VMEM((WIDE, 2 * cache_dev + TILE), F32)] * 2
-    scratch += [pltpu.VMEM((TILE, dim), BF16), pltpu.VMEM((TILE, 2 * dim), BF16)]
-    partials = jax.ShapeDtypeStruct((near,) + message.shape, BF16)
-
-    def attend_blocks(blocks, before, away, name):
-        return pl.pallas_call(
-            functools.partial(blocks_kernel, where, away, *sizes),
-            out_shape=partials,
-            in_specs=[smem] + [vmem] * 3 + [anywhere],
-            out_specs=vmem,
-            scratch_shapes=scratch,
-            compiler_params=params,
-            cost_estimate=cost,
-            name=name,
-        )(spans, own, other, blocks, before)
-
-    far_out = attend_blocks(q_far, q_far, True, "far_blocks")
     far_got = quad(far_out)
-    near_out = attend_blocks(q_near, far_out, False, "near_blocks")
+    near_out = attend_call(near_kernel, anywhere, partials, 2, near, "near_blocks")(spans, own, other, q_near, far_out)
     far_sum, near_out = pl.pallas_call(
         merge_kernel,
         out_shape=[message, partials],

time: 83.6 us -> 81.4 us (0.974)
  the two profiles are of different devices: /device:TPU:76 before, /device:TPU:66 now
where the time goes in v5:
time: 81.4 us; the launch traced here: 80.6 us
  starting transfers between devices  40.5 us (50%)
  Pallas kernels  20.3 us (25%)
  local copies, waits for them, and re-layouts  12.4 us (15%)
  waiting for transfers between devices  6.57 us (8%)
    all_to_all x4, starting transfers between devices, quad(): return lax.all_to_all(x, 'near', split_axis=0, concat_axis=0, tiled=True)  22.8 us
    ppermute x3, starting transfers between devices, across(): return lax.ppermute(x, axis, [(0, 1), (1, 0)])  17.7 us
    unnamed x36, local copies, waits for them, and re-layouts  12.4 us
    pallas_call x1, Pallas kernels, on_device(): attend_call(far_kernel, vmem, partials, near - 1, near - 1, 'far_blocks')  8.04 us
    pallas_call x1, Pallas kernels, on_device(): attend_call(near_kernel, anywhere, partials, 2, near, 'near_blocks')  6.73 us
    ppermute x3, waiting for transfers between devices, across(): return lax.ppermute(x, axis, [(0, 1), (1, 0)])  5.55 us
    pallas_call x1, Pallas kernels, on_device(): attend_call(own_far_kernel, vmem, [message, slots], 1, 1, 'own_far')  3.42 us
  transfers between devices with their start and end apart: 7, of which 2 were waited for; matrix products, arithmetic and copies ran while one was open for 0% of the time, Pallas kernels for 24%

profile of v5, /device:TPU:66, one launch (start us, length us, event | category | flops | bytes accessed | tf_op | source)
XLA Modules:
  0.0 80.6 jit_solution(17182789636569455639)
XLA Ops:
  0.0 9.1 %collective-permute-start = (bf16[256,128]{1,0:T(8,128)(2,1)}, bf16[256,128]{1,0:T(8,128)(2,1)S(1)}, u32[]{:S(2)}, u32[]{:S(2)}) collective-permute-start(bf16[256,128]{1,0:T(8,128)(2,1)} %bitcast.7), channel_id=1, source_target_pairs={{0,256},{256,0},{1,257},{257,1},{2,258},{258,2},{3,259},{259,3},{4... | collective-permute-start | bytes 196616 | tf_op jit(solution)/shard_map/ppermute | solution.py:229
  9.7 0.0 copy-start.3
  9.8 1.0 %copy-done.3 = bf16[1,2048,128]{2,1,0:T(8,128)(2,1)S(1)} copy-done((bf16[1,2048,128]{2,1,0:T(8,128)(2,1)S(1)}, bf16[1,2048,128]{2,1,0:T(8,128)(2,1)}, u32[]{:S(2)}) %copy-start.3) | copy-done | bytes 524312
  10.8 0.0 copy-start.4
  10.8 1.0 %copy-done.4 = bf16[1,2048,128]{2,1,0:T(8,128)(2,1)S(1)} copy-done((bf16[1,2048,128]{2,1,0:T(8,128)(2,1)S(1)}, bf16[1,2048,128]{2,1,0:T(8,128)(2,1)}, u32[]{:S(2)}) %copy-start.4) | copy-done | bytes 524312
  11.8 0.0 copy-start.10
  11.8 0.7 copy-done.10
  12.5 0.0 copy-start.11
  12.5 0.7 copy-done.11
  13.2 0.0 copy-start.15
  13.2 0.7 copy-done.15
  13.9 1.2 %pack.1._ = bf16[6176,128]{1,0:T(8,128)(2,1)S(1)} custom-call(bf16[1,2048,128]{2,1,0:T(8,128)(2,1)S(1)} %copy-done.3, bf16[1,2048,128]{2,1,0:T(8,128)(2,1)S(1)} %copy-done.4, bf16[16,128]{1,0:T(8,128)(2,1)S(1)} %bitcast.9, bf16[16,128]{1,0:T(8,128)(2,1)S(1)} %bitcast.10, s32[16]{0:T(128)S(1)} %copy-done.15, s32[1]{0:T(128)S(6)} %copy.14.refs_5_), custom_call_target="tpu_custom_call" | custom-call | tf_op jit(solution)/shard_map/pack/pallas_call | solution.py:243
  15.1 0.0 copy-start.9
  15.1 0.0 collective-permute-done.q.q_far
  15.1 0.0 copy-start.7
  15.1 0.7 copy-done.7
  15.8 1.9 %collective-permute-start.1 = (bf16[6176,128]{1,0:T(8,128)(2,1)S(1)}, bf16[6176,128]{1,0:T(8,128)(2,1)S(1)}, u32[]{:S(2)}, u32[]{:S(2)}) collective-permute-start(bf16[6176,128]{1,0:T(8,128)(2,1)S(1)} %get-tuple-element.11.own), channel_id=1, source_target_pairs={{0,32},{32,0},{1,33},{33,1},{2,34},{34,2},{3,35},{35,3},{4,36},{36... | collective-permute-start | bytes 4743176 | tf_op jit(solution)/shard_map/ppermute | solution.py:229
  17.7 5.6 %all-to-all-start = ((bf16[4,256,128]{2,1,0:T(8,128)(2,1)}), bf16[4,256,128]{2,1,0:T(8,128)(2,1)S(1)}, u32[]{:S(2)}, u32[]{:S(2)}) async-start(bf16[4,256,128]{2,1,0:T(8,128)(2,1)} %copy-done.7), calls=%async_computation | async-start | bytes 524288 | tf_op jit(solution)/shard_map/all_to_all | solution.py:232
  23.3 0.0 collective-permute-done.1.other
  23.3 0.0 copy-done.9
  23.3 0.7 copy-done.12
  24.0 3.4 %own_far.1 = (bf16[144,256]{1,0:T(8,128)(2,1)S(1)}, bf16[4,256,128]{2,1,0:T(8,128)(2,1)S(1)}) custom-call(s32[2,4]{1,0:T(2,128)S(1)} %bitcast.11, bf16[6176,128]{1,0:T(8,128)(2,1)S(1)} %get-tuple-element.11.own, bf16[6176,128]{1,0:T(8,128)(2,1)S(1)} %collective-permute-done.1.other, bf16[256,128]{1,0:T(8,128)(2,1)S(1)} %collective-permute-done.q.q_far, ...), custom_call_target="tpu_custom_call" | custom-call | flops 536870912 | bytes 4194304 | tf_op jit(solution)/shard_map/own_far/pallas_call | solution.py:293
  27.4 0.0 copy-start.8
  27.4 0.7 copy-done.8
  28.1 0.6 copy-done.16
  28.8 1.0 %all-to-all-done.q_ref = bf16[4,256,128]{2,1,0:T(8,128)(2,1)S(1)} async-done(((bf16[4,256,128]{2,1,0:T(8,128)(2,1)}), bf16[4,256,128]{2,1,0:T(8,128)(2,1)S(1)}, u32[]{:S(2)}, u32[]{:S(2)}) %all-to-all-start) | async-done | bytes 262176 | tf_op jit(solution)/shard_map/all_to_all | solution.py:232
  29.8 7.1 %all-to-all-start.2 = ((bf16[4,256,128]{2,1,0:T(8,128)(2,1)}), bf16[4,256,128]{2,1,0:T(8,128)(2,1)}, u32[]{:S(2)}, u32[]{:S(2)}) async-start(bf16[4,256,128]{2,1,0:T(8,128)(2,1)} %copy-done.8), calls=%async_computation.2 | async-start | bytes 524288 | tf_op jit(solution)/shard_map/all_to_all | solution.py:232
  36.8 0.7 copy-done.13
  37.5 0.9 %copy-done.17 = bf16[144,256]{1,0:T(8,128)(2,1)S(1)} copy-done((bf16[144,256]{1,0:T(8,128)(2,1)S(1)}, bf16[144,256]{1,0:T(8,128)(2,1)}, u32[]{:S(2)}) %copy-start.17) | copy-done | bytes 73752
  38.4 8.0 %far_blocks.1._ = bf16[4,144,256]{2,1,0:T(8,128)(2,1)S(1)} custom-call(s32[2,4]{1,0:T(2,128)S(1)} %bitcast.12, bf16[6176,128]{1,0:T(8,128)(2,1)S(1)} %get-tuple-element.11.own, bf16[6176,128]{1,0:T(8,128)(2,1)S(1)} %collective-permute-done.1.other, bf16[4,256,128]{2,1,0:T(8,128)(2,1)S(1)} %all-to-all-done.q_ref, bf16[144,256]{1,0:T(8,128)(2,1)S(1)} %copy-done.17), custom_call_target="tpu_custom_call" | custom-call | flops 1610612736 | bytes 4194304 | tf_op jit(solution)/shard_map/far_blocks/pallas_call | solution.py:295
  46.5 0.0 copy-start.5
  46.5 0.7 copy-done.5
  47.2 0.0 all-to-all-done.2.q_ref
  47.2 5.1 %all-to-all-start.1 = ((bf16[4,144,256]{2,1,0:T(8,128)(2,1)}), bf16[4,144,256]{2,1,0:T(8,128)(2,1)S(1)}, u32[]{:S(2)}, u32[]{:S(2)}) async-start(bf16[4,144,256]{2,1,0:T(8,128)(2,1)} %copy-done.5), calls=%async_computation.1 | async-start | bytes 589824 | tf_op jit(solution)/shard_map/all_to_all | solution.py:232
  52.3 0.0 copy-done.14
  52.3 1.0 %copy-done.6 = bf16[4,144,256]{2,1,0:T(8,128)(2,1)S(1)} copy-done((bf16[4,144,256]{2,1,0:T(8,128)(2,1)S(1)}, bf16[4,144,256]{2,1,0:T(8,128)(2,1)}, u32[]{:S(2)}) %copy-start.6) | copy-done | bytes 294936
  53.3 6.7 %near_blocks.1._ = bf16[4,144,256]{2,1,0:T(8,128)(2,1)S(1)} custom-call(s32[2,4]{1,0:T(2,128)S(1)} %bitcast.13, bf16[6176,128]{1,0:T(8,128)(2,1)S(1)} %get-tuple-element.11.own, bf16[6176,128]{1,0:T(8,128)(2,1)S(1)} %collective-permute-done.1.other, bf16[4,256,128]{2,1,0:T(8,128)(2,1)} %all-to-all-done.2.q_ref, bf16[4,144,256]{2,1,0:T(8,128)(2,1)S(1)} %copy-done.6), custom_call_target="tpu_custom_call" | custom-call | flops 2147483648 | bytes 4194304 | tf_op jit(solution)/shard_map/near_blocks/pallas_call | solution.py:299
  60.0 0.7 copy-done
  60.7 0.0 all-to-all-done.1.got
  60.7 1.0 %copy-done.1 = bf16[4,144,256]{2,1,0:T(8,128)(2,1)S(1)} copy-done((bf16[4,144,256]{2,1,0:T(8,128)(2,1)S(1)}, bf16[4,144,256]{2,1,0:T(8,128)(2,1)}, u32[]{:S(2)}) %copy-start.1) | copy-done | bytes 294936
  61.7 0.1 merge_far.1
  61.7 0.0 copy-start.2
  61.8 0.7 copy-done.2
  62.5 5.1 %all-to-all-start.3 = ((bf16[4,144,256]{2,1,0:T(8,128)(2,1)}), bf16[4,144,256]{2,1,0:T(8,128)(2,1)S(1)}, u32[]{:S(2)}, u32[]{:S(2)}) async-start(bf16[4,144,256]{2,1,0:T(8,128)(2,1)} %copy-done.2), calls=%async_computation.3 | async-start | bytes 589824 | tf_op jit(solution)/shard_map/all_to_all | solution.py:232
  67.5 6.7 %collective-permute-start.2 = (bf16[144,256]{1,0:T(8,128)(2,1)S(1)}, bf16[144,256]{1,0:T(8,128)(2,1)S(1)}, u32[]{:S(2)}, u32[]{:S(2)}) collective-permute-start(bf16[144,256]{1,0:T(8,128)(2,1)S(1)} %get-tuple-element.16), channel_id=1, source_target_pairs={{0,256},{256,0},{1,257},{257,1},{2,258},{258,2},{3,259},{259,3},{4... | collective-permute-start | bytes 221192 | tf_op jit(solution)/shard_map/ppermute | solution.py:229
  74.2 5.5 %collective-permute-done.2.back = bf16[144,256]{1,0:T(8,128)(2,1)S(1)} collective-permute-done((bf16[144,256]{1,0:T(8,128)(2,1)S(1)}, bf16[144,256]{1,0:T(8,128)(2,1)S(1)}, u32[]{:S(2)}, u32[]{:S(2)}) %collective-permute-start.2) | collective-permute-done | bytes 73760 | tf_op jit(solution)/shard_map/ppermute | solution.py:229
  79.8 0.0 all-to-all-done.3.got
  79.8 0.8 merge_all.1
  (9 shorter events, 0.0 us)
Async XLA Ops:
  0.0 15.1 %collective-permute-start = (bf16[256,128]{1,0:T(8,128)(2,1)}, bf16[256,128]{1,0:T(8,128)(2,1)S(1)}, u32[]{:S(2)}, u32[]{:S(2)}) collective-permute-start(bf16[256,128]{1,0:T(8,128)(2,1)} %bitcast.7), channel_id=1, source_target_pairs={{0,256},{256,0},{1,257},{257,1},{2,258},{258,2},{3,259},{259,3},{4... | collective-permute-start | bytes 196616 | tf_op jit(solution)/shard_map/ppermute | solution.py:229
  9.7 1.0 %copy-start.3 = (bf16[1,2048,128]{2,1,0:T(8,128)(2,1)S(1)}, bf16[1,2048,128]{2,1,0:T(8,128)(2,1)}, u32[]{:S(2)}) copy-start(bf16[1,2048,128]{2,1,0:T(8,128)(2,1)} %refs_0_.1) | copy-start | bytes 1572868
  10.8 1.0 %copy-start.4 = (bf16[1,2048,128]{2,1,0:T(8,128)(2,1)S(1)}, bf16[1,2048,128]{2,1,0:T(8,128)(2,1)}, u32[]{:S(2)}) copy-start(bf16[1,2048,128]{2,1,0:T(8,128)(2,1)} %refs_1_.1) | copy-start | bytes 1572868
  11.8 0.7 copy-start.10
  12.5 0.7 copy-start.11
  13.2 0.7 copy-start.15
  15.1 8.2 %copy-start.9 = (bf16[16,1,16,128]{3,2,1,0:T(8,128)(2,1)S(1)}, bf16[16,1,16,128]{3,2,1,0:T(8,128)(2,1)}, u32[]{:S(2)}) copy-start(bf16[16,1,16,128]{3,2,1,0:T(8,128)(2,1)} %param.8) | copy-start | bytes 196612
  15.1 0.7 copy-start.7
  15.8 7.5 %collective-permute-start.1 = (bf16[6176,128]{1,0:T(8,128)(2,1)S(1)}, bf16[6176,128]{1,0:T(8,128)(2,1)S(1)}, u32[]{:S(2)}, u32[]{:S(2)}) collective-permute-start(bf16[6176,128]{1,0:T(8,128)(2,1)S(1)} %get-tuple-element.11.own), channel_id=1, source_target_pairs={{0,32},{32,0},{1,33},{33,1},{2,34},{34,2},{3,35},{35,3},{4,36},{36... | collective-permute-start | bytes 4743176 | tf_op jit(solution)/shard_map/ppermute | solution.py:229
  17.7 12.0 %all-to-all-start = ((bf16[4,256,128]{2,1,0:T(8,128)(2,1)}), bf16[4,256,128]{2,1,0:T(8,128)(2,1)S(1)}, u32[]{:S(2)}, u32[]{:S(2)}) async-start(bf16[4,256,128]{2,1,0:T(8,128)(2,1)} %copy-done.7), calls=%async_computation | async-start | bytes 524288 | tf_op jit(solution)/shard_map/all_to_all | solution.py:232
  23.3 0.7 copy-start.12
  27.4 0.7 copy-start.8
  28.1 0.6 copy-start.16
  29.8 17.4 %all-to-all-start.2 = ((bf16[4,256,128]{2,1,0:T(8,128)(2,1)}), bf16[4,256,128]{2,1,0:T(8,128)(2,1)}, u32[]{:S(2)}, u32[]{:S(2)}) async-start(bf16[4,256,128]{2,1,0:T(8,128)(2,1)} %copy-done.8), calls=%async_computation.2 | async-start | bytes 524288 | tf_op jit(solution)/shard_map/all_to_all | solution.py:232
  36.8 0.7 copy-start.13
  37.5 0.9 %copy-start.17 = (bf16[144,256]{1,0:T(8,128)(2,1)S(1)}, bf16[144,256]{1,0:T(8,128)(2,1)}, u32[]{:S(2)}) copy-start(bf16[144,256]{1,0:T(8,128)(2,1)} %copy-done.16) | copy-start | bytes 221188
  38.4 13.9 %copy-start.14 = (s32[4,2]{0,1:T(2,128)S(1)}, s32[4,2]{0,1:T(2,128)}, u32[]{:S(2)}) copy-start(s32[4,2]{0,1:T(2,128)} %param.13) | copy-start | bytes 100
  46.5 0.7 copy-start.5
  47.2 13.5 %all-to-all-start.1 = ((bf16[4,144,256]{2,1,0:T(8,128)(2,1)}), bf16[4,144,256]{2,1,0:T(8,128)(2,1)S(1)}, u32[]{:S(2)}, u32[]{:S(2)}) async-start(bf16[4,144,256]{2,1,0:T(8,128)(2,1)} %copy-done.5), calls=%async_computation.1 | async-start | bytes 589824 | tf_op jit(solution)/shard_map/all_to_all | solution.py:232
  52.3 1.0 %copy-start.6 = (bf16[4,144,256]{2,1,0:T(8,128)(2,1)S(1)}, bf16[4,144,256]{2,1,0:T(8,128)(2,1)}, u32[]{:S(2)}) copy-start(bf16[4,144,256]{2,1,0:T(8,128)(2,1)} %copy-done.5) | copy-start | bytes 884740
  60.0 0.7 copy-start
  60.7 1.0 %copy-start.1 = (bf16[4,144,256]{2,1,0:T(8,128)(2,1)S(1)}, bf16[4,144,256]{2,1,0:T(8,128)(2,1)}, u32[]{:S(2)}) copy-start(bf16[4,144,256]{2,1,0:T(8,128)(2,1)} %copy-done) | copy-start | bytes 884740
  61.7 0.7 copy-start.2
  62.5 17.3 %all-to-all-start.3 = ((bf16[4,144,256]{2,1,0:T(8,128)(2,1)}), bf16[4,144,256]{2,1,0:T(8,128)(2,1)S(1)}, u32[]{:S(2)}, u32[]{:S(2)}) async-start(bf16[4,144,256]{2,1,0:T(8,128)(2,1)} %copy-done.2), calls=%async_computation.3 | async-start | bytes 589824 | tf_op jit(solution)/shard_map/all_to_all | solution.py:232
  67.5 12.2 %collective-permute-start.2 = (bf16[144,256]{1,0:T(8,128)(2,1)S(1)}, bf16[144,256]{1,0:T(8,128)(2,1)S(1)}, u32[]{:S(2)}, u32[]{:S(2)}) collective-permute-start(bf16[144,256]{1,0:T(8,128)(2,1)S(1)} %get-tuple-element.16), channel_id=1, source_target_pairs={{0,256},{256,0},{1,257},{257,1},{2,258},{258,2},{3,259},{259,3},{4... | collective-permute-start | bytes 221192 | tf_op jit(solution)/shard_map/ppermute | solution.py:229

commit v6 on v2

--- a/solution.py
+++ b/solution.py
@@ -12,7 +12,7 @@
 F32 = jnp.float32
 BF16 = jnp.bfloat16
 HIDDEN = -1e30
-CHUNK = 512
+CHUNK = 1024
 TILE = 128
 WIDE = 512
 EXTRA = 16

time: 73.3 us -> 73 us (level)
  no operation moved by 1% of the time
where the time goes in v6:
time: 73 us; the launch traced here: 72.4 us
  starting transfers between devices  40.2 us (55%)
  Pallas kernels  18.4 us (25%)
  waiting for transfers between devices  8.97 us (12%)
  local copies, waits for them, and re-layouts  4.11 us (6%)
  between operations  0.73 us (1%)
    all_to_all x4, starting transfers between devices, quad(): return lax.all_to_all(x, 'near', split_axis=0, concat_axis=0, tiled=True)  22.2 us
    ppermute x3, starting transfers between devices, across(): return lax.ppermute(x, axis, [(0, 1), (1, 0)])  18 us
    pallas_call x2, Pallas kernels, attend(): pl.pallas_call(functools.partial(attend_kernel, where, away, cache_dev, n...  15.3 us
    ppermute x3, waiting for transfers between devices, across(): return lax.ppermute(x, axis, [(0, 1), (1, 0)])  5.35 us
    unnamed x14, local copies, waits for them, and re-layouts  4.11 us
    all_to_all x4, waiting for transfers between devices, quad(): return lax.all_to_all(x, 'near', split_axis=0, concat_axis=0, tiled=True)  3.62 us
  transfers between devices with their start and end apart: 7, of which 2 were waited for; matrix products, arithmetic and copies ran while one was open for 0% of the time, Pallas kernels for 23%

profile of v6, /device:TPU:76, one launch (start us, length us, event | category | flops | bytes accessed | tf_op | source)
XLA Modules:
  0.0 72.4 jit_solution(12290389646153290928)
XLA Ops:
  0.0 9.1 %collective-permute-start.1 = (bf16[256,128]{1,0:T(8,128)(2,1)}, bf16[256,128]{1,0:T(8,128)(2,1)S(1)}, u32[]{:S(2)}, u32[]{:S(2)}) collective-permute-start(bf16[256,128]{1,0:T(8,128)(2,1)} %bitcast.7), channel_id=1, source_target_pairs={{0,256},{256,0},{1,257},{257,1},{2,258},{258,2},{3,259},{259,3},{4... | collective-permute-start | bytes 196616 | tf_op jit(solution)/shard_map/ppermute | solution.py:211
  9.7 0.0 copy-start
  9.7 1.0 %copy-done = bf16[1,2048,128]{2,1,0:T(8,128)(2,1)S(1)} copy-done((bf16[1,2048,128]{2,1,0:T(8,128)(2,1)S(1)}, bf16[1,2048,128]{2,1,0:T(8,128)(2,1)}, u32[]{:S(2)}) %copy-start) | copy-done | bytes 524312
  10.8 0.0 copy-start.1
  10.8 1.0 %copy-done.1 = bf16[1,2048,128]{2,1,0:T(8,128)(2,1)S(1)} copy-done((bf16[1,2048,128]{2,1,0:T(8,128)(2,1)S(1)}, bf16[1,2048,128]{2,1,0:T(8,128)(2,1)}, u32[]{:S(2)}) %copy-start.1) | copy-done | bytes 524312
  11.8 0.0 copy-start.3
  11.8 0.7 copy-done.3
  12.5 0.0 copy-start.4
  12.5 0.7 copy-done.4
  13.2 0.0 copy-start.5
  13.2 0.7 copy-done.5
  13.9 0.0 copy-start.2
  13.9 1.4 %pack.1._.own = bf16[4512,128]{1,0:T(8,128)(2,1)S(1)} custom-call(bf16[1,2048,128]{2,1,0:T(8,128)(2,1)S(1)} %copy-done, bf16[1,2048,128]{2,1,0:T(8,128)(2,1)S(1)} %copy-done.1, bf16[16,128]{1,0:T(8,128)(2,1)S(1)} %bitcast.9, bf16[16,128]{1,0:T(8,128)(2,1)S(1)} %bitcast.10, s32[16]{0:T(128)S(1)} %copy-done.5, s32[1]{0:T(128)S(6)} %copy.12.refs_5_), custom_call_target="tpu_custom_call" | custom-call | tf_op jit(solution)/shard_map/pack/pallas_call | solution.py:225
  15.2 0.0 copy-start.6
  15.2 0.0 collective-permute-done.1.q_far
  15.3 0.0 copy-done.2
  15.3 0.9 %spread.1 = (bf16[4,256,128]{2,1,0:T(8,128)(2,1)}, bf16[4,256,128]{2,1,0:T(8,128)(2,1)}) custom-call(bf16[256,128]{1,0:T(8,128)(2,1)S(1)} %bitcast.8, bf16[256,128]{1,0:T(8,128)(2,1)S(1)} %collective-permute-done.1.q_far, bf16[4512,128]{1,0:T(8,128)(2,1)S(1)} %pack.1._.own), custom_call_target="tpu_custom_call" | custom-call | tf_op jit(solution)/shard_map/spread/pallas_call | solution.py:242
  16.1 5.5 %all-to-all-start = ((bf16[4,256,128]{2,1,0:T(8,128)(2,1)}), bf16[4,256,128]{2,1,0:T(8,128)(2,1)S(1)}, u32[]{:S(2)}, u32[]{:S(2)}) async-start(bf16[4,256,128]{2,1,0:T(8,128)(2,1)} %get-tuple-element.9), calls=%async_computation | async-start | bytes 524288 | tf_op jit(solution)/shard_map/all_to_all | solution.py:214
  21.7 1.9 %collective-permute-start = (bf16[4512,128]{1,0:T(8,128)(2,1)S(1)}, bf16[4512,128]{1,0:T(8,128)(2,1)S(1)}, u32[]{:S(2)}, u32[]{:S(2)}) collective-permute-start(bf16[4512,128]{1,0:T(8,128)(2,1)S(1)} %pack.1._.own), channel_id=1, source_target_pairs={{0,32},{32,0},{1,33},{33,1},{2,34},{34,2},{3,35},{35,3},{4,36},{36... | collective-permute-start | bytes 3465224 | tf_op jit(solution)/shard_map/ppermute | solution.py:211
  23.6 3.6 %all-to-all-done.q_ref = bf16[4,256,128]{2,1,0:T(8,128)(2,1)S(1)} async-done(((bf16[4,256,128]{2,1,0:T(8,128)(2,1)}), bf16[4,256,128]{2,1,0:T(8,128)(2,1)S(1)}, u32[]{:S(2)}, u32[]{:S(2)}) %all-to-all-start) | async-done | bytes 262176 | tf_op jit(solution)/shard_map/all_to_all | solution.py:214
  27.2 6.4 %all-to-all-start.2 = ((bf16[4,256,128]{2,1,0:T(8,128)(2,1)}), bf16[4,256,128]{2,1,0:T(8,128)(2,1)S(1)}, u32[]{:S(2)}, u32[]{:S(2)}) async-start(bf16[4,256,128]{2,1,0:T(8,128)(2,1)} %get-tuple-element.10), calls=%async_computation.2 | async-start | bytes 524288 | tf_op jit(solution)/shard_map/all_to_all | solution.py:214
  33.7 0.0 collective-permute-done.other
  33.7 0.0 copy-done.6
  33.7 7.6 %far_blocks.1 = bf16[4,144,256]{2,1,0:T(8,128)(2,1)} custom-call(s32[2,4]{1,0:T(2,128)S(1)} %bitcast.11, bf16[4512,128]{1,0:T(8,128)(2,1)S(1)} %pack.1._.own, bf16[4512,128]{1,0:T(8,128)(2,1)S(1)} %collective-permute-done.other, bf16[4,256,128]{2,1,0:T(8,128)(2,1)S(1)} %all-to-all-done.q_ref), custom_call_target="tpu_custom_call" | custom-call | flops 2147483648 | bytes 4194304 | tf_op jit(solution)/shard_map/far_blocks/pallas_call | solution.py:262
  41.3 0.0 all-to-all-done.2.q_ref
  41.3 5.1 %all-to-all-start.1 = ((bf16[4,144,256]{2,1,0:T(8,128)(2,1)}), bf16[4,144,256]{2,1,0:T(8,128)(2,1)S(1)}, u32[]{:S(2)}, u32[]{:S(2)}) async-start(bf16[4,144,256]{2,1,0:T(8,128)(2,1)} %far_blocks.1), calls=%async_computation.1 | async-start | bytes 589824 | tf_op jit(solution)/shard_map/all_to_all | solution.py:214
  46.4 7.6 %near_blocks.1._ = bf16[4,144,256]{2,1,0:T(8,128)(2,1)} custom-call(s32[2,4]{1,0:T(2,128)S(1)} %bitcast.12, bf16[4512,128]{1,0:T(8,128)(2,1)S(1)} %pack.1._.own, bf16[4512,128]{1,0:T(8,128)(2,1)S(1)} %collective-permute-done.other, bf16[4,256,128]{2,1,0:T(8,128)(2,1)S(1)} %all-to-all-done.2.q_ref), custom_call_target="tpu_custom_call" | custom-call | flops 2147483648 | bytes 4194304 | tf_op jit(solution)/shard_map/near_blocks/pallas_call | solution.py:262
  54.0 0.0 all-to-all-done.1.got
  54.0 0.1 merge_far.1
  54.1 5.1 %all-to-all-start.3 = ((bf16[4,144,256]{2,1,0:T(8,128)(2,1)}), bf16[4,144,256]{2,1,0:T(8,128)(2,1)S(1)}, u32[]{:S(2)}, u32[]{:S(2)}) async-start(bf16[4,144,256]{2,1,0:T(8,128)(2,1)} %get-tuple-element.11), calls=%async_computation.3 | async-start | bytes 589824 | tf_op jit(solution)/shard_map/all_to_all | solution.py:214
  59.2 7.0 %collective-permute-start.2 = (bf16[144,256]{1,0:T(8,128)(2,1)S(1)}, bf16[144,256]{1,0:T(8,128)(2,1)S(1)}, u32[]{:S(2)}, u32[]{:S(2)}) collective-permute-start(bf16[144,256]{1,0:T(8,128)(2,1)S(1)} %get-tuple-element.12), channel_id=1, source_target_pairs={{0,256},{256,0},{1,257},{257,1},{2,258},{258,2},{3,259},{259,3},{4... | collective-permute-start | bytes 221192 | tf_op jit(solution)/shard_map/ppermute | solution.py:211
  66.2 5.3 %collective-permute-done.2.back = bf16[144,256]{1,0:T(8,128)(2,1)S(1)} collective-permute-done((bf16[144,256]{1,0:T(8,128)(2,1)S(1)}, bf16[144,256]{1,0:T(8,128)(2,1)S(1)}, u32[]{:S(2)}, u32[]{:S(2)}) %collective-permute-start.2) | collective-permute-done | bytes 73760 | tf_op jit(solution)/shard_map/ppermute | solution.py:211
  71.6 0.0 all-to-all-done.3.got
  71.6 0.8 %merge_all.1 = bf16[256,128]{1,0:T(8,128)(2,1)} custom-call(bf16[4,144,256]{2,1,0:T(8,128)(2,1)S(1)} %all-to-all-done.3.got, bf16[144,256]{1,0:T(8,128)(2,1)S(1)} %collective-permute-done.2.back), custom_call_target="tpu_custom_call" | custom-call | tf_op jit(solution)/shard_map/merge_all/pallas_call | solution.py:289
Async XLA Ops:
  0.0 15.3 %collective-permute-start.1 = (bf16[256,128]{1,0:T(8,128)(2,1)}, bf16[256,128]{1,0:T(8,128)(2,1)S(1)}, u32[]{:S(2)}, u32[]{:S(2)}) collective-permute-start(bf16[256,128]{1,0:T(8,128)(2,1)} %bitcast.7), channel_id=1, source_target_pairs={{0,256},{256,0},{1,257},{257,1},{2,258},{258,2},{3,259},{259,3},{4... | collective-permute-start | bytes 196616 | tf_op jit(solution)/shard_map/ppermute | solution.py:211
  9.7 1.0 %copy-start = (bf16[1,2048,128]{2,1,0:T(8,128)(2,1)S(1)}, bf16[1,2048,128]{2,1,0:T(8,128)(2,1)}, u32[]{:S(2)}) copy-start(bf16[1,2048,128]{2,1,0:T(8,128)(2,1)} %refs_0_.1) | copy-start | bytes 1572868
  10.8 1.0 %copy-start.1 = (bf16[1,2048,128]{2,1,0:T(8,128)(2,1)S(1)}, bf16[1,2048,128]{2,1,0:T(8,128)(2,1)}, u32[]{:S(2)}) copy-start(bf16[1,2048,128]{2,1,0:T(8,128)(2,1)} %refs_1_.1) | copy-start | bytes 1572868
  11.8 0.7 copy-start.3
  12.5 0.7 copy-start.4
  13.2 0.7 copy-start.5
  13.9 1.4 %copy-start.2 = (bf16[16,1,16,128]{3,2,1,0:T(8,128)(2,1)S(1)}, bf16[16,1,16,128]{3,2,1,0:T(8,128)(2,1)}, u32[]{:S(2)}) copy-start(bf16[16,1,16,128]{3,2,1,0:T(8,128)(2,1)} %param.8) | copy-start | bytes 196612
  15.2 18.4 %copy-start.6 = (s32[4,2]{0,1:T(2,128)S(1)}, s32[4,2]{0,1:T(2,128)}, u32[]{:S(2)}) copy-start(s32[4,2]{0,1:T(2,128)} %param.13) | copy-start | bytes 100
  16.1 11.1 %all-to-all-start = ((bf16[4,256,128]{2,1,0:T(8,128)(2,1)}), bf16[4,256,128]{2,1,0:T(8,128)(2,1)S(1)}, u32[]{:S(2)}, u32[]{:S(2)}) async-start(bf16[4,256,128]{2,1,0:T(8,128)(2,1)} %get-tuple-element.9), calls=%async_computation | async-start | bytes 524288 | tf_op jit(solution)/shard_map/all_to_all | solution.py:214
  21.7 12.0 %collective-permute-start = (bf16[4512,128]{1,0:T(8,128)(2,1)S(1)}, bf16[4512,128]{1,0:T(8,128)(2,1)S(1)}, u32[]{:S(2)}, u32[]{:S(2)}) collective-permute-start(bf16[4512,128]{1,0:T(8,128)(2,1)S(1)} %pack.1._.own), channel_id=1, source_target_pairs={{0,32},{32,0},{1,33},{33,1},{2,34},{34,2},{3,35},{35,3},{4,36},{36... | collective-permute-start | bytes 3465224 | tf_op jit(solution)/shard_map/ppermute | solution.py:211
  27.2 14.1 %all-to-all-start.2 = ((bf16[4,256,128]{2,1,0:T(8,128)(2,1)}), bf16[4,256,128]{2,1,0:T(8,128)(2,1)S(1)}, u32[]{:S(2)}, u32[]{:S(2)}) async-start(bf16[4,256,128]{2,1,0:T(8,128)(2,1)} %get-tuple-element.10), calls=%async_computation.2 | async-start | bytes 524288 | tf_op jit(solution)/shard_map/all_to_all | solution.py:214
  41.3 12.7 %all-to-all-start.1 = ((bf16[4,144,256]{2,1,0:T(8,128)(2,1)}), bf16[4,144,256]{2,1,0:T(8,128)(2,1)S(1)}, u32[]{:S(2)}, u32[]{:S(2)}) async-start(bf16[4,144,256]{2,1,0:T(8,128)(2,1)} %far_blocks.1), calls=%async_computation.1 | async-start | bytes 589824 | tf_op jit(solution)/shard_map/all_to_all | solution.py:214
  54.1 17.5 %all-to-all-start.3 = ((bf16[4,144,256]{2,1,0:T(8,128)(2,1)}), bf16[4,144,256]{2,1,0:T(8,128)(2,1)S(1)}, u32[]{:S(2)}, u32[]{:S(2)}) async-start(bf16[4,144,256]{2,1,0:T(8,128)(2,1)} %get-tuple-element.11), calls=%async_computation.3 | async-start | bytes 589824 | tf_op jit(solution)/shard_map/all_to_all | solution.py:214
  59.2 12.4 %collective-permute-start.2 = (bf16[144,256]{1,0:T(8,128)(2,1)S(1)}, bf16[144,256]{1,0:T(8,128)(2,1)S(1)}, u32[]{:S(2)}, u32[]{:S(2)}) collective-permute-start(bf16[144,256]{1,0:T(8,128)(2,1)S(1)} %get-tuple-element.12), channel_id=1, source_target_pairs={{0,256},{256,0},{1,257},{257,1},{2,258},{258,2},{3,259},{259,3},{4... | collective-permute-start | bytes 221192 | tf_op jit(solution)/shard_map/ppermute | solution.py:211

commit v7 on v6

--- a/solution.py
+++ b/solution.py
@@ -181,10 +181,9 @@
             write_message(out.at[pair * b + j], acc[0:dim, cut], top[:, cut] * scale2, acc[dim : dim + 1, cut])
 
 
-def spread_kernel(q, q_far, _, near_out, far_out):
-    for j in range(near_out.shape[0]):
-        near_out[j] = q[...]
-        far_out[j] = q_far[...]
+def spread_kernel(q, _, out):
+    for j in range(out.shape[0]):
+        out[j] = q[...]
 
 
 def merge_kernel(got, _, out, kept):
@@ -238,15 +237,18 @@
         compiler_params=params,
         name="pack",
     )(cache_k, cache_v, new_keys.reshape(new, dim), new_values.reshape(new, dim), cache_len, doc_start)
-    slots = jax.ShapeDtypeStruct((near, rows, dim), BF16)
-    q_near, q_far = pl.pallas_call(
-        spread_kernel,
-        out_shape=[slots] * 2,
-        in_specs=[vmem, vmem, pl.BlockSpec(memory_space=pl.ANY)],
-        out_specs=[vmem] * 2,
-        compiler_params=params,
-        name="spread",
-    )(q, q_far, own)
+    def spread(block, before, name):
+        return pl.pallas_call(
+            spread_kernel,
+            out_shape=jax.ShapeDtypeStruct((near, rows, dim), BF16),
+            in_specs=[vmem, pl.BlockSpec(memory_space=pl.ANY)],
+            out_specs=vmem,
+            compiler_params=params,
+            name=name,
+        )(block, before)
+
+    q_far = spread(q_far, own, "spread_far")
+    q_near = spread(q, q_far, "spread_near")
     q_far = quad(q_far)
     other = across(own, "core")
     q_near = quad(q_near)

time: 73 us -> 73.1 us (level)
  the two profiles are of different devices: /device:TPU:76 before, /device:TPU:90 now
where the time goes in v7:
time: 73.1 us; the launch traced here: 72.4 us
  starting transfers between devices  40.3 us (55%)
  Pallas kernels  19 us (26%)
  waiting for transfers between devices  8.23 us (11%)
  local copies, waits for them, and re-layouts  4.11 us (6%)
    all_to_all x4, starting transfers between devices, quad(): return lax.all_to_all(x, 'near', split_axis=0, concat_axis=0, tiled=True)  22.3 us
    ppermute x3, starting transfers between devices, across(): return lax.ppermute(x, axis, [(0, 1), (1, 0)])  18 us
    pallas_call x2, Pallas kernels, attend(): pl.pallas_call(functools.partial(attend_kernel, where, away, cache_dev, n...  15.3 us
    ppermute x3, waiting for transfers between devices, across(): return lax.ppermute(x, axis, [(0, 1), (1, 0)])  5.35 us
    unnamed x14, local copies, waits for them, and re-layouts  4.11 us
    all_to_all x4, waiting for transfers between devices, quad(): return lax.all_to_all(x, 'near', split_axis=0, concat_axis=0, tiled=True)  2.88 us
    pallas_call x2, Pallas kernels, spread(): pl.pallas_call(spread_kernel, out_shape=jax.ShapeDtypeStruct((near, rows,...  1.47 us
  transfers between devices with their start and end apart: 7, of which 2 were waited for; matrix products, arithmetic and copies ran while one was open for 0% of the time, Pallas kernels for 24%

profile of v7, /device:TPU:90, one launch (start us, length us, event | category | flops | bytes accessed | tf_op | source)
XLA Modules:
  0.0 72.4 jit_solution(11017521670349812799)
XLA Ops:
  0.0 9.1 %collective-permute-start.1 = (bf16[256,128]{1,0:T(8,128)(2,1)}, bf16[256,128]{1,0:T(8,128)(2,1)S(1)}, u32[]{:S(2)}, u32[]{:S(2)}) collective-permute-start(bf16[256,128]{1,0:T(8,128)(2,1)} %bitcast.7), channel_id=1, source_target_pairs={{0,256},{256,0},{1,257},{257,1},{2,258},{258,2},{3,259},{259,3},{4... | collective-permute-start | bytes 196616 | tf_op jit(solution)/shard_map/ppermute | solution.py:210
  9.7 0.0 copy-start
  9.8 1.0 %copy-done = bf16[1,2048,128]{2,1,0:T(8,128)(2,1)S(1)} copy-done((bf16[1,2048,128]{2,1,0:T(8,128)(2,1)S(1)}, bf16[1,2048,128]{2,1,0:T(8,128)(2,1)}, u32[]{:S(2)}) %copy-start) | copy-done | bytes 524312
  10.8 0.0 copy-start.1
  10.8 1.0 %copy-done.1 = bf16[1,2048,128]{2,1,0:T(8,128)(2,1)S(1)} copy-done((bf16[1,2048,128]{2,1,0:T(8,128)(2,1)S(1)}, bf16[1,2048,128]{2,1,0:T(8,128)(2,1)}, u32[]{:S(2)}) %copy-start.1) | copy-done | bytes 524312
  11.8 0.0 copy-start.3
  11.8 0.7 copy-done.3
  12.5 0.0 copy-start.4
  12.5 0.7 copy-done.4
  13.2 0.0 copy-start.5
  13.2 0.7 copy-done.5
  13.9 1.4 %pack.1._.own = bf16[4512,128]{1,0:T(8,128)(2,1)S(1)} custom-call(bf16[1,2048,128]{2,1,0:T(8,128)(2,1)S(1)} %copy-done, bf16[1,2048,128]{2,1,0:T(8,128)(2,1)S(1)} %copy-done.1, bf16[16,128]{1,0:T(8,128)(2,1)S(1)} %bitcast.9, bf16[16,128]{1,0:T(8,128)(2,1)S(1)} %bitcast.10, s32[16]{0:T(128)S(1)} %copy-done.5, s32[1]{0:T(128)S(6)} %copy.12.refs_5_), custom_call_target="tpu_custom_call" | custom-call | tf_op jit(solution)/shard_map/pack/pallas_call | solution.py:224
  15.2 0.0 copy-start.2
  15.2 0.0 collective-permute-done.1.q
  15.3 0.7 %spread_far.1._ = bf16[4,256,128]{2,1,0:T(8,128)(2,1)} custom-call(bf16[256,128]{1,0:T(8,128)(2,1)S(1)} %collective-permute-done.1.q, bf16[4512,128]{1,0:T(8,128)(2,1)S(1)} %pack.1._.own), custom_call_target="tpu_custom_call" | custom-call | tf_op jit(solution)/shard_map/spread_far/pallas_call | solution.py:241
  16.0 0.0 copy-start.6
  16.0 5.7 %all-to-all-start = ((bf16[4,256,128]{2,1,0:T(8,128)(2,1)}), bf16[4,256,128]{2,1,0:T(8,128)(2,1)S(1)}, u32[]{:S(2)}, u32[]{:S(2)}) async-start(bf16[4,256,128]{2,1,0:T(8,128)(2,1)} %spread_far.1._), calls=%async_computation | async-start | bytes 524288 | tf_op jit(solution)/shard_map/all_to_all | solution.py:213
  21.7 1.9 %collective-permute-start = (bf16[4512,128]{1,0:T(8,128)(2,1)S(1)}, bf16[4512,128]{1,0:T(8,128)(2,1)S(1)}, u32[]{:S(2)}, u32[]{:S(2)}) collective-permute-start(bf16[4512,128]{1,0:T(8,128)(2,1)S(1)} %pack.1._.own), channel_id=1, source_target_pairs={{0,32},{32,0},{1,33},{33,1},{2,34},{34,2},{3,35},{35,3},{4,36},{36... | collective-permute-start | bytes 3465224 | tf_op jit(solution)/shard_map/ppermute | solution.py:210
  23.6 0.0 copy-done.2
  23.6 0.7 %spread_near.1 = bf16[4,256,128]{2,1,0:T(8,128)(2,1)} custom-call(bf16[256,128]{1,0:T(8,128)(2,1)S(1)} %bitcast.8, bf16[4,256,128]{2,1,0:T(8,128)(2,1)} %spread_far.1._), custom_call_target="tpu_custom_call" | custom-call | tf_op jit(solution)/shard_map/spread_near/pallas_call | solution.py:241
  24.3 2.9 %all-to-all-done.q_ref = bf16[4,256,128]{2,1,0:T(8,128)(2,1)S(1)} async-done(((bf16[4,256,128]{2,1,0:T(8,128)(2,1)}), bf16[4,256,128]{2,1,0:T(8,128)(2,1)S(1)}, u32[]{:S(2)}, u32[]{:S(2)}) %all-to-all-start) | async-done | bytes 262176 | tf_op jit(solution)/shard_map/all_to_all | solution.py:213
  27.2 6.4 %all-to-all-start.2 = ((bf16[4,256,128]{2,1,0:T(8,128)(2,1)}), bf16[4,256,128]{2,1,0:T(8,128)(2,1)S(1)}, u32[]{:S(2)}, u32[]{:S(2)}) async-start(bf16[4,256,128]{2,1,0:T(8,128)(2,1)} %spread_near.1), calls=%async_computation.2 | async-start | bytes 524288 | tf_op jit(solution)/shard_map/all_to_all | solution.py:213
  33.7 0.0 collective-permute-done.other
  33.7 0.0 copy-done.6
  33.7 7.6 %far_blocks.1 = bf16[4,144,256]{2,1,0:T(8,128)(2,1)} custom-call(s32[2,4]{1,0:T(2,128)S(1)} %bitcast.11, bf16[4512,128]{1,0:T(8,128)(2,1)S(1)} %pack.1._.own, bf16[4512,128]{1,0:T(8,128)(2,1)S(1)} %collective-permute-done.other, bf16[4,256,128]{2,1,0:T(8,128)(2,1)S(1)} %all-to-all-done.q_ref), custom_call_target="tpu_custom_call" | custom-call | flops 2147483648 | bytes 4194304 | tf_op jit(solution)/shard_map/far_blocks/pallas_call | solution.py:264
  41.3 0.0 all-to-all-done.2.q_ref
  41.3 5.1 %all-to-all-start.1 = ((bf16[4,144,256]{2,1,0:T(8,128)(2,1)}), bf16[4,144,256]{2,1,0:T(8,128)(2,1)S(1)}, u32[]{:S(2)}, u32[]{:S(2)}) async-start(bf16[4,144,256]{2,1,0:T(8,128)(2,1)} %far_blocks.1), calls=%async_computation.1 | async-start | bytes 589824 | tf_op jit(solution)/shard_map/all_to_all | solution.py:213
  46.4 7.7 %near_blocks.1._ = bf16[4,144,256]{2,1,0:T(8,128)(2,1)} custom-call(s32[2,4]{1,0:T(2,128)S(1)} %bitcast.12, bf16[4512,128]{1,0:T(8,128)(2,1)S(1)} %pack.1._.own, bf16[4512,128]{1,0:T(8,128)(2,1)S(1)} %collective-permute-done.other, bf16[4,256,128]{2,1,0:T(8,128)(2,1)S(1)} %all-to-all-done.2.q_ref), custom_call_target="tpu_custom_call" | custom-call | flops 2147483648 | bytes 4194304 | tf_op jit(solution)/shard_map/near_blocks/pallas_call | solution.py:264
  54.1 0.0 all-to-all-done.1.got
  54.1 0.1 merge_far.1
  54.1 5.1 %all-to-all-start.3 = ((bf16[4,144,256]{2,1,0:T(8,128)(2,1)}), bf16[4,144,256]{2,1,0:T(8,128)(2,1)S(1)}, u32[]{:S(2)}, u32[]{:S(2)}) async-start(bf16[4,144,256]{2,1,0:T(8,128)(2,1)} %get-tuple-element.7), calls=%async_computation.3 | async-start | bytes 589824 | tf_op jit(solution)/shard_map/all_to_all | solution.py:213
  59.2 7.0 %collective-permute-start.2 = (bf16[144,256]{1,0:T(8,128)(2,1)S(1)}, bf16[144,256]{1,0:T(8,128)(2,1)S(1)}, u32[]{:S(2)}, u32[]{:S(2)}) collective-permute-start(bf16[144,256]{1,0:T(8,128)(2,1)S(1)} %get-tuple-element.8), channel_id=1, source_target_pairs={{0,256},{256,0},{1,257},{257,1},{2,258},{258,2},{3,259},{259,3},{4... | collective-permute-start | bytes 221192 | tf_op jit(solution)/shard_map/ppermute | solution.py:210
  66.3 5.3 %collective-permute-done.2.back = bf16[144,256]{1,0:T(8,128)(2,1)S(1)} collective-permute-done((bf16[144,256]{1,0:T(8,128)(2,1)S(1)}, bf16[144,256]{1,0:T(8,128)(2,1)S(1)}, u32[]{:S(2)}, u32[]{:S(2)}) %collective-permute-start.2) | collective-permute-done | bytes 73760 | tf_op jit(solution)/shard_map/ppermute | solution.py:210
  71.6 0.0 all-to-all-done.3.got
  71.6 0.8 %merge_all.1 = bf16[256,128]{1,0:T(8,128)(2,1)} custom-call(bf16[4,144,256]{2,1,0:T(8,128)(2,1)S(1)} %all-to-all-done.3.got, bf16[144,256]{1,0:T(8,128)(2,1)S(1)} %collective-permute-done.2.back), custom_call_target="tpu_custom_call" | custom-call | tf_op jit(solution)/shard_map/merge_all/pallas_call | solution.py:291
Async XLA Ops:
  0.0 15.3 %collective-permute-start.1 = (bf16[256,128]{1,0:T(8,128)(2,1)}, bf16[256,128]{1,0:T(8,128)(2,1)S(1)}, u32[]{:S(2)}, u32[]{:S(2)}) collective-permute-start(bf16[256,128]{1,0:T(8,128)(2,1)} %bitcast.7), channel_id=1, source_target_pairs={{0,256},{256,0},{1,257},{257,1},{2,258},{258,2},{3,259},{259,3},{4... | collective-permute-start | bytes 196616 | tf_op jit(solution)/shard_map/ppermute | solution.py:210
  9.7 1.0 %copy-start = (bf16[1,2048,128]{2,1,0:T(8,128)(2,1)S(1)}, bf16[1,2048,128]{2,1,0:T(8,128)(2,1)}, u32[]{:S(2)}) copy-start(bf16[1,2048,128]{2,1,0:T(8,128)(2,1)} %refs_0_.1) | copy-start | bytes 1572868
  10.8 1.0 %copy-start.1 = (bf16[1,2048,128]{2,1,0:T(8,128)(2,1)S(1)}, bf16[1,2048,128]{2,1,0:T(8,128)(2,1)}, u32[]{:S(2)}) copy-start(bf16[1,2048,128]{2,1,0:T(8,128)(2,1)} %refs_1_.1) | copy-start | bytes 1572868
  11.8 0.7 copy-start.3
  12.5 0.7 copy-start.4
  13.2 0.7 copy-start.5
  15.2 8.4 %copy-start.2 = (bf16[16,1,16,128]{3,2,1,0:T(8,128)(2,1)S(1)}, bf16[16,1,16,128]{3,2,1,0:T(8,128)(2,1)}, u32[]{:S(2)}) copy-start(bf16[16,1,16,128]{3,2,1,0:T(8,128)(2,1)} %param.8) | copy-start | bytes 196612
  16.0 17.7 %copy-start.6 = (s32[4,2]{0,1:T(2,128)S(1)}, s32[4,2]{0,1:T(2,128)}, u32[]{:S(2)}) copy-start(s32[4,2]{0,1:T(2,128)} %param.13) | copy-start | bytes 100
  16.0 11.2 %all-to-all-start = ((bf16[4,256,128]{2,1,0:T(8,128)(2,1)}), bf16[4,256,128]{2,1,0:T(8,128)(2,1)S(1)}, u32[]{:S(2)}, u32[]{:S(2)}) async-start(bf16[4,256,128]{2,1,0:T(8,128)(2,1)} %spread_far.1._), calls=%async_computation | async-start | bytes 524288 | tf_op jit(solution)/shard_map/all_to_all | solution.py:213
  21.7 12.0 %collective-permute-start = (bf16[4512,128]{1,0:T(8,128)(2,1)S(1)}, bf16[4512,128]{1,0:T(8,128)(2,1)S(1)}, u32[]{:S(2)}, u32[]{:S(2)}) collective-permute-start(bf16[4512,128]{1,0:T(8,128)(2,1)S(1)} %pack.1._.own), channel_id=1, source_target_pairs={{0,32},{32,0},{1,33},{33,1},{2,34},{34,2},{3,35},{35,3},{4,36},{36... | collective-permute-start | bytes 3465224 | tf_op jit(solution)/shard_map/ppermute | solution.py:210
  27.2 14.1 %all-to-all-start.2 = ((bf16[4,256,128]{2,1,0:T(8,128)(2,1)}), bf16[4,256,128]{2,1,0:T(8,128)(2,1)S(1)}, u32[]{:S(2)}, u32[]{:S(2)}) async-start(bf16[4,256,128]{2,1,0:T(8,128)(2,1)} %spread_near.1), calls=%async_computation.2 | async-start | bytes 524288 | tf_op jit(solution)/shard_map/all_to_all | solution.py:213
  41.3 12.8 %all-to-all-start.1 = ((bf16[4,144,256]{2,1,0:T(8,128)(2,1)}), bf16[4,144,256]{2,1,0:T(8,128)(2,1)S(1)}, u32[]{:S(2)}, u32[]{:S(2)}) async-start(bf16[4,144,256]{2,1,0:T(8,128)(2,1)} %far_blocks.1), calls=%async_computation.1 | async-start | bytes 589824 | tf_op jit(solution)/shard_map/all_to_all | solution.py:213
  54.1 17.5 %all-to-all-start.3 = ((bf16[4,144,256]{2,1,0:T(8,128)(2,1)}), bf16[4,144,256]{2,1,0:T(8,128)(2,1)S(1)}, u32[]{:S(2)}, u32[]{:S(2)}) async-start(bf16[4,144,256]{2,1,0:T(8,128)(2,1)} %get-tuple-element.7), calls=%async_computation.3 | async-start | bytes 589824 | tf_op jit(solution)/shard_map/all_to_all | solution.py:213
  59.2 12.4 %collective-permute-start.2 = (bf16[144,256]{1,0:T(8,128)(2,1)S(1)}, bf16[144,256]{1,0:T(8,128)(2,1)S(1)}, u32[]{:S(2)}, u32[]{:S(2)}) collective-permute-start(bf16[144,256]{1,0:T(8,128)(2,1)S(1)} %get-tuple-element.8), channel_id=1, source_target_pairs={{0,256},{256,0},{1,257},{257,1},{2,258},{258,2},{3,259},{259,3},{4... | collective-permute-start | bytes 221192 | tf_op jit(solution)/shard_map/ppermute | solution.py:210

commit v8 on v7

--- a/solution.py
+++ b/solution.py
@@ -12,7 +12,7 @@
 F32 = jnp.float32
 BF16 = jnp.bfloat16
 HIDDEN = -1e30
-CHUNK = 1024
+CHUNK = 2048
 TILE = 128
 WIDE = 512
 EXTRA = 16

time: 73.1 us -> 73 us (level)
  the two profiles are of different devices: /device:TPU:90 before, /device:TPU:94 now
where the time goes in v8:
time: 73 us; the launch traced here: 72.3 us
  starting transfers between devices  40.3 us (55%)
  Pallas kernels  18.9 us (26%)
  waiting for transfers between devices  8.23 us (11%)
  local copies, waits for them, and re-layouts  4.11 us (6%)
  between operations  0.73 us (1%)
    all_to_all x4, starting transfers between devices, quad(): return lax.all_to_all(x, 'near', split_axis=0, concat_axis=0, tiled=True)  22.3 us
    ppermute x3, starting transfers between devices, across(): return lax.ppermute(x, axis, [(0, 1), (1, 0)])  18 us
    pallas_call x2, Pallas kernels, attend(): pl.pallas_call(functools.partial(attend_kernel, where, away, cache_dev, n...  15.2 us
    ppermute x3, waiting for transfers between devices, across(): return lax.ppermute(x, axis, [(0, 1), (1, 0)])  5.35 us
    unnamed x14, local copies, waits for them, and re-layouts  4.11 us
    all_to_all x4, waiting for transfers between devices, quad(): return lax.all_to_all(x, 'near', split_axis=0, concat_axis=0, tiled=True)  2.88 us
    pallas_call x2, Pallas kernels, spread(): pl.pallas_call(spread_kernel, out_shape=jax.ShapeDtypeStruct((near, rows,...  1.47 us
  transfers between devices with their start and end apart: 7, of which 2 were waited for; matrix products, arithmetic and copies ran while one was open for 0% of the time, Pallas kernels for 24%

profile of v8, /device:TPU:94, one launch (start us, length us, event | category | flops | bytes accessed | tf_op | source)
XLA Modules:
  0.0 72.3 jit_solution(4507948979604691411)
XLA Ops:
  0.0 9.1 %collective-permute-start.1 = (bf16[256,128]{1,0:T(8,128)(2,1)}, bf16[256,128]{1,0:T(8,128)(2,1)S(1)}, u32[]{:S(2)}, u32[]{:S(2)}) collective-permute-start(bf16[256,128]{1,0:T(8,128)(2,1)} %bitcast.7), channel_id=1, source_target_pairs={{0,256},{256,0},{1,257},{257,1},{2,258},{258,2},{3,259},{259,3},{4... | collective-permute-start | bytes 196616 | tf_op jit(solution)/shard_map/ppermute | solution.py:210
  9.7 0.0 copy-start
  9.8 1.0 %copy-done = bf16[1,2048,128]{2,1,0:T(8,128)(2,1)S(1)} copy-done((bf16[1,2048,128]{2,1,0:T(8,128)(2,1)S(1)}, bf16[1,2048,128]{2,1,0:T(8,128)(2,1)}, u32[]{:S(2)}) %copy-start) | copy-done | bytes 524312
  10.8 0.0 copy-start.1
  10.8 1.0 %copy-done.1 = bf16[1,2048,128]{2,1,0:T(8,128)(2,1)S(1)} copy-done((bf16[1,2048,128]{2,1,0:T(8,128)(2,1)S(1)}, bf16[1,2048,128]{2,1,0:T(8,128)(2,1)}, u32[]{:S(2)}) %copy-start.1) | copy-done | bytes 524312
  11.8 0.0 copy-start.3
  11.8 0.7 copy-done.3
  12.5 0.0 copy-start.4
  12.5 0.7 copy-done.4
  13.2 0.0 copy-start.5
  13.2 0.7 copy-done.5
  13.9 1.4 %pack.1._.own = bf16[4512,128]{1,0:T(8,128)(2,1)S(1)} custom-call(bf16[1,2048,128]{2,1,0:T(8,128)(2,1)S(1)} %copy-done, bf16[1,2048,128]{2,1,0:T(8,128)(2,1)S(1)} %copy-done.1, bf16[16,128]{1,0:T(8,128)(2,1)S(1)} %bitcast.9, bf16[16,128]{1,0:T(8,128)(2,1)S(1)} %bitcast.10, s32[16]{0:T(128)S(1)} %copy-done.5, s32[1]{0:T(128)S(6)} %copy.12.refs_5_), custom_call_target="tpu_custom_call" | custom-call | tf_op jit(solution)/shard_map/pack/pallas_call | solution.py:224
  15.2 0.0 copy-start.2
  15.2 0.0 collective-permute-done.1.q
  15.3 0.7 %spread_far.1._ = bf16[4,256,128]{2,1,0:T(8,128)(2,1)} custom-call(bf16[256,128]{1,0:T(8,128)(2,1)S(1)} %collective-permute-done.1.q, bf16[4512,128]{1,0:T(8,128)(2,1)S(1)} %pack.1._.own), custom_call_target="tpu_custom_call" | custom-call | tf_op jit(solution)/shard_map/spread_far/pallas_call | solution.py:241
  16.0 0.0 copy-start.6
  16.0 5.7 %all-to-all-start = ((bf16[4,256,128]{2,1,0:T(8,128)(2,1)}), bf16[4,256,128]{2,1,0:T(8,128)(2,1)S(1)}, u32[]{:S(2)}, u32[]{:S(2)}) async-start(bf16[4,256,128]{2,1,0:T(8,128)(2,1)} %spread_far.1._), calls=%async_computation | async-start | bytes 524288 | tf_op jit(solution)/shard_map/all_to_all | solution.py:213
  21.7 1.9 %collective-permute-start = (bf16[4512,128]{1,0:T(8,128)(2,1)S(1)}, bf16[4512,128]{1,0:T(8,128)(2,1)S(1)}, u32[]{:S(2)}, u32[]{:S(2)}) collective-permute-start(bf16[4512,128]{1,0:T(8,128)(2,1)S(1)} %pack.1._.own), channel_id=1, source_target_pairs={{0,32},{32,0},{1,33},{33,1},{2,34},{34,2},{3,35},{35,3},{4,36},{36... | collective-permute-start | bytes 3465224 | tf_op jit(solution)/shard_map/ppermute | solution.py:210
  23.6 0.0 copy-done.2
  23.6 0.7 %spread_near.1 = bf16[4,256,128]{2,1,0:T(8,128)(2,1)} custom-call(bf16[256,128]{1,0:T(8,128)(2,1)S(1)} %bitcast.8, bf16[4,256,128]{2,1,0:T(8,128)(2,1)} %spread_far.1._), custom_call_target="tpu_custom_call" | custom-call | tf_op jit(solution)/shard_map/spread_near/pallas_call | solution.py:241
  24.3 2.9 %all-to-all-done.q_ref = bf16[4,256,128]{2,1,0:T(8,128)(2,1)S(1)} async-done(((bf16[4,256,128]{2,1,0:T(8,128)(2,1)}), bf16[4,256,128]{2,1,0:T(8,128)(2,1)S(1)}, u32[]{:S(2)}, u32[]{:S(2)}) %all-to-all-start) | async-done | bytes 262176 | tf_op jit(solution)/shard_map/all_to_all | solution.py:213
  27.2 6.4 %all-to-all-start.2 = ((bf16[4,256,128]{2,1,0:T(8,128)(2,1)}), bf16[4,256,128]{2,1,0:T(8,128)(2,1)S(1)}, u32[]{:S(2)}, u32[]{:S(2)}) async-start(bf16[4,256,128]{2,1,0:T(8,128)(2,1)} %spread_near.1), calls=%async_computation.2 | async-start | bytes 524288 | tf_op jit(solution)/shard_map/all_to_all | solution.py:213
  33.7 0.0 collective-permute-done.other
  33.7 0.0 copy-done.6
  33.7 7.6 %far_blocks.1 = bf16[4,144,256]{2,1,0:T(8,128)(2,1)} custom-call(s32[2,4]{1,0:T(2,128)S(1)} %bitcast.11, bf16[4512,128]{1,0:T(8,128)(2,1)S(1)} %pack.1._.own, bf16[4512,128]{1,0:T(8,128)(2,1)S(1)} %collective-permute-done.other, bf16[4,256,128]{2,1,0:T(8,128)(2,1)S(1)} %all-to-all-done.q_ref), custom_call_target="tpu_custom_call" | custom-call | flops 2147483648 | bytes 4194304 | tf_op jit(solution)/shard_map/far_blocks/pallas_call | solution.py:264
  41.3 0.0 all-to-all-done.2.q_ref
  41.3 5.1 %all-to-all-start.1 = ((bf16[4,144,256]{2,1,0:T(8,128)(2,1)}), bf16[4,144,256]{2,1,0:T(8,128)(2,1)S(1)}, u32[]{:S(2)}, u32[]{:S(2)}) async-start(bf16[4,144,256]{2,1,0:T(8,128)(2,1)} %far_blocks.1), calls=%async_computation.1 | async-start | bytes 589824 | tf_op jit(solution)/shard_map/all_to_all | solution.py:213
  46.4 7.6 %near_blocks.1._ = bf16[4,144,256]{2,1,0:T(8,128)(2,1)} custom-call(s32[2,4]{1,0:T(2,128)S(1)} %bitcast.12, bf16[4512,128]{1,0:T(8,128)(2,1)S(1)} %pack.1._.own, bf16[4512,128]{1,0:T(8,128)(2,1)S(1)} %collective-permute-done.other, bf16[4,256,128]{2,1,0:T(8,128)(2,1)S(1)} %all-to-all-done.2.q_ref), custom_call_target="tpu_custom_call" | custom-call | flops 2147483648 | bytes 4194304 | tf_op jit(solution)/shard_map/near_blocks/pallas_call | solution.py:264
  54.0 0.0 all-to-all-done.1.got
  54.0 0.1 merge_far.1
  54.1 5.1 %all-to-all-start.3 = ((bf16[4,144,256]{2,1,0:T(8,128)(2,1)}), bf16[4,144,256]{2,1,0:T(8,128)(2,1)S(1)}, u32[]{:S(2)}, u32[]{:S(2)}) async-start(bf16[4,144,256]{2,1,0:T(8,128)(2,1)} %get-tuple-element.7), calls=%async_computation.3 | async-start | bytes 589824 | tf_op jit(solution)/shard_map/all_to_all | solution.py:213
  59.2 7.0 %collective-permute-start.2 = (bf16[144,256]{1,0:T(8,128)(2,1)S(1)}, bf16[144,256]{1,0:T(8,128)(2,1)S(1)}, u32[]{:S(2)}, u32[]{:S(2)}) collective-permute-start(bf16[144,256]{1,0:T(8,128)(2,1)S(1)} %get-tuple-element.8), channel_id=1, source_target_pairs={{0,256},{256,0},{1,257},{257,1},{2,258},{258,2},{3,259},{259,3},{4... | collective-permute-start | bytes 221192 | tf_op jit(solution)/shard_map/ppermute | solution.py:210
  66.2 5.3 %collective-permute-done.2.back = bf16[144,256]{1,0:T(8,128)(2,1)S(1)} collective-permute-done((bf16[144,256]{1,0:T(8,128)(2,1)S(1)}, bf16[144,256]{1,0:T(8,128)(2,1)S(1)}, u32[]{:S(2)}, u32[]{:S(2)}) %collective-permute-start.2) | collective-permute-done | bytes 73760 | tf_op jit(solution)/shard_map/ppermute | solution.py:210
  71.5 0.0 all-to-all-done.3.got
  71.5 0.8 %merge_all.1 = bf16[256,128]{1,0:T(8,128)(2,1)} custom-call(bf16[4,144,256]{2,1,0:T(8,128)(2,1)S(1)} %all-to-all-done.3.got, bf16[144,256]{1,0:T(8,128)(2,1)S(1)} %collective-permute-done.2.back), custom_call_target="tpu_custom_call" | custom-call | tf_op jit(solution)/shard_map/merge_all/pallas_call | solution.py:291
Async XLA Ops:
  0.0 15.3 %collective-permute-start.1 = (bf16[256,128]{1,0:T(8,128)(2,1)}, bf16[256,128]{1,0:T(8,128)(2,1)S(1)}, u32[]{:S(2)}, u32[]{:S(2)}) collective-permute-start(bf16[256,128]{1,0:T(8,128)(2,1)} %bitcast.7), channel_id=1, source_target_pairs={{0,256},{256,0},{1,257},{257,1},{2,258},{258,2},{3,259},{259,3},{4... | collective-permute-start | bytes 196616 | tf_op jit(solution)/shard_map/ppermute | solution.py:210
  9.7 1.0 %copy-start = (bf16[1,2048,128]{2,1,0:T(8,128)(2,1)S(1)}, bf16[1,2048,128]{2,1,0:T(8,128)(2,1)}, u32[]{:S(2)}) copy-start(bf16[1,2048,128]{2,1,0:T(8,128)(2,1)} %refs_0_.1) | copy-start | bytes 1572868
  10.8 1.0 %copy-start.1 = (bf16[1,2048,128]{2,1,0:T(8,128)(2,1)S(1)}, bf16[1,2048,128]{2,1,0:T(8,128)(2,1)}, u32[]{:S(2)}) copy-start(bf16[1,2048,128]{2,1,0:T(8,128)(2,1)} %refs_1_.1) | copy-start | bytes 1572868
  11.8 0.7 copy-start.3
  12.5 0.7 copy-start.4
  13.2 0.7 copy-start.5
  15.2 8.4 %copy-start.2 = (bf16[16,1,16,128]{3,2,1,0:T(8,128)(2,1)S(1)}, bf16[16,1,16,128]{3,2,1,0:T(8,128)(2,1)}, u32[]{:S(2)}) copy-start(bf16[16,1,16,128]{3,2,1,0:T(8,128)(2,1)} %param.8) | copy-start | bytes 196612
  16.0 17.7 %copy-start.6 = (s32[4,2]{0,1:T(2,128)S(1)}, s32[4,2]{0,1:T(2,128)}, u32[]{:S(2)}) copy-start(s32[4,2]{0,1:T(2,128)} %param.13) | copy-start | bytes 100
  16.0 11.2 %all-to-all-start = ((bf16[4,256,128]{2,1,0:T(8,128)(2,1)}), bf16[4,256,128]{2,1,0:T(8,128)(2,1)S(1)}, u32[]{:S(2)}, u32[]{:S(2)}) async-start(bf16[4,256,128]{2,1,0:T(8,128)(2,1)} %spread_far.1._), calls=%async_computation | async-start | bytes 524288 | tf_op jit(solution)/shard_map/all_to_all | solution.py:213
  21.7 12.0 %collective-permute-start = (bf16[4512,128]{1,0:T(8,128)(2,1)S(1)}, bf16[4512,128]{1,0:T(8,128)(2,1)S(1)}, u32[]{:S(2)}, u32[]{:S(2)}) collective-permute-start(bf16[4512,128]{1,0:T(8,128)(2,1)S(1)} %pack.1._.own), channel_id=1, source_target_pairs={{0,32},{32,0},{1,33},{33,1},{2,34},{34,2},{3,35},{35,3},{4,36},{36... | collective-permute-start | bytes 3465224 | tf_op jit(solution)/shard_map/ppermute | solution.py:210
  27.2 14.0 %all-to-all-start.2 = ((bf16[4,256,128]{2,1,0:T(8,128)(2,1)}), bf16[4,256,128]{2,1,0:T(8,128)(2,1)S(1)}, u32[]{:S(2)}, u32[]{:S(2)}) async-start(bf16[4,256,128]{2,1,0:T(8,128)(2,1)} %spread_near.1), calls=%async_computation.2 | async-start | bytes 524288 | tf_op jit(solution)/shard_map/all_to_all | solution.py:213
  41.3 12.7 %all-to-all-start.1 = ((bf16[4,144,256]{2,1,0:T(8,128)(2,1)}), bf16[4,144,256]{2,1,0:T(8,128)(2,1)S(1)}, u32[]{:S(2)}, u32[]{:S(2)}) async-start(bf16[4,144,256]{2,1,0:T(8,128)(2,1)} %far_blocks.1), calls=%async_computation.1 | async-start | bytes 589824 | tf_op jit(solution)/shard_map/all_to_all | solution.py:213
  54.1 17.5 %all-to-all-start.3 = ((bf16[4,144,256]{2,1,0:T(8,128)(2,1)}), bf16[4,144,256]{2,1,0:T(8,128)(2,1)S(1)}, u32[]{:S(2)}, u32[]{:S(2)}) async-start(bf16[4,144,256]{2,1,0:T(8,128)(2,1)} %get-tuple-element.7), calls=%async_computation.3 | async-start | bytes 589824 | tf_op jit(solution)/shard_map/all_to_all | solution.py:213
  59.2 12.4 %collective-permute-start.2 = (bf16[144,256]{1,0:T(8,128)(2,1)S(1)}, bf16[144,256]{1,0:T(8,128)(2,1)S(1)}, u32[]{:S(2)}, u32[]{:S(2)}) collective-permute-start(bf16[144,256]{1,0:T(8,128)(2,1)S(1)} %get-tuple-element.8), channel_id=1, source_target_pairs={{0,256},{256,0},{1,257},{257,1},{2,258},{258,2},{3,259},{259,3},{4... | collective-permute-start | bytes 221192 | tf_op jit(solution)/shard_map/ppermute | solution.py:210
